TPU v7x, 32 devices: a whole 2x2x4 slice. The times are simulated.
32 devices in a mesh: section: 8 (over z, x), dp: 4 (over y, core).
Axes of the slice: x: 2, y: 2, z: 4, core: 2. Of those that a mesh axis runs over, the one named last changes fastest.
Arguments:
- hidden: bfloat16 [256, 4608], P('dp', 'section'), may hold values from -6 to 6
- norm_gain: float32 [4608], replicated, may hold values from -0.5 to 0.5
- weight: bfloat16 [32000, 4608], P(('section', 'dp'))
- targets: int32 [4, 64], replicated, may hold values from 0 to 31999
- segment_ids: int32 [4, 64], replicated, may hold values from 0 to 7, never falling along the last dimension, each value on 1 to 16 neighbouring positions
- pairing: int32 [4, 8], replicated, may hold values from 0 to 7, each once within a row
- ref_logp: float32 [4, 8], replicated, may hold values from -30 to -20
Outputs:
- hidden_grad: float32 [256, 4608], P('dp', 'section')
- margins: float32 [4, 4], P('dp')
- dpo_loss: float32 [], replicated
Inputs may be any that keep to these rules, and one draw needn't show every extreme that they name: `segment_ids`: within each group's row the segment ids never fall and every one of the 8 segments holds at least one token; one segment of each row holds exactly 16. `pairing`: each row holds every segment number once.
All inputs are finite; a program needn't handle non-finite values.
Results may differ from a plain program's by a relative error of at most 0.0046.
Values may be sent and summed in bfloat16 or wider, within the bound.
No kernel may reach another device: no remote copies, remote signals or barrier semaphores. Data moves between devices by JAX's collectives and lax.ppermute only.
A program may use at most 128 MiB of HBM per device.

v0:
```python
import jax
import jax.numpy as jnp
from jax import lax
from jax.sharding import PartitionSpec as P

SOFTCAP = 30.0
DPO_BETA = 0.5
LOSS_SCALE = 65536.0
EPSILON = 1e-06


def dpo_terms(token_logp, segment_ids, pairing, ref_logp):
    num_groups, group_tokens = segment_ids.shape
    seg_count = pairing.shape[1]
    pair_count = seg_count // 2
    logp_rows = token_logp.reshape(num_groups, group_tokens)
    seg_range = jnp.arange(seg_count, dtype=jnp.int32)
    member = (segment_ids[:, :, None] == seg_range[None, None, :]).astype(jnp.float32)
    counts = jnp.sum(member, axis=1)
    seg_mean = jnp.sum(member * logp_rows[:, :, None], axis=1) / counts
    adjusted = seg_mean - ref_logp
    chosen_hot = (pairing[:, 0::2, None] == seg_range[None, None, :]).astype(jnp.float32)
    rejected_hot = (pairing[:, 1::2, None] == seg_range[None, None, :]).astype(jnp.float32)
    chosen = jnp.sum(chosen_hot * adjusted[:, None, :], axis=2)
    rejected = jnp.sum(rejected_hot * adjusted[:, None, :], axis=2)
    margins = DPO_BETA * (chosen - rejected)
    dpo_loss = jnp.mean(jax.nn.softplus(-margins))
    margin_pull = -jax.nn.sigmoid(-margins) * (LOSS_SCALE / (num_groups * pair_count))
    seg_pull = (
        DPO_BETA * jnp.sum((chosen_hot - rejected_hot) * margin_pull[:, :, None], axis=1) / counts
    )
    token_weight = jnp.sum(member * seg_pull[:, None, :], axis=2).reshape(-1)
    return (margins, dpo_loss, token_weight)


def per_device(hidden, norm_gain, weight, targets, segment_ids, pairing, ref_logp):
    section_count = lax.axis_size("section")
    group_count = lax.axis_size("dp")
    section_index = lax.axis_index("section")
    group_index = lax.axis_index("dp")
    group_tokens, col_count = hidden.shape
    model_width = col_count * section_count
    vocab_rows = weight.shape[0]
    gain_scale = 1.0 + norm_gain
    own_scale = lax.dynamic_slice_in_dim(gain_scale, section_index * col_count, col_count)
    hidden32 = hidden.astype(jnp.float32)
    own_squares = jnp.sum(hidden32 * hidden32, axis=1)
    row_squares = lax.psum(own_squares, "section")
    own_inv = lax.rsqrt(row_squares / model_width + EPSILON)
    outgoing = (hidden32 * own_inv[:, None] * own_scale[None, :]).astype(jnp.bfloat16)
    full_rows = lax.all_gather(outgoing, "section", axis=1, tiled=True)
    raw_logits = lax.dot_general(
        weight,
        lax.all_gather(full_rows, "dp", axis=0, tiled=True),
        (((1,), (1,)), ((), ())),
        preferred_element_type=jnp.float32,
    )
    capped = SOFTCAP * jnp.tanh(raw_logits / SOFTCAP)
    vocab_start = (section_index * group_count + group_index) * vocab_rows
    flat_targets = targets.reshape(-1)
    vocab_ids = vocab_start + lax.broadcasted_iota(jnp.int32, (vocab_rows, 1), 0)
    target_hot = vocab_ids == flat_targets[None, :]
    exp_logits = jnp.exp(capped)
    local_total = jnp.sum(exp_logits, axis=0)
    local_pick = jnp.sum(jnp.where(target_hot, capped, 0.0), axis=0)
    exp_total, picked = lax.psum((local_total, local_pick), ("section", "dp"))
    token_logp = picked - jnp.log(exp_total)
    margins, dpo_loss, token_weight = dpo_terms(token_logp, segment_ids, pairing, ref_logp)
    token_prob = exp_logits / exp_total[None, :]
    cap_slope = 1.0 - capped / SOFTCAP * (capped / SOFTCAP)
    dlogit = (
        token_weight[None, :] * (target_hot.astype(jnp.float32) - token_prob) * cap_slope
    ).astype(jnp.bfloat16)
    own_rows = lax.psum_scatter(
        lax.dot_general(
            dlogit, weight, (((0,), (0,)), ((), ())), preferred_element_type=jnp.float32
        ),
        "dp",
        scatter_dimension=0,
        tiled=True,
    )
    grad_normed = lax.psum_scatter(own_rows, "section", scatter_dimension=1, tiled=True)
    dot_part = jnp.sum(grad_normed * own_scale[None, :] * hidden32, axis=1)
    row_dot = lax.psum(dot_part, "section")
    hidden_grad = (
        own_scale[None, :] * own_inv[:, None] * grad_normed
        - hidden32 * (row_dot * own_inv * own_inv * own_inv / model_width)[:, None]
    )
    own_margins = lax.dynamic_slice_in_dim(margins, group_index, 1, 0)
    return (hidden_grad, own_margins, dpo_loss)


def solution(mesh):
    in_specs = (P("dp", "section"), P(), P(("section", "dp"), None), P(), P(), P(), P())
    out_specs = (P("dp", "section"), P("dp", None), P())
    return jax.shard_map(
        per_device, mesh=mesh, in_specs=in_specs, out_specs=out_specs, check_vma=False
    )
```

profile of v0, /device:TPU:0, one launch (start us, length us, event | category | flops | bytes accessed | tf_op | source)
XLA Modules:
  0.0 294.7 jit_solution(4881066057423018740)
XLA Ops:
  7.2 0.0 all-gather.3.cloned.1.call-start
  7.2 1.0 fusion.15
  8.2 23.1 %psum.28 = f32[64]{0:T(128)S(1)} all-reduce(f32[64]{0:T(128)S(1)} %fusion.15), channel_id=1, replica_groups=mesh['section'=8,'dp'=4] {'section'}, use_global_device_ids=true, to_apply=%region_1.0 | all-reduce | flops 64 | bytes 512 | tf_op jit(solution)/shard_map/psum | solution.py:48
  31.3 0.8 dynamic-slice_add_fusion
  32.1 1.0 fusion.20
  33.1 32.0 %all-gather = bf16[8,576,64]{1,2,0:T(8,128)(2,1)S(1)} all-gather(bf16[1,576,64]{1,2,0:T(8,128)(2,1)S(1)} %fusion.20), channel_id=1, replica_groups=mesh['section'=8,'dp'=4] {'section'}, dimensions={0}, use_global_device_ids=true | all-gather | bytes 663552 | tf_op jit(solution)/shard_map/all_gather | solution.py:51
  65.1 0.4 copy.12
  65.4 1.3 reshape.40
  66.7 0.0 all-gather.3.cloned.1.call-update
  66.7 0.0 reduce-scatter.5.cloned.1.call-start
  66.8 0.8 slice.7
  67.6 0.8 slice.6
  68.3 0.8 eq.64
  69.1 0.0 copy-start.1
  69.1 0.0 copy-start.2
  69.1 19.2 %all-gather.3.cloned.1.call-done = bf16[256,4608]{1,0:T(8,128)(2,1)} async-done(((bf16[64,4608]{1,0:T(8,128)(2,1)}), bf16[256,4608]{1,0:T(8,128)(2,1)}) %all-gather.3.cloned.1.call-update) | async-done | bytes 2359312 | tf_op jit(solution)/shard_map/all_gather | solution.py:54
  88.3 6.2 %fusion.1 = (f32[256]{0:T(256)S(1)}, f32[256]{0:T(256)S(1)}, f32[256,1000]{0,1:T(8,128)S(1)}) fusion(s32[256]{0:T(256)S(1)} %eq.64, s32[1000]{0:T(1024)S(1)} %iota_add_fusion, bf16[256,4608]{1,0:T(8,128)(2,1)} %all-gather.3.cloned.1.call-done, bf16[1000,4608]{1,0:T(8,128)(2,1)} %param.9), kind=kOutput, calls=%fused_computation.4 | convolution fusion | flops 2360831488 | bytes 12606368 | tf_op jit(solution)/shard_map/dot_general | solution.py:52
  94.4 39.4 %all-reduce = (f32[256]{0:T(256)S(1)}, f32[256]{0:T(256)S(1)}) all-reduce(f32[256]{0:T(256)S(1)} %get-tuple-element.4, f32[256]{0:T(256)S(1)} %get-tuple-element.3), channel_id=1, replica_groups=mesh['section'=8,'dp'=4] {'section','dp'}, use_global_device_ids=true, to_apply=%region_5.6 | all-reduce | flops 512 | bytes 4096 | tf_op jit(solution)/shard_map/psum | solution.py:66
  133.8 0.1 mul.164
  133.9 0.0 copy-done.1
  133.9 0.1 select_reduce_fusion.1
  134.0 0.0 copy-done.2
  134.0 0.2 select_reduce_fusion.2
  134.2 0.6 fusion.21
  134.8 0.1 multiply_reduce_fusion
  134.9 0.1 select_reduce_fusion
  135.0 0.1 mul.178
  135.1 8.6 %fusion.7 = f32[256,4608]{1,0:T(8,128)} fusion(bf16[1000,4608]{1,0:T(8,128)(2,1)} %param.9, f32[256,1000]{0,1:T(8,128)S(1)} %get-tuple-element.13, f32[256]{0:T(256)S(1)} %get-tuple-element.9, f32[256]{0:T(256)S(1)} %mul.178, s32[256]{0:T(256)S(1)} %eq.64, s32[1000]{0:T(1024)S(1)} %iota_add_fusion), kind=kOutput, calls=%fused_computation.11 | convolution fusion | flops 2361856000 | bytes 14965664 | tf_op jit(solution)/shard_map/dot_general | solution.py:75
  143.7 0.0 copy-start
  143.7 0.0 reduce-scatter.5.cloned.1.call-update
  143.7 0.0 reduce-scatter.7.cloned.1.call-start
  143.8 48.7 %reduce-scatter.5.cloned.1.call-done = f32[64,4608]{1,0:T(8,128)} async-done(((f32[256,4608]{1,0:T(8,128)}), f32[64,4608]{1,0:T(8,128)}) %reduce-scatter.5.cloned.1.call-update) | async-done | bytes 1179664 | tf_op jit(solution)/shard_map/reduce_scatter | solution.py:74
  192.5 2.9 copy.13
  195.4 0.0 reduce-scatter.7.cloned.1.call-update
  196.0 0.5 constant_dynamic-slice_fusion
  196.6 69.3 %reduce-scatter.7.cloned.1.call-done = f32[576,64]{1,0:T(8,128)} async-done(((f32[4608,64]{1,0:T(8,128)}), f32[576,64]{1,0:T(8,128)}) %reduce-scatter.7.cloned.1.call-update) | async-done | bytes 147472
  265.9 1.1 copy.14
  267.0 0.0 copy-done
  267.0 0.1 fusion.18
  267.1 19.1 %psum.31 = f32[64]{0:T(128)S(1)} all-reduce(f32[64]{0:T(128)S(1)} %fusion.18), channel_id=1, replica_groups=mesh['section'=8,'dp'=4] {'section'}, use_global_device_ids=true, to_apply=%region_15.16 | all-reduce | flops 64 | bytes 512 | tf_op jit(solution)/shard_map/psum | solution.py:84
  286.3 0.8 fusion.19
  (7 shorter events, 0.0 us)
Async XLA Ops:
  7.2 81.1 %all-gather.3.cloned.1.call-start = ((), (), s32[]{:S(2)}) async-start(), calls=%async_computation.2 | async-start | bytes 2949120 | tf_op jit(solution)/shard_map/all_gather | solution.py:54
  66.7 125.8 %reduce-scatter.5.cloned.1.call-start = ((), (), s32[]{:S(2)}) async-start(), calls=%async_computation.3 | async-start | bytes 5898240 | tf_op jit(solution)/shard_map/reduce_scatter | solution.py:74
  69.1 64.8 %copy-start.1 = (s32[4,64]{1,0:T(4,128)S(1)}, s32[4,64]{1,0:T(4,128)}, u32[]{:S(2)}) copy-start(s32[4,64]{1,0:T(4,128)} %param.11) | copy-start | bytes 3076
  69.1 64.9 %copy-start.2 = (f32[4,8]{1,0:T(4,128)S(1)}, f32[4,8]{1,0:T(4,128)}, u32[]{:S(2)}) copy-start(f32[4,8]{1,0:T(4,128)} %param.13) | copy-start | bytes 388
  143.7 123.3 %copy-start = (bf16[64,576]{1,0:T(8,128)(2,1)S(1)}, bf16[64,576]{1,0:T(8,128)(2,1)}, u32[]{:S(2)}) copy-start(bf16[64,576]{1,0:T(8,128)(2,1)} %param.7) | copy-start | bytes 221188
  143.7 122.2 %reduce-scatter.7.cloned.1.call-start = ((), (), s32[]{:S(2)}) async-start(), calls=%async_computation.4 | async-start | bytes 2654208
Sparse Core Ops, SparseCore 0:
  66.9 21.3 all-gather.2
  143.8 48.6 reduce-scatter.4
  196.4 69.4 reduce-scatter.6
where the time goes:
time: 295 us
  waiting for transfers between devices  137 us (46%)
  blocking collectives  114 us (39%)
  between operations  15.6 us (5%)
  matrix products  14.7 us (5%)
  local copies, waits for them, and re-layouts  8.62 us (3%)
  other arithmetic  4.76 us (2%)
    unnamed x4, waiting for transfers between devices  69.3 us
    reduce_scatter x1, waiting for transfers between devices, per_device(): lax.psum_scatter(lax.dot_general(dlogit, weight, (((0,), (0,)), ((), ()))...  48.7 us
    psum x1, blocking collectives, per_device(): exp_total, picked = lax.psum((local_total, local_pick), ('section', 'dp'))  39.4 us
    all_gather x1, blocking collectives, per_device(): full_rows = lax.all_gather(outgoing, 'section', axis=1, tiled=True)  32 us
    psum x1, blocking collectives, per_device(): row_squares = lax.psum(own_squares, 'section')  23.1 us
    all_gather x1, waiting for transfers between devices, per_device(): lax.all_gather(full_rows, 'dp', axis=0, tiled=True)  19.2 us
    psum x1, blocking collectives, per_device(): row_dot = lax.psum(dot_part, 'section')  19.1 us
    dot_general x1, matrix products, per_device(): lax.dot_general(dlogit, weight, (((0,), (0,)), ((), ())), preferred_eleme...  8.59 us
  transfers between devices with their start and end apart: 3, of which 3 were waited for; matrix products, arithmetic and copies ran while one was open for 1% of the time, Pallas kernels for 0%

commit v1 on v0

v1 whole, which is shorter than its diff:
```python
import functools

import jax
import jax.numpy as jnp
from jax import lax
from jax.experimental import pallas as pl
from jax.experimental.pallas import tpu as pltpu
from jax.sharding import PartitionSpec as P

SOFTCAP = 30.0
DPO_BETA = 0.5
LOSS_SCALE = 65536.0
EPSILON = 1e-06


def swap_bits(arr, index, axis):
    count = arr.shape[axis]
    bit = 1
    while bit < count:
        shape = arr.shape[:axis] + (count // (2 * bit), 2, bit) + arr.shape[axis + 1 :]
        swapped = jnp.flip(arr.reshape(shape), axis + 1).reshape(arr.shape)
        arr = jnp.where((index & bit) != 0, swapped, arr)
        bit *= 2
    return arr


def exchange(arr, axis, size, mask):
    return lax.ppermute(arr, axis, [(i, i ^ mask) for i in range(size)])


def tree_sum(items):
    items = list(items)
    while len(items) > 1:
        items = [items[i] + items[i + 1] for i in range(0, len(items), 2)]
    return items[0]


def dpo_terms(token_logp, segment_ids, pairing, ref_logp):
    num_groups, group_tokens = segment_ids.shape
    seg_count = pairing.shape[1]
    pair_count = seg_count // 2
    logp_rows = token_logp.reshape(num_groups, group_tokens)
    seg_range = jnp.arange(seg_count, dtype=jnp.int32)
    member = (segment_ids[:, :, None] == seg_range[None, None, :]).astype(jnp.float32)
    counts = jnp.sum(member, axis=1)
    seg_mean = jnp.sum(member * logp_rows[:, :, None], axis=1) / counts
    adjusted = seg_mean - ref_logp
    chosen_hot = (pairing[:, 0::2, None] == seg_range[None, None, :]).astype(jnp.float32)
    rejected_hot = (pairing[:, 1::2, None] == seg_range[None, None, :]).astype(jnp.float32)
    chosen = jnp.sum(chosen_hot * adjusted[:, None, :], axis=2)
    rejected = jnp.sum(rejected_hot * adjusted[:, None, :], axis=2)
    margins = DPO_BETA * (chosen - rejected)
    losses = jax.nn.softplus(-margins)
    dpo_loss = jnp.sum(tree_sum([losses[k] for k in range(num_groups)])) / (num_groups * pair_count)
    margin_pull = -jax.nn.sigmoid(-margins) * (LOSS_SCALE / (num_groups * pair_count))
    seg_pull = (
        DPO_BETA * jnp.sum((chosen_hot - rejected_hot) * margin_pull[:, :, None], axis=1) / counts
    )
    token_weight = jnp.sum(member * seg_pull[:, None, :], axis=2).reshape(-1)
    return (margins, dpo_loss, token_weight)


def general_path(hidden, norm_gain, weight, targets, segment_ids, pairing, ref_logp):
    n_sec = lax.axis_size("section")
    n_dp = lax.axis_size("dp")
    n_z, n_y = n_sec // 2, n_dp // 2
    sec = lax.axis_index("section")
    dp = lax.axis_index("dp")
    z, x = sec >> 1, sec & 1
    tok, cols = hidden.shape
    half = tok // 2
    width = cols * n_sec
    vocab_rows = weight.shape[0]
    gain_scale = 1.0 + norm_gain
    own_scale = lax.dynamic_slice_in_dim(gain_scale, sec * cols, cols)

    over_core = lambda a: exchange(a, "dp", n_dp, 1)
    over_x = lambda a: exchange(a, "section", n_sec, 1)
    over_y = lambda a, k: exchange(a, "dp", n_dp, 2 * k)
    over_z = lambda a, k: exchange(a, "section", n_sec, 2 * k)

    targets = swap_bits(targets, dp, 0)
    segment_ids = swap_bits(segment_ids, dp, 0)
    pairing = swap_bits(pairing, dp, 0)
    ref_logp = swap_bits(ref_logp, dp, 0)

    def join_x(mine):
        other = over_x(mine)
        first = x == 0
        both = jnp.stack([jnp.where(first, mine, other), jnp.where(first, other, mine)], axis=-2)
        return both.reshape(both.shape[:-3] + (width,))

    pieces = jnp.stack([hidden] + [over_z(hidden, k) for k in range(1, n_z)], axis=1)
    pieces = swap_bits(pieces, z, 1)
    rows_a = join_x(pieces[:half])
    rows_a = jnp.stack([rows_a] + [over_y(rows_a, k) for k in range(1, n_y)])
    raw_b = pieces[half:]
    raw_b = jnp.stack([raw_b] + [over_y(raw_b, k) for k in range(1, n_y)])
    rows_b = join_x(raw_b)
    rows = jnp.concatenate([rows_a, rows_b], axis=1)
    rows = jnp.stack([rows, over_core(rows)], axis=1).reshape(n_dp * tok, width)

    rows32 = rows.astype(jnp.float32)
    inv_rms = lax.rsqrt(jnp.mean(rows32 * rows32, axis=1) + EPSILON)
    normed = (rows32 * inv_rms[:, None] * gain_scale[None, :]).astype(jnp.bfloat16)
    raw_logits = lax.dot_general(
        weight, normed, (((1,), (1,)), ((), ())), preferred_element_type=jnp.float32
    )
    bent = jnp.tanh(raw_logits / SOFTCAP)
    capped = SOFTCAP * bent
    cap_slope = 1.0 - bent * bent
    vocab_start = (sec * n_dp + dp) * vocab_rows
    vocab_ids = vocab_start + lax.broadcasted_iota(jnp.int32, (vocab_rows, 1), 0)
    target_hot = vocab_ids == targets.reshape(-1)[None, :]
    exp_logits = jnp.where(target_hot, 0.0, jnp.exp(capped))
    sums = jnp.stack(
        [
            jnp.sum(exp_logits, axis=0),
            jnp.sum(exp_logits * cap_slope * raw_logits, axis=0),
            jnp.sum(jnp.where(target_hot, raw_logits, 0.0), axis=0),
        ]
    )
    sums = swap_bits(sums.reshape(3, n_dp, tok), dp, 1)
    sums = sums + over_core(sums)
    sums = tree_sum([sums] + [over_y(sums, k) for k in range(1, n_y)])
    sums = sums + over_x(sums)
    sums = tree_sum([sums] + [over_z(sums, k) for k in range(1, n_z)])
    sums = swap_bits(sums, dp, 1).reshape(3, n_dp * tok)
    others, pulled, raw_target = sums[0], sums[1], sums[2]

    bent_target = jnp.tanh(raw_target / SOFTCAP)
    capped_target = SOFTCAP * bent_target
    exp_total = others + jnp.exp(capped_target)
    token_logp = capped_target - jnp.log(exp_total)
    margins, dpo_loss, token_weight = dpo_terms(token_logp, segment_ids, pairing, ref_logp)
    off_scale = token_weight / exp_total
    hit_scale = off_scale * others
    dlogit = (
        jnp.where(target_hot, hit_scale[None, :], -off_scale[None, :] * exp_logits) * cap_slope
    ).astype(jnp.bfloat16)
    row_dot_inv = hit_scale * (1.0 - bent_target * bent_target) * raw_target - off_scale * pulled

    grad = lax.dot_general(
        dlogit, weight, (((0,), (0,)), ((), ())), preferred_element_type=jnp.float32
    )

    def send(fn, arr, *args):
        return fn(arr.astype(jnp.bfloat16), *args).astype(jnp.float32)

    def split_x(arr):
        arr = arr.reshape(arr.shape[:-1] + (n_z, 2, cols))
        first = x == 0
        lo, hi = arr[..., 0, :], arr[..., 1, :]
        return jnp.where(first, lo, hi) + send(over_x, jnp.where(first, hi, lo))

    def split_y(arr):
        return tree_sum([arr[0]] + [send(over_y, arr[k], k) for k in range(1, n_y)])

    grad = grad.reshape(n_y, 2, tok, width)
    grad = grad[:, 0] + send(over_core, grad[:, 1])
    grad_a = split_y(split_x(grad[:, :half]))
    grad_b = split_x(split_y(grad[:, half:]))
    grad = jnp.moveaxis(jnp.concatenate([grad_a, grad_b], axis=0), 1, 0)
    grad = swap_bits(grad, z, 0)
    grad = tree_sum([grad[0]] + [send(over_z, grad[k], k) for k in range(1, n_z)])

    own_inv = inv_rms[:tok]
    hidden_grad = (
        own_scale[None, :] * own_inv[:, None] * grad
        - hidden.astype(jnp.float32) * (row_dot_inv[:tok] * own_inv * own_inv / width)[:, None]
    )
    return (hidden_grad, margins[:1], dpo_loss)


LANES = 128
HALF = LANES // 2
VMEM = pl.BlockSpec(memory_space=pltpu.VMEM)


def halves(a, b):
    lane = lax.broadcasted_iota(jnp.int32, a.shape, 1)
    crossed = pltpu.roll(jnp.where(lane < HALF, b, a), HALF, 1)
    return jnp.where(lane < HALF, a, crossed), jnp.where(lane < HALF, crossed, b)


def whereabouts():
    sec, dp = lax.axis_index("section"), lax.axis_index("dp")
    return sec >> 1, sec & 1, dp & 1, dp, sec * lax.axis_size("dp") + dp


def relative_rows(ids):
    dp = whereabouts()[3]
    return [ids[pl.ds(dp ^ ((r & 1) * 2 + (r >> 1)), 1), :] for r in range(4)]


def turn_kernel(cols, n_z, targets, weight, turned_a, turned_b, keep, send, flat, hot):
    z, x, _, _, index = whereabouts()
    vocab = weight.shape[0]
    block = 2 * cols
    flat[...] = jnp.concatenate(relative_rows(targets), axis=1) - index * vocab
    row = lax.broadcasted_iota(jnp.int32, hot.shape, 0)
    hot[...] = jnp.where(row == flat[...], 1.0, 0.0).astype(jnp.bfloat16)
    for k in range(n_z):
        at = pl.multiple_of((z ^ k) * block, LANES)
        strip = [weight[:, pl.ds(at + c, LANES)].T for c in range(0, block, LANES)]
        strip = jnp.concatenate(strip, axis=0)
        turned = turned_a if k & 1 else turned_b
        for side in range(2):
            part = strip[side * cols : (side + 1) * cols, :]
            here = pl.multiple_of(((x ^ side) * (n_z // 2) + (k >> 1)) * cols, HALF)
            turned[pl.ds(here, cols), :] = part
            rows = lax.dot_general(
                part, hot[...], (((1,), (0,)), ((), ())), preferred_element_type=jnp.float32
            ).astype(jnp.bfloat16)
            here = pl.multiple_of(((x ^ side) * n_z + (k >> 1) + (0 if k & 1 else n_z // 2)) * cols, HALF)
            keep[pl.ds(here, cols), :] = rows[:, :LANES]
            send[pl.ds(here, cols), :] = rows[:, LANES:]


def strips_kernel(*refs):
    strips, out = refs[:-1], refs[-1]
    rows = out.shape[0] // len(strips)
    for k, strip in enumerate(strips):
        flipped = wide(strip[...]).T
        both = jnp.concatenate([flipped[:rows], flipped[rows:]], axis=1)
        out[k * rows : (k + 1) * rows, :] = both.astype(out.dtype)


def gain_kernel(gain, table):
    for i in range(gain.shape[0]):
        row = jnp.broadcast_to(1.0 + gain[i : i + 1, :], (LANES, LANES))
        table[i * LANES : (i + 1) * LANES, :] = row.T


def norm_kernel(cols, n_z, *refs):
    stacks, table, normed, inv_own, own_scale = refs[:8], refs[8], refs[9], refs[10], refs[11]
    z, x, core, _, _ = whereabouts()
    rows = cols // 2
    own = pl.multiple_of((z * 2 + x) * cols, HALF)
    upper = table[pl.ds(pl.multiple_of(own + rows, 32), rows), :]
    own_scale[...] = halves(table[pl.ds(own, rows), :], upper)[0]
    width = normed.shape[0]
    lane = lax.broadcasted_iota(jnp.int32, (1, LANES), 1)

    def piece(ref, k):
        return wide(ref[k * rows : (k + 1) * rows, :])

    def squares(ref):
        parts = [piece(ref, k) for k in range(n_z)]
        return sum(jnp.sum(part * part, axis=0, keepdims=True) for part in parts)

    invs = []
    for far in range(2):
        base, one, two, three = stacks[4 * far : 4 * far + 4]
        x_first = core == far
        near, away = squares(base), squares(three)
        first, second = squares(one), squares(two)
        near = near + jnp.where(x_first, first, second)
        away = away + jnp.where(x_first, second, first)
        inv = [lax.rsqrt((sq + pltpu.roll(sq, HALF, 1)) / width + EPSILON) for sq in (near, away)]
        invs.append(jnp.where(lane < HALF, inv[0], inv[1]))
    inv_own[...] = invs[0]
    for k in range(n_z):
        for side in range(2):
            at = ((z ^ k) * 2 + (x ^ side)) * cols
            for far in range(2):
                base, one, two, three = stacks[4 * far : 4 * far + 4]
                x_first = core == far
                first, second = piece(one, k), piece(two, k)
                if side == 0:
                    near, away = piece(base, k), jnp.where(x_first, second, first)
                else:
                    near, away = jnp.where(x_first, first, second), piece(three, k)
                for part, value in enumerate(halves(near, away)):
                    here = pl.ds(pl.multiple_of(at + part * rows, 32), rows)
                    value = value * invs[far] * table[here, :]
                    normed[here, far * LANES : (far + 1) * LANES] = value.astype(jnp.bfloat16)


def post_kernel(grad, send):
    for at in chunks(grad.shape[0]):
        send[at, :] = grad[at, LANES:].astype(send.dtype)


def count_kernel(stats, got, sums):
    mine, theirs = stats[...], got[...]
    total = [mine[:, :LANES] + theirs[:, LANES:], mine[:, LANES:] + theirs[:, :LANES]]
    sums[...] = jnp.concatenate(total + [jnp.zeros((2, LANES), jnp.float32)], axis=0)


def chunks(rows):
    count = next(n for n in (8, 4, 2, 1) if rows % (16 * n) == 0)
    step = rows // count
    return [slice(i * step, (i + 1) * step) for i in range(count)]


def after(at, rows):
    return slice(at.start + rows, at.stop + rows)


def wide(a):
    return a.astype(jnp.float32)


def fold_core_kernel(mine, got, keep, send):
    rows = mine.shape[0] // 2

    def split(one_side):
        for at in chunks(rows):
            top = wide(mine[at, :LANES]) + wide(got[at, :])
            low = after(at, rows)
            bottom = wide(mine[low, :LANES]) + wide(got[low, :])
            if not one_side:
                top, bottom = halves(top, bottom)
            keep[at, :] = top.astype(keep.dtype)
            send[at, :] = bottom.astype(send.dtype)

    core = whereabouts()[2]
    pl.when(core == 0)(lambda: split(True))
    pl.when(core != 0)(lambda: split(False))


def tally_kernel(sums, heard, segments, pairing, ref_logp, scales, margins_out, loss_out):
    sums = sums[...] + heard[...]
    groups, places = pairing.shape
    total_pairs = groups * places // 2

    def both(i):
        return jnp.concatenate([sums[i : i + 1], sums[i + 3 : i + 4]], axis=0)

    others, pulled, raw_target = both(0), both(1), both(2)
    bent = jnp.tanh(raw_target / SOFTCAP)
    capped = SOFTCAP * bent
    exp_total = others + jnp.exp(capped)
    token_logp = capped - jnp.log(exp_total)

    seg_rows, pair_rows, ref_rows = relative_rows(segments), relative_rows(pairing), relative_rows(ref_logp)
    seg_id = lax.broadcasted_iota(jnp.int32, (places, places), 0)
    place = lax.broadcasted_iota(jnp.int32, (places, places), 1)
    even = (place[0:1] & 1) == 0
    lane = lax.broadcasted_iota(jnp.int32, (1, LANES), 1)
    losses, weight = [], jnp.zeros((1, LANES), jnp.float32)
    for r in range(groups):
        seg = jnp.concatenate([seg_rows[r & 2], seg_rows[(r & 2) + 1]], axis=1)
        inside = jnp.logical_and(seg == seg_id[:, 0:1], (lane >= HALF) == ((r & 1) == 1))
        member = jnp.where(inside, 1.0, 0.0)
        counts = jnp.sum(member, axis=1, keepdims=True)
        c = r >> 1
        seg_mean = jnp.sum(member * token_logp[c : c + 1], axis=1, keepdims=True) / counts
        seg_ref = jnp.sum(jnp.where(seg_id == place, ref_rows[r], 0.0), axis=1, keepdims=True)
        hot = jnp.where(pair_rows[r] == seg_id, 1.0, 0.0)
        value = jnp.sum(hot * (seg_mean - seg_ref), axis=0, keepdims=True)
        pair = [value[:, k : k + 1] - value[:, k + 1 : k + 2] for k in range(0, places, 2)]
        margins = DPO_BETA * jnp.concatenate([p for p in pair for _ in range(2)], axis=1)
        down = -margins
        loss = jnp.maximum(down, 0.0) + jnp.log1p(jnp.exp(-jnp.abs(down)))
        losses.append(jnp.where(even, loss, 0.0))
        if r == 0:
            margins_out[...] = jnp.concatenate([DPO_BETA * p for p in pair], axis=1)
        if c == 0:
            pull = -(LOSS_SCALE / total_pairs) / (1.0 + jnp.exp(margins))
            pull = jnp.where(even, pull, -pull)
            seg_pull = DPO_BETA * jnp.sum(hot * pull, axis=1, keepdims=True) / counts
            weight = weight + jnp.sum(member * seg_pull, axis=0, keepdims=True)
    loss_out[...] = jnp.sum(tree_sum(losses), axis=1, keepdims=True) / total_pairs

    off = weight / exp_total[0:1]
    hit = off * others[0:1] * (1.0 - bent[0:1] * bent[0:1])
    dot = hit * raw_target[0:1] - off * pulled[0:1]
    scales[...] = jnp.concatenate([halves(off, off)[0], dot, jnp.zeros((6, LANES), jnp.float32)], axis=0)


def fold_half_kernel(mine, got, keep, send):
    rows = mine.shape[0] // 2
    for at in chunks(rows):
        low = after(at, rows)
        left, right = halves(wide(mine[at, :]) + wide(got[at, :]), wide(mine[low, :]) + wide(got[low, :]))
        keep[at, :] = left.astype(keep.dtype)
        send[at, :] = right.astype(send.dtype)


def join_kernel(first_row, mine, got, hit_mine, hit_got, sums, heard, left, right):
    total = sums[...] + heard[...]
    bent = jnp.tanh(total[2:3] / SOFTCAP)
    ratio = total[0:1] * (1.0 - bent * bent)
    ratio = jnp.where(whereabouts()[2] == 0, ratio, halves(ratio, ratio)[0])
    rows = mine.shape[0] // 2

    def joined(at):
        there = after(at, first_row)
        hit = wide(hit_mine[there, :]) + wide(hit_got[there, :])
        return ratio * hit - (mine[at, :] + wide(got[at, :]))

    for at in chunks(rows):
        near, away = halves(joined(at), joined(after(at, rows)))
        left[at, :] = near.astype(left.dtype)
        right[at, :] = away.astype(right.dtype)


def finish_kernel(width, mine, one, two, three, scales, inv_own, own_scale, hidden, out):
    tok = hidden.shape[0]
    grad = (mine[...] + wide(one[...])) + (wide(two[...]) + wide(three[...]))
    grad = (grad * scales[0:1, :] * own_scale[...]).T
    grad = jnp.concatenate([grad[:tok], grad[tok:]], axis=1)
    columns = jnp.concatenate([scales[1:2, :], inv_own[...], jnp.zeros((6, LANES), jnp.float32)], axis=0).T
    dot, inv = columns[:tok, 0:1], columns[:tok, 1:2]
    out[...] = inv * grad - wide(hidden[...]) * (dot * inv * inv / width)


def call(kernel, name, outs, in_specs, out_specs, scratch, limit, flops, moved, *args):
    return pl.pallas_call(
        kernel,
        out_shape=outs,
        in_specs=in_specs,
        out_specs=out_specs,
        scratch_shapes=scratch,
        compiler_params=pltpu.CompilerParams(vmem_limit_bytes=limit << 20),
        cost_estimate=pl.CostEstimate(flops=flops, bytes_accessed=moved, transcendentals=0),
        name=name,
    )(*args)


def fast_path(hidden, norm_gain, weight, targets, segment_ids, pairing, ref_logp):
    n_sec = lax.axis_size("section")
    n_dp = lax.axis_size("dp")
    n_z = n_sec // 2
    tok, cols = hidden.shape
    tokens = n_dp * tok
    width = cols * n_sec
    vocab = weight.shape[0]
    block = 2 * cols
    padded = -(-vocab // LANES) * LANES
    shape = jax.ShapeDtypeStruct
    half, full = jnp.bfloat16, jnp.float32

    def pairs(of):
        return [(s * n_dp + d, of(s, d)) for s in range(n_sec) for d in range(n_dp)]

    both_axes = ("section", "dp")
    one_pairs = pairs(lambda s, d: (s ^ 1) * n_dp + d if d & 1 == 0 else s * n_dp + (d ^ 2))
    two_pairs = pairs(lambda s, d: (s ^ 1) * n_dp + d if d & 1 == 1 else s * n_dp + (d ^ 2))
    to_one = lambda a: lax.ppermute(a, both_axes, one_pairs)
    to_two = lambda a: lax.ppermute(a, both_axes, two_pairs)
    over_core = lambda a: exchange(a, "dp", n_dp, 1)
    over_x = lambda a: exchange(a, "section", n_sec, 1)
    over_y = lambda a: exchange(a, "dp", n_dp, 2)
    over_z = lambda a, k: exchange(a, "section", n_sec, 2 * k)

    def hold(value, *others):
        return lax.optimization_barrier((value,) + others)[0]

    strips = [hidden] + [over_z(hidden, k) for k in range(1, n_z)]

    turned_a, turned_b, hit_keep, hit_send, flat = call(
        functools.partial(turn_kernel, cols, n_z), "turn_weight",
        (shape((width // 2, vocab), half),) * 2
        + (shape((width, LANES), half), shape((width, LANES), half), shape((1, tokens), jnp.int32)),
        [VMEM, VMEM], (VMEM,) * 5, [pltpu.VMEM((vocab, tokens), half)],
        8, 2 * tokens * vocab * width, 4 * vocab * width, targets, weight,
    )

    base = call(
        strips_kernel, "strips", shape((n_z * cols // 2, LANES), half), [VMEM] * n_z, VMEM, [], 4,
        tok * width, 0, *[hold(s, hit_send) for s in strips],
    )
    one = to_one(base)
    two = to_two(base)
    table = call(
        gain_kernel, "gain_table", shape((width, LANES), full), [VMEM], VMEM, [], 4, width * LANES,
        16 * width * LANES, hold(norm_gain.reshape(-1, LANES), base),
    )
    half_rows = (shape((width // 2, LANES), half),) * 2
    hit_keep, hit_send = call(
        fold_core_kernel, "fold_rows", half_rows, [VMEM, VMEM], (VMEM, VMEM), [], 4,
        0, 96 * width * LANES, hit_keep, over_core(hold(hit_send, base)),
    )
    three = to_two(one)
    stacks = [base, one, two, three]
    stacks = stacks + [over_core(s) for s in (base, one, two, hold(three, hit_send, table))]
    hit_got = to_one(hold(hit_send, three, table))

    normed, inv_own, own_scale = call(
        functools.partial(norm_kernel, cols, n_z), "norm",
        (shape((width, tokens), half), shape((1, LANES), full), shape((cols // 2, LANES), full)),
        [VMEM] * 9, (VMEM,) * 3, [], 4, 8 * tokens * width, 0, *stacks, table,
    )
    raw_logits = lax.dot_general(
        weight, normed, (((1,), (0,)), ((), ())), preferred_element_type=jnp.float32
    )
    bent = jnp.tanh(raw_logits / SOFTCAP)
    hot = lax.broadcasted_iota(jnp.int32, (vocab, 1), 0) == flat
    power = jnp.where(hot, 0.0, jnp.exp(SOFTCAP * bent))
    sloped = power * (1.0 - bent * bent)
    stats = [
        jnp.sum(power, axis=0),
        jnp.sum(sloped * raw_logits, axis=0),
        jnp.sum(jnp.where(hot, raw_logits, 0.0), axis=0),
    ]
    stats = jnp.stack(stats)
    sloped = hold(sloped.astype(half), stats)

    def product(turned, sloped):
        return lax.dot_general(turned, sloped, (((1,), (0,)), ((), ())), preferred_element_type=full)

    def halved(kind, rows):
        return (shape((rows, LANES), kind), shape((rows, LANES), half))

    def fold(kernel, name, mine, got, kind=full):
        return call(
            kernel, name, halved(kind, mine.shape[0] // 2), [VMEM] * 2, (VMEM,) * 2, [], 4, 0, 0, mine, got
        )

    rows = width // 2
    grad_a = product(turned_a, sloped)
    send_a = call(post_kernel, "post", shape((rows, LANES), half), [VMEM], VMEM, [], 4, 0, 0, grad_a)
    got_a = over_core(send_a)
    sums = call(
        count_kernel, "count", shape((8, LANES), full), [VMEM] * 2, VMEM, [], 4, 0, 0, stats, over_core(stats)
    )
    grad_b = product(turned_b, hold(sloped, send_a, sums))
    sums = sums + over_x(sums)
    send_b = call(post_kernel, "post", shape((rows, LANES), half), [VMEM], VMEM, [], 4, 0, 0, hold(grad_b, sums))
    got_b = over_core(hold(send_b, hit_got))
    keep_a, send_a = fold(fold_core_kernel, "fold_core", grad_a, hold(got_a, sums))
    got_a = to_one(send_a)
    heard = over_y(sums)
    keep_b, send_b = fold(fold_core_kernel, "fold_core", grad_b, hold(got_b, send_a))
    got_b = to_one(send_b)
    sums = sums + jnp.concatenate([heard[:, HALF:], heard[:, :HALF]], axis=1)
    sums = sums + over_z(sums, 1)
    heard = over_z(sums, 2)

    rows = width // 4

    def join(name, first_row, mine, got):
        return call(
            functools.partial(join_kernel, first_row), name, halved(full, rows // 2),
            [VMEM] * 6, (VMEM,) * 2, [], 4, 0, 0, mine, got, hit_keep, hit_got, sums, heard,
        )

    keep_a, send_a = join("join_a", 0, keep_a, got_a)
    got_a = to_two(send_a)
    keep_b, send_b = join("join_b", rows, keep_b, hold(got_b, send_a))
    got_b = to_two(send_b)
    send_1, send_3 = fold(fold_half_kernel, "fold_last_a", keep_a, got_a, half)
    got_3 = over_z(send_3, 3)
    keep, send_2 = fold(fold_half_kernel, "fold_last_b", keep_b, hold(got_b, send_3))
    got_2, got_1 = over_z(send_2, 2), over_z(hold(send_1, send_2), 1)
    scales, margins, dpo_loss = call(
        tally_kernel, "tally",
        (shape((8, LANES), full), shape((1, ref_logp.shape[1] // 2), full), shape((1, 1), full)),
        [VMEM] * 5, (VMEM,) * 3, [], 4, 0, 0, sums, hold(heard, send_2), segment_ids, pairing, ref_logp,
    )
    hidden_grad = call(
        functools.partial(finish_kernel, width), "finish", shape((tok, cols), full),
        [VMEM] * 8, VMEM, [], 4, 0, 0,
        keep, got_1, got_2, got_3, scales, inv_own, own_scale, hidden,
    )
    return (hidden_grad, margins, dpo_loss.reshape(()))


def per_device(hidden, norm_gain, weight, *rest):
    n_sec, n_dp = lax.axis_size("section"), lax.axis_size("dp")
    tok, cols = hidden.shape
    vocab = weight.shape[0]
    fits = n_dp == 4 and n_sec == 8 and tok == HALF and cols % HALF == 0 and vocab % 8 == 0
    fits = fits and norm_gain.shape[0] % LANES == 0
    path = fast_path if fits else general_path
    return path(hidden, norm_gain, weight, *rest)


def solution(mesh):
    in_specs = (P("dp", "section"), P(), P(("section", "dp"), None), P(), P(), P(), P())
    out_specs = (P("dp", "section"), P("dp", None), P())
    return jax.shard_map(
        per_device, mesh=mesh, in_specs=in_specs, out_specs=out_specs, check_vma=False
    )
```

time: 295 us -> 71.8 us (0.24)
  waiting for transfers between devices: 137 us -> 19.5 us
  blocking collectives: 114 us -> 0 us
  starting transfers between devices: 0.12 us -> 31 us
  between operations: 15.6 us -> 0.87 us
  Pallas kernels: 0 us -> 9.91 us
  matrix products: 14.7 us -> 5.83 us
  other arithmetic: 4.76 us -> 0.09 us
  local copies, waits for them, and re-layouts: 8.62 us -> 4.4 us
    psum x3 -> x0, blocking collectives: 81.6 us -> none  [the longest x1 39.4 us: per_device(): exp_total, picked = lax.psum((local_total, local_pick), ('section', 'dp'))]
    unnamed x4 -> x0, waiting for transfers between devices: 69.3 us -> none
    reduce_scatter x1 -> x0, waiting for transfers between devices: 48.7 us -> none  [per_device(): lax.psum_scatter(lax.dot_general(dlogit, weight, (((0,), (0,)), ((), ()))...]
    all_gather x1 -> x0, blocking collectives: 32 us -> none  [per_device(): full_rows = lax.all_gather(outgoing, 'section', axis=1, tiled=True)]
    ppermute x0 -> x26, starting transfers between devices: none -> 31 us  [the longest x18 19.4 us: exchange(): return lax.ppermute(arr, axis, [(i, i ^ mask) for i in range(size)])]
    ppermute x0 -> x26, waiting for transfers between devices: none -> 19.5 us  [the longest x18 8.11 us: exchange(): return lax.ppermute(arr, axis, [(i, i ^ mask) for i in range(size)])]
    all_gather x1 -> x0, waiting for transfers between devices: 19.2 us -> none  [per_device(): lax.all_gather(full_rows, 'dp', axis=0, tiled=True)]
    pallas_call x0 -> x16, Pallas kernels: none -> 9.91 us  [call(): pl.pallas_call(kernel, out_shape=outs, in_specs=in_specs, out_specs=out_s...]
  transfers between devices with their start and end apart: 3 -> 26, of which waited for: 3 -> 8; matrix products, arithmetic and copies ran while one was open for 1% -> 8% of each run, Pallas kernels for 0% -> 12%
where the time goes in v1:
time: 71.8 us; the launch traced here: 71.6 us
  starting transfers between devices  31 us (43%)
  waiting for transfers between devices  19.5 us (27%)
  Pallas kernels  9.91 us (14%)
  matrix products  5.83 us (8%)
  local copies, waits for them, and re-layouts  4.4 us (6%)
  between operations  0.87 us (1%)
    ppermute x18, starting transfers between devices, exchange(): return lax.ppermute(arr, axis, [(i, i ^ mask) for i in range(size)])  19.4 us
    pallas_call x16, Pallas kernels, call(): pl.pallas_call(kernel, out_shape=outs, in_specs=in_specs, out_specs=out_s...  9.91 us
    ppermute x18, waiting for transfers between devices, exchange(): return lax.ppermute(arr, axis, [(i, i ^ mask) for i in range(size)])  8.11 us
    ppermute x4, starting transfers between devices, fast_path(): to_one = lambda a: lax.ppermute(a, both_axes, one_pairs)  5.8 us
    ppermute x4, starting transfers between devices, fast_path(): to_two = lambda a: lax.ppermute(a, both_axes, two_pairs)  5.79 us
    ppermute x4, waiting for transfers between devices, fast_path(): to_one = lambda a: lax.ppermute(a, both_axes, one_pairs)  5.75 us
    ppermute x4, waiting for transfers between devices, fast_path(): to_two = lambda a: lax.ppermute(a, both_axes, two_pairs)  5.68 us
    unnamed x16, local copies, waits for them, and re-layouts  4.33 us
  transfers between devices with their start and end apart: 26, of which 8 were waited for; matrix products, arithmetic and copies ran while one was open for 8% of the time, Pallas kernels for 12%

profile of v1, /device:TPU:0, one launch (start us, length us, event | category | flops | bytes accessed | tf_op | source)
XLA Modules:
  0.0 71.6 jit_solution(5351202092429694029)
XLA Ops:
  0.6 4.1 %collective-permute-start.1 = (bf16[64,576]{1,0:T(8,128)(2,1)}, bf16[64,576]{1,0:T(8,128)(2,1)S(1)}, u32[]{:S(2)}, u32[]{:S(2)}) collective-permute-start(bf16[64,576]{1,0:T(8,128)(2,1)} %hidden.1), channel_id=1, source_target_pairs={{0,16},{4,20},{8,24},{12,28},{16,0},{20,4},{24,8},{28,12},{1,17},{... | collective-permute-start | bytes 221192 | tf_op jit(solution)/shard_map/ppermute | solution.py:28
  4.7 1.6 %collective-permute-start = (bf16[64,576]{1,0:T(8,128)(2,1)}, bf16[64,576]{1,0:T(8,128)(2,1)S(1)}, u32[]{:S(2)}, u32[]{:S(2)}) collective-permute-start(bf16[64,576]{1,0:T(8,128)(2,1)} %hidden.1), channel_id=1, source_target_pairs={{0,8},{4,12},{8,0},{12,4},{16,24},{20,28},{24,16},{28,20},{1,9},{5... | collective-permute-start | bytes 221192 | tf_op jit(solution)/shard_map/ppermute | solution.py:28
  6.3 0.0 collective-permute-start.2
  6.3 3.6 %copy-done = bf16[1000,4608]{1,0:T(8,128)(2,1)S(1)} copy-done((bf16[1000,4608]{1,0:T(8,128)(2,1)S(1)}, bf16[1000,4608]{1,0:T(8,128)(2,1)}, u32[]{:S(2)}) %copy-start) | copy-done | bytes 9216024
  9.9 0.7 copy-done.4
  10.6 3.3 %turn_weight.1 = (bf16[2304,1000]{1,0:T(8,128)(2,1)S(1)}, bf16[2304,1000]{1,0:T(8,128)(2,1)S(1)}, bf16[4608,128]{1,0:T(8,128)(2,1)S(1)}, bf16[4608,128]{1,0:T(8,128)(2,1)S(1)}, s32[1,256]{1,0:T(1,128)S(1)}) custom-call(s32[4,64]{1,0:T(4,128)S(1)} %copy-done.4, bf16[1000,4608]{1,0:T(8,128)(2,1)S(1)} %copy-done), custom_call_target="tpu_custom_call" | custom-call | flops 2359296000 | bytes 18432000 | tf_op jit(solution)/shard_map/turn_weight/pallas_call | solution.py:411
  13.9 0.0 collective-permute-done.2.refs_3_
  13.9 0.0 collective-permute-done.refs_1_
  14.0 0.3 strips.1.refs_0_
  14.3 0.1 collective-permute-start.9
  14.4 1.8 %collective-permute-start.3 = (bf16[1152,128]{1,0:T(8,128)(2,1)S(1)}, bf16[1152,128]{1,0:T(8,128)(2,1)S(1)}, u32[]{:S(2)}, u32[]{:S(2)}) collective-permute-start(bf16[1152,128]{1,0:T(8,128)(2,1)S(1)} %strips.1.refs_0_), channel_id=1, source_target_pairs={{0,4},{1,3},{2,6},{3,1},{4,0},{5,7},{6,2},{7,5},{8,12},{9,11},{10,... | collective-permute-start | bytes 884744 | tf_op jit(solution)/shard_map/ppermute | solution.py:442
  16.1 1.5 %collective-permute-start.4 = (bf16[1152,128]{1,0:T(8,128)(2,1)S(1)}, bf16[1152,128]{1,0:T(8,128)(2,1)S(1)}, u32[]{:S(2)}, u32[]{:S(2)}) collective-permute-start(bf16[1152,128]{1,0:T(8,128)(2,1)S(1)} %strips.1.refs_0_), channel_id=1, source_target_pairs={{0,2},{1,5},{2,0},{3,7},{4,6},{5,1},{6,4},{7,3},{8,10},{9,13},{10,... | collective-permute-start | bytes 884744 | tf_op jit(solution)/shard_map/ppermute | solution.py:443
  17.7 5.7 %collective-permute-done.3.refs_1_ = bf16[1152,128]{1,0:T(8,128)(2,1)S(1)} collective-permute-done((bf16[1152,128]{1,0:T(8,128)(2,1)S(1)}, bf16[1152,128]{1,0:T(8,128)(2,1)S(1)}, u32[]{:S(2)}, u32[]{:S(2)}) %collective-permute-start.3) | collective-permute-done | bytes 294944 | tf_op jit(solution)/shard_map/ppermute | solution.py:442
  23.4 2.1 %collective-permute-start.5 = (bf16[1152,128]{1,0:T(8,128)(2,1)S(1)}, bf16[1152,128]{1,0:T(8,128)(2,1)S(1)}, u32[]{:S(2)}, u32[]{:S(2)}) collective-permute-start(bf16[1152,128]{1,0:T(8,128)(2,1)S(1)} %collective-permute-done.3.refs_1_), channel_id=1, source_target_pairs={{0,2},{1,5},{2,0},{3,7},{4,6},{5,1},{6,4},{7,3},{8,10},{9,13},{10,... | collective-permute-start | bytes 884744 | tf_op jit(solution)/shard_map/ppermute | solution.py:443
  25.5 0.7 gain_table.1.refs_8_
  26.2 0.6 collective-permute-start.7
  26.8 0.0 collective-permute-done.4.refs_2_
  26.8 0.1 collective-permute-start.8
  26.9 0.0 collective-permute-done.9.got
  26.9 0.5 fold_rows.1
  27.4 2.9 %collective-permute-done.5.refs_3_ = bf16[1152,128]{1,0:T(8,128)(2,1)S(1)} collective-permute-done((bf16[1152,128]{1,0:T(8,128)(2,1)S(1)}, bf16[1152,128]{1,0:T(8,128)(2,1)S(1)}, u32[]{:S(2)}, u32[]{:S(2)}) %collective-permute-start.5) | collective-permute-done | bytes 294944 | tf_op jit(solution)/shard_map/ppermute | solution.py:443
  30.2 0.0 collective-permute-start.10
  30.2 1.9 %collective-permute-start.13 = (bf16[2304,128]{1,0:T(8,128)(2,1)S(1)}, bf16[2304,128]{1,0:T(8,128)(2,1)S(1)}, u32[]{:S(2)}, u32[]{:S(2)}) collective-permute-start(bf16[2304,128]{1,0:T(8,128)(2,1)S(1)} %get-tuple-element.63), channel_id=1, source_target_pairs={{0,4},{1,3},{2,6},{3,1},{4,0},{5,7},{6,2},{7,5},{8,12},{9,11},{10,... | collective-permute-start | bytes 1769480 | tf_op jit(solution)/shard_map/ppermute | solution.py:442
  32.1 0.0 collective-permute-done.8.refs_6_
  32.1 0.0 collective-permute-done.7.refs_5_
  32.1 2.0 %norm.1 = (bf16[4608,256]{1,0:T(8,128)(2,1)S(1)}, f32[1,128]{1,0:T(1,128)S(1)}, f32[288,128]{1,0:T(8,128)S(1)}) custom-call(bf16[1152,128]{1,0:T(8,128)(2,1)S(1)} %strips.1.refs_0_, bf16[1152,128]{1,0:T(8,128)(2,1)S(1)} %collective-permute-done.3.refs_1_, bf16[1152,128]{1,0:T(8,128)(2,1)S(1)} %collective-permute-done.4.refs_2_, ...), custom_call_target="tpu_custom_call" | custom-call | flops 9437184 | tf_op jit(solution)/shard_map/norm/pallas_call | solution.py:411
  34.2 2.9 %fusion = (f32[256]{0:T(256)S(1)}, f32[256]{0:T(256)S(1)}, f32[256]{0:T(256)S(1)}, bf16[1000,256]{1,0:T(8,128)(2,1)S(1)}) fusion(s32[256]{0:T(256)S(1)} %bitcast.15, bf16[4608,256]{1,0:T(8,128)(2,1)S(1)} %get-tuple-element.58, bf16[1000,4608]{1,0:T(8,128)(2,1)S(1)} %copy-done.1), kind=kOutput, calls=%fused_computation.5 | convolution fusion | flops 2362623232 | bytes 12091392 | tf_op jit(solution)/shard_map/dot_general | solution.py:487
  37.1 0.4 collective-permute-start.11
  37.6 1.5 %fusion.3.grad.mine = f32[2304,256]{1,0:T(8,128)S(1)} fusion(bf16[2304,1000]{1,0:T(8,128)(2,1)S(1)} %get-tuple-element.60, bf16[1000,256]{1,0:T(8,128)(2,1)S(1)} %get-tuple-element.61), kind=kOutput, calls=%fused_computation.12 | convolution fusion | flops 1179648000 | bytes 7479296 | tf_op jit(solution)/shard_map/dot_general | solution.py:503
  39.0 0.1 post.2
  39.1 0.2 collective-permute-start.15
  39.3 1.7 %collective-permute-start.12 = (f32[8,128]{1,0:T(8,128)S(1)}, f32[8,128]{1,0:T(8,128)S(1)}, u32[]{:S(2)}, u32[]{:S(2)}) collective-permute-start(f32[8,128]{1,0:T(8,128)S(1)} %count.1), channel_id=1, source_target_pairs={{0,4},{4,0},{8,12},{12,8},{16,20},{20,16},{24,28},{28,24},{1,5},{5... | collective-permute-start | bytes 12296 | tf_op jit(solution)/shard_map/ppermute | solution.py:28
  41.0 1.5 %fusion.4.grad.mine = f32[2304,256]{1,0:T(8,128)S(1)} fusion(bf16[2304,1000]{1,0:T(8,128)(2,1)S(1)} %get-tuple-element.46, bf16[1000,256]{1,0:T(8,128)(2,1)S(1)} %get-tuple-element.61), kind=kOutput, calls=%fused_computation.13 | convolution fusion | flops 1179648000 | bytes 7479296 | tf_op jit(solution)/shard_map/dot_general | solution.py:503
  42.5 0.6 collective-permute-done.12
  43.0 0.1 post.3
  43.1 0.1 collective-permute-start.14
  43.2 1.9 %collective-permute-start.18 = (f32[8,128]{1,0:T(8,128)S(1)}, f32[8,128]{1,0:T(8,128)S(1)}, u32[]{:S(2)}, u32[]{:S(2)}) collective-permute-start(f32[8,128]{1,0:T(8,128)S(1)} %add.9), channel_id=1, source_target_pairs={{0,2},{1,3},{2,0},{3,1},{4,6},{5,7},{6,4},{7,5},{8,10},{9,11},{10,... | collective-permute-start | bytes 12296 | tf_op jit(solution)/shard_map/ppermute | solution.py:28
  45.1 0.1 fold_core.2
  45.2 0.0 copy-start.5
  45.2 0.0 copy-start.6
  45.2 0.0 copy-start.7
  45.3 1.6 %collective-permute-start.17 = (bf16[1152,128]{1,0:T(8,128)(2,1)S(1)}, bf16[1152,128]{1,0:T(8,128)(2,1)S(1)}, u32[]{:S(2)}, u32[]{:S(2)}) collective-permute-start(bf16[1152,128]{1,0:T(8,128)(2,1)S(1)} %get-tuple-element.66), channel_id=1, source_target_pairs={{0,4},{1,3},{2,6},{3,1},{4,0},{5,7},{6,2},{7,5},{8,12},{9,11},{10,... | collective-permute-start | bytes 884744 | tf_op jit(solution)/shard_map/ppermute | solution.py:442
  46.9 0.1 fold_core.3
  47.0 0.5 collective-permute-start.16
  47.6 0.1 fusion.2
  47.6 0.1 maximum_add_fusion
  47.7 0.7 %collective-permute-start.19 = (f32[8,128]{1,0:T(8,128)S(1)}, f32[8,128]{1,0:T(8,128)S(1)}, u32[]{:S(2)}, u32[]{:S(2)}) collective-permute-start(f32[8,128]{1,0:T(8,128)S(1)} %maximum_add_fusion), channel_id=1, source_target_pairs={{0,8},{4,12},{8,0},{12,4},{16,24},{20,28},{24,16},{28,20},{1,9},{5... | collective-permute-start | bytes 12296 | tf_op jit(solution)/shard_map/ppermute | solution.py:28
  48.4 2.9 %collective-permute-done.19 = f32[8,128]{1,0:T(8,128)S(1)} collective-permute-done((f32[8,128]{1,0:T(8,128)S(1)}, f32[8,128]{1,0:T(8,128)S(1)}, u32[]{:S(2)}, u32[]{:S(2)}) %collective-permute-start.19) | collective-permute-done | bytes 4128 | tf_op jit(solution)/shard_map/ppermute | solution.py:28
  51.3 2.2 %collective-permute-start.20 = (f32[8,128]{1,0:T(8,128)S(1)}, f32[8,128]{1,0:T(8,128)S(1)}, u32[]{:S(2)}, u32[]{:S(2)}) collective-permute-start(f32[8,128]{1,0:T(8,128)S(1)} %add.11.sums), channel_id=1, source_target_pairs={{0,16},{4,20},{8,24},{12,28},{16,0},{20,4},{24,8},{28,12},{1,17},{... | collective-permute-start | bytes 12296 | tf_op jit(solution)/shard_map/ppermute | solution.py:28
  53.5 2.3 %collective-permute-done.20.heard = f32[8,128]{1,0:T(8,128)S(1)} collective-permute-done((f32[8,128]{1,0:T(8,128)S(1)}, f32[8,128]{1,0:T(8,128)S(1)}, u32[]{:S(2)}, u32[]{:S(2)}) %collective-permute-start.20) | collective-permute-done | bytes 4128 | tf_op jit(solution)/shard_map/ppermute | solution.py:28
  55.8 0.2 join_a.1
  56.1 1.3 %collective-permute-start.22 = (bf16[576,128]{1,0:T(8,128)(2,1)S(1)}, bf16[576,128]{1,0:T(8,128)(2,1)S(1)}, u32[]{:S(2)}, u32[]{:S(2)}) collective-permute-start(bf16[576,128]{1,0:T(8,128)(2,1)S(1)} %get-tuple-element.72), channel_id=1, source_target_pairs={{0,2},{1,5},{2,0},{3,7},{4,6},{5,1},{6,4},{7,3},{8,10},{9,13},{10,... | collective-permute-start | bytes 442376 | tf_op jit(solution)/shard_map/ppermute | solution.py:443
  57.4 0.2 join_b.1
  57.6 0.9 %collective-permute-start.21 = (bf16[576,128]{1,0:T(8,128)(2,1)S(1)}, bf16[576,128]{1,0:T(8,128)(2,1)S(1)}, u32[]{:S(2)}, u32[]{:S(2)}) collective-permute-start(bf16[576,128]{1,0:T(8,128)(2,1)S(1)} %get-tuple-element.75), channel_id=1, source_target_pairs={{0,2},{1,5},{2,0},{3,7},{4,6},{5,1},{6,4},{7,3},{8,10},{9,13},{10,... | collective-permute-start | bytes 442376 | tf_op jit(solution)/shard_map/ppermute | solution.py:443
  58.5 2.8 %collective-permute-done.22.got = bf16[576,128]{1,0:T(8,128)(2,1)S(1)} collective-permute-done((bf16[576,128]{1,0:T(8,128)(2,1)S(1)}, bf16[576,128]{1,0:T(8,128)(2,1)S(1)}, u32[]{:S(2)}, u32[]{:S(2)}) %collective-permute-start.22) | collective-permute-done | bytes 147488 | tf_op jit(solution)/shard_map/ppermute | solution.py:443
  61.3 0.1 fold_last_a.1
  61.4 3.7 %collective-permute-start.25 = (bf16[288,128]{1,0:T(8,128)(2,1)S(1)}, bf16[288,128]{1,0:T(8,128)(2,1)S(1)}, u32[]{:S(2)}, u32[]{:S(2)}) collective-permute-start(bf16[288,128]{1,0:T(8,128)(2,1)S(1)} %get-tuple-element.77), channel_id=1, source_target_pairs={{0,24},{4,28},{8,16},{12,20},{16,8},{20,12},{24,0},{28,4},{1,25},{... | collective-permute-start | bytes 221192 | tf_op jit(solution)/shard_map/ppermute | solution.py:28
  65.1 0.1 fold_last_b.1
  65.2 0.1 collective-permute-start.23
  65.3 1.9 %collective-permute-start.24 = (bf16[288,128]{1,0:T(8,128)(2,1)S(1)}, bf16[288,128]{1,0:T(8,128)(2,1)S(1)}, u32[]{:S(2)}, u32[]{:S(2)}) collective-permute-start(bf16[288,128]{1,0:T(8,128)(2,1)S(1)} %get-tuple-element.81), channel_id=1, source_target_pairs={{0,16},{4,20},{8,24},{12,28},{16,0},{20,4},{24,8},{28,12},{1,17},{... | collective-permute-start | bytes 221192 | tf_op jit(solution)/shard_map/ppermute | solution.py:28
  67.3 1.0 %tally.1 = (f32[8,128]{1,0:T(8,128)S(1)}, f32[1,4]{1,0:T(1,128)}, f32[1,1]{1,0:T(1,128)}) custom-call(f32[8,128]{1,0:T(8,128)S(1)} %add.11.sums, f32[8,128]{1,0:T(8,128)S(1)} %collective-permute-done.20.heard, s32[4,64]{1,0:T(4,128)S(1)} %copy-done.5, s32[4,8]{1,0:T(4,128)S(1)} %copy-done.6, f32[4,8]{1,0:T(4,128)S(1)} %copy-done.7), custom_call_target="tpu_custom_call" | custom-call | tf_op jit(solution)/shard_map/tally/pallas_call | solution.py:411
  68.3 1.4 %collective-permute-done.23.one = bf16[288,128]{1,0:T(8,128)(2,1)S(1)} collective-permute-done((bf16[288,128]{1,0:T(8,128)(2,1)S(1)}, bf16[288,128]{1,0:T(8,128)(2,1)S(1)}, u32[]{:S(2)}, u32[]{:S(2)}) %collective-permute-start.23) | collective-permute-done | bytes 73760 | tf_op jit(solution)/shard_map/ppermute | solution.py:28
  69.6 1.0 %collective-permute-done.24.two = bf16[288,128]{1,0:T(8,128)(2,1)S(1)} collective-permute-done((bf16[288,128]{1,0:T(8,128)(2,1)S(1)}, bf16[288,128]{1,0:T(8,128)(2,1)S(1)}, u32[]{:S(2)}, u32[]{:S(2)}) %collective-permute-start.24) | collective-permute-done | bytes 73760 | tf_op jit(solution)/shard_map/ppermute | solution.py:28
  70.6 1.0 %finish.1 = f32[64,576]{1,0:T(8,128)} custom-call(f32[288,128]{1,0:T(8,128)S(1)} %get-tuple-element.79.mine, bf16[288,128]{1,0:T(8,128)(2,1)S(1)} %collective-permute-done.23.one, bf16[288,128]{1,0:T(8,128)(2,1)S(1)} %collective-permute-done.24.two, bf16[288,128]{1,0:T(8,128)(2,1)S(1)} %collective-permute-done.25.three, ...), custom_call_target="tpu_custom_call" | custom-call | tf_op jit(solution)/shard_map/finish/pallas_call | solution.py:411
  (28 shorter events, 0.1 us)
Async XLA Ops:
  0.6 13.3 %collective-permute-start.1 = (bf16[64,576]{1,0:T(8,128)(2,1)}, bf16[64,576]{1,0:T(8,128)(2,1)S(1)}, u32[]{:S(2)}, u32[]{:S(2)}) collective-permute-start(bf16[64,576]{1,0:T(8,128)(2,1)} %hidden.1), channel_id=1, source_target_pairs={{0,16},{4,20},{8,24},{12,28},{16,0},{20,4},{24,8},{28,12},{1,17},{... | collective-permute-start | bytes 221192 | tf_op jit(solution)/shard_map/ppermute | solution.py:28
  4.7 9.2 %collective-permute-start = (bf16[64,576]{1,0:T(8,128)(2,1)}, bf16[64,576]{1,0:T(8,128)(2,1)S(1)}, u32[]{:S(2)}, u32[]{:S(2)}) collective-permute-start(bf16[64,576]{1,0:T(8,128)(2,1)} %hidden.1), channel_id=1, source_target_pairs={{0,8},{4,12},{8,0},{12,4},{16,24},{20,28},{24,16},{28,20},{1,9},{5... | collective-permute-start | bytes 221192 | tf_op jit(solution)/shard_map/ppermute | solution.py:28
  6.3 7.6 %collective-permute-start.2 = (bf16[64,576]{1,0:T(8,128)(2,1)}, bf16[64,576]{1,0:T(8,128)(2,1)S(1)}, u32[]{:S(2)}, u32[]{:S(2)}) collective-permute-start(bf16[64,576]{1,0:T(8,128)(2,1)} %hidden.1), channel_id=1, source_target_pairs={{0,24},{4,28},{8,16},{12,20},{16,8},{20,12},{24,0},{28,4},{1,25},{... | collective-permute-start | bytes 221192 | tf_op jit(solution)/shard_map/ppermute | solution.py:28
  6.3 3.6 %copy-start = (bf16[1000,4608]{1,0:T(8,128)(2,1)S(1)}, bf16[1000,4608]{1,0:T(8,128)(2,1)}, u32[]{:S(2)}) copy-start(bf16[1000,4608]{1,0:T(8,128)(2,1)} %weight.1) | copy-start | bytes 27648004
  9.9 0.7 copy-start.4
  10.6 3.3 %copy-start.2 = (bf16[64,576]{1,0:T(8,128)(2,1)S(1)}, bf16[64,576]{1,0:T(8,128)(2,1)}, u32[]{:S(2)}) copy-start(bf16[64,576]{1,0:T(8,128)(2,1)} %hidden.1) | copy-start | bytes 221188
  10.6 14.9 %copy-start.3 = (f32[4608]{0:T(1024)S(1)}, f32[4608]{0:T(1024)}, u32[]{:S(2)}) copy-start(f32[4608]{0:T(1024)} %param.8) | copy-start | bytes 55300
  14.3 12.6 %collective-permute-start.9 = (bf16[4608,128]{1,0:T(8,128)(2,1)S(1)}, bf16[4608,128]{1,0:T(8,128)(2,1)S(1)}, u32[]{:S(2)}, u32[]{:S(2)}) collective-permute-start(bf16[4608,128]{1,0:T(8,128)(2,1)S(1)} %get-tuple-element.54), channel_id=1, source_target_pairs={{0,1},{1,0},{2,3},{3,2},{4,5},{5,4},{6,7},{7,6},{8,9},{9,8},{10,11... | collective-permute-start | bytes 3538952 | tf_op jit(solution)/shard_map/ppermute | solution.py:28
  14.4 9.0 %collective-permute-start.3 = (bf16[1152,128]{1,0:T(8,128)(2,1)S(1)}, bf16[1152,128]{1,0:T(8,128)(2,1)S(1)}, u32[]{:S(2)}, u32[]{:S(2)}) collective-permute-start(bf16[1152,128]{1,0:T(8,128)(2,1)S(1)} %strips.1.refs_0_), channel_id=1, source_target_pairs={{0,4},{1,3},{2,6},{3,1},{4,0},{5,7},{6,2},{7,5},{8,12},{9,11},{10,... | collective-permute-start | bytes 884744 | tf_op jit(solution)/shard_map/ppermute | solution.py:442
  16.1 10.6 %collective-permute-start.4 = (bf16[1152,128]{1,0:T(8,128)(2,1)S(1)}, bf16[1152,128]{1,0:T(8,128)(2,1)S(1)}, u32[]{:S(2)}, u32[]{:S(2)}) collective-permute-start(bf16[1152,128]{1,0:T(8,128)(2,1)S(1)} %strips.1.refs_0_), channel_id=1, source_target_pairs={{0,2},{1,5},{2,0},{3,7},{4,6},{5,1},{6,4},{7,3},{8,10},{9,13},{10,... | collective-permute-start | bytes 884744 | tf_op jit(solution)/shard_map/ppermute | solution.py:443
  23.4 6.8 %collective-permute-start.5 = (bf16[1152,128]{1,0:T(8,128)(2,1)S(1)}, bf16[1152,128]{1,0:T(8,128)(2,1)S(1)}, u32[]{:S(2)}, u32[]{:S(2)}) collective-permute-start(bf16[1152,128]{1,0:T(8,128)(2,1)S(1)} %collective-permute-done.3.refs_1_), channel_id=1, source_target_pairs={{0,2},{1,5},{2,0},{3,7},{4,6},{5,1},{6,4},{7,3},{8,10},{9,13},{10,... | collective-permute-start | bytes 884744 | tf_op jit(solution)/shard_map/ppermute | solution.py:443
  25.5 6.6 %collective-permute-start.6 = (bf16[1152,128]{1,0:T(8,128)(2,1)S(1)}, bf16[1152,128]{1,0:T(8,128)(2,1)S(1)}, u32[]{:S(2)}, u32[]{:S(2)}) collective-permute-start(bf16[1152,128]{1,0:T(8,128)(2,1)S(1)} %strips.1.refs_0_), channel_id=1, source_target_pairs={{0,1},{1,0},{2,3},{3,2},{4,5},{5,4},{6,7},{7,6},{8,9},{9,8},{10,11... | collective-permute-start | bytes 884744 | tf_op jit(solution)/shard_map/ppermute | solution.py:28
  25.5 8.6 %copy-start.1 = (bf16[1000,4608]{1,0:T(8,128)(2,1)S(1)}, bf16[1000,4608]{1,0:T(8,128)(2,1)}, u32[]{:S(2)}) copy-start(bf16[1000,4608]{1,0:T(8,128)(2,1)} %weight.1) | copy-start | bytes 27648004
  26.2 5.9 %collective-permute-start.7 = (bf16[1152,128]{1,0:T(8,128)(2,1)S(1)}, bf16[1152,128]{1,0:T(8,128)(2,1)S(1)}, u32[]{:S(2)}, u32[]{:S(2)}) collective-permute-start(bf16[1152,128]{1,0:T(8,128)(2,1)S(1)} %collective-permute-done.3.refs_1_), channel_id=1, source_target_pairs={{0,1},{1,0},{2,3},{3,2},{4,5},{5,4},{6,7},{7,6},{8,9},{9,8},{10,11... | collective-permute-start | bytes 884744 | tf_op jit(solution)/shard_map/ppermute | solution.py:28
  26.8 5.3 %collective-permute-start.8 = (bf16[1152,128]{1,0:T(8,128)(2,1)S(1)}, bf16[1152,128]{1,0:T(8,128)(2,1)S(1)}, u32[]{:S(2)}, u32[]{:S(2)}) collective-permute-start(bf16[1152,128]{1,0:T(8,128)(2,1)S(1)} %collective-permute-done.4.refs_2_), channel_id=1, source_target_pairs={{0,1},{1,0},{2,3},{3,2},{4,5},{5,4},{6,7},{7,6},{8,9},{9,8},{10,11... | collective-permute-start | bytes 884744 | tf_op jit(solution)/shard_map/ppermute | solution.py:28
  30.2 1.9 %collective-permute-start.10 = (bf16[1152,128]{1,0:T(8,128)(2,1)S(1)}, bf16[1152,128]{1,0:T(8,128)(2,1)S(1)}, u32[]{:S(2)}, u32[]{:S(2)}) collective-permute-start(bf16[1152,128]{1,0:T(8,128)(2,1)S(1)} %collective-permute-done.5.refs_3_), channel_id=1, source_target_pairs={{0,1},{1,0},{2,3},{3,2},{4,5},{5,4},{6,7},{7,6},{8,9},{9,8},{10,11... | collective-permute-start | bytes 884744 | tf_op jit(solution)/shard_map/ppermute | solution.py:28
  30.2 12.9 %collective-permute-start.13 = (bf16[2304,128]{1,0:T(8,128)(2,1)S(1)}, bf16[2304,128]{1,0:T(8,128)(2,1)S(1)}, u32[]{:S(2)}, u32[]{:S(2)}) collective-permute-start(bf16[2304,128]{1,0:T(8,128)(2,1)S(1)} %get-tuple-element.63), channel_id=1, source_target_pairs={{0,4},{1,3},{2,6},{3,1},{4,0},{5,7},{6,2},{7,5},{8,12},{9,11},{10,... | collective-permute-start | bytes 1769480 | tf_op jit(solution)/shard_map/ppermute | solution.py:442
  37.1 2.2 %collective-permute-start.11 = (f32[3,256]{1,0:T(4,128)S(1)}, f32[3,256]{1,0:T(4,128)S(1)}, u32[]{:S(2)}, u32[]{:S(2)}) collective-permute-start(f32[3,256]{1,0:T(4,128)S(1)} %pad_maximum_fusion.stats), channel_id=1, source_target_pairs={{0,1},{1,0},{2,3},{3,2},{4,5},{5,4},{6,7},{7,6},{8,9},{9,8},{10,11... | collective-permute-start | bytes 9224 | tf_op jit(solution)/shard_map/ppermute | solution.py:28
  39.1 6.0 %collective-permute-start.15 = (bf16[2304,128]{1,0:T(8,128)(2,1)S(1)}, bf16[2304,128]{1,0:T(8,128)(2,1)S(1)}, u32[]{:S(2)}, u32[]{:S(2)}) collective-permute-start(bf16[2304,128]{1,0:T(8,128)(2,1)S(1)} %post.2), channel_id=1, source_target_pairs={{0,1},{1,0},{2,3},{3,2},{4,5},{5,4},{6,7},{7,6},{8,9},{9,8},{10,11... | collective-permute-start | bytes 1769480 | tf_op jit(solution)/shard_map/ppermute | solution.py:28
  39.3 3.7 %collective-permute-start.12 = (f32[8,128]{1,0:T(8,128)S(1)}, f32[8,128]{1,0:T(8,128)S(1)}, u32[]{:S(2)}, u32[]{:S(2)}) collective-permute-start(f32[8,128]{1,0:T(8,128)S(1)} %count.1), channel_id=1, source_target_pairs={{0,4},{4,0},{8,12},{12,8},{16,20},{20,16},{24,28},{28,24},{1,5},{5... | collective-permute-start | bytes 12296 | tf_op jit(solution)/shard_map/ppermute | solution.py:28
  43.1 3.8 %collective-permute-start.14 = (bf16[2304,128]{1,0:T(8,128)(2,1)S(1)}, bf16[2304,128]{1,0:T(8,128)(2,1)S(1)}, u32[]{:S(2)}, u32[]{:S(2)}) collective-permute-start(bf16[2304,128]{1,0:T(8,128)(2,1)S(1)} %post.3), channel_id=1, source_target_pairs={{0,1},{1,0},{2,3},{3,2},{4,5},{5,4},{6,7},{7,6},{8,9},{9,8},{10,11... | collective-permute-start | bytes 1769480 | tf_op jit(solution)/shard_map/ppermute | solution.py:28
  43.2 4.4 %collective-permute-start.18 = (f32[8,128]{1,0:T(8,128)S(1)}, f32[8,128]{1,0:T(8,128)S(1)}, u32[]{:S(2)}, u32[]{:S(2)}) collective-permute-start(f32[8,128]{1,0:T(8,128)S(1)} %add.9), channel_id=1, source_target_pairs={{0,2},{1,3},{2,0},{3,1},{4,6},{5,7},{6,4},{7,5},{8,10},{9,11},{10,... | collective-permute-start | bytes 12296 | tf_op jit(solution)/shard_map/ppermute | solution.py:28
  45.2 22.0 %copy-start.5 = (s32[4,64]{1,0:T(4,128)S(1)}, s32[4,64]{1,0:T(4,128)}, u32[]{:S(2)}) copy-start(s32[4,64]{1,0:T(4,128)} %segments.1) | copy-start | bytes 3076
  45.2 22.0 %copy-start.6 = (s32[4,8]{1,0:T(4,128)S(1)}, s32[4,8]{1,0:T(4,128)}, u32[]{:S(2)}) copy-start(s32[4,8]{1,0:T(4,128)} %pairing.1) | copy-start | bytes 388
  45.2 22.0 %copy-start.7 = (f32[4,8]{1,0:T(4,128)S(1)}, f32[4,8]{1,0:T(4,128)}, u32[]{:S(2)}) copy-start(f32[4,8]{1,0:T(4,128)} %ref_logp.1) | copy-start | bytes 388
  45.3 10.6 %collective-permute-start.17 = (bf16[1152,128]{1,0:T(8,128)(2,1)S(1)}, bf16[1152,128]{1,0:T(8,128)(2,1)S(1)}, u32[]{:S(2)}, u32[]{:S(2)}) collective-permute-start(bf16[1152,128]{1,0:T(8,128)(2,1)S(1)} %get-tuple-element.66), channel_id=1, source_target_pairs={{0,4},{1,3},{2,6},{3,1},{4,0},{5,7},{6,2},{7,5},{8,12},{9,11},{10,... | collective-permute-start | bytes 884744 | tf_op jit(solution)/shard_map/ppermute | solution.py:442
  47.0 10.4 %collective-permute-start.16 = (bf16[1152,128]{1,0:T(8,128)(2,1)S(1)}, bf16[1152,128]{1,0:T(8,128)(2,1)S(1)}, u32[]{:S(2)}, u32[]{:S(2)}) collective-permute-start(bf16[1152,128]{1,0:T(8,128)(2,1)S(1)} %get-tuple-element.69), channel_id=1, source_target_pairs={{0,4},{1,3},{2,6},{3,1},{4,0},{5,7},{6,2},{7,5},{8,12},{9,11},{10,... | collective-permute-start | bytes 884744 | tf_op jit(solution)/shard_map/ppermute | solution.py:442
  47.7 3.6 %collective-permute-start.19 = (f32[8,128]{1,0:T(8,128)S(1)}, f32[8,128]{1,0:T(8,128)S(1)}, u32[]{:S(2)}, u32[]{:S(2)}) collective-permute-start(f32[8,128]{1,0:T(8,128)S(1)} %maximum_add_fusion), channel_id=1, source_target_pairs={{0,8},{4,12},{8,0},{12,4},{16,24},{20,28},{24,16},{28,20},{1,9},{5... | collective-permute-start | bytes 12296 | tf_op jit(solution)/shard_map/ppermute | solution.py:28
  51.3 4.5 %collective-permute-start.20 = (f32[8,128]{1,0:T(8,128)S(1)}, f32[8,128]{1,0:T(8,128)S(1)}, u32[]{:S(2)}, u32[]{:S(2)}) collective-permute-start(f32[8,128]{1,0:T(8,128)S(1)} %add.11.sums), channel_id=1, source_target_pairs={{0,16},{4,20},{8,24},{12,28},{16,0},{20,4},{24,8},{28,12},{1,17},{... | collective-permute-start | bytes 12296 | tf_op jit(solution)/shard_map/ppermute | solution.py:28
  56.1 5.2 %collective-permute-start.22 = (bf16[576,128]{1,0:T(8,128)(2,1)S(1)}, bf16[576,128]{1,0:T(8,128)(2,1)S(1)}, u32[]{:S(2)}, u32[]{:S(2)}) collective-permute-start(bf16[576,128]{1,0:T(8,128)(2,1)S(1)} %get-tuple-element.72), channel_id=1, source_target_pairs={{0,2},{1,5},{2,0},{3,7},{4,6},{5,1},{6,4},{7,3},{8,10},{9,13},{10,... | collective-permute-start | bytes 442376 | tf_op jit(solution)/shard_map/ppermute | solution.py:443
  57.6 7.5 %collective-permute-start.21 = (bf16[576,128]{1,0:T(8,128)(2,1)S(1)}, bf16[576,128]{1,0:T(8,128)(2,1)S(1)}, u32[]{:S(2)}, u32[]{:S(2)}) collective-permute-start(bf16[576,128]{1,0:T(8,128)(2,1)S(1)} %get-tuple-element.75), channel_id=1, source_target_pairs={{0,2},{1,5},{2,0},{3,7},{4,6},{5,1},{6,4},{7,3},{8,10},{9,13},{10,... | collective-permute-start | bytes 442376 | tf_op jit(solution)/shard_map/ppermute | solution.py:443
  61.4 6.9 %collective-permute-start.25 = (bf16[288,128]{1,0:T(8,128)(2,1)S(1)}, bf16[288,128]{1,0:T(8,128)(2,1)S(1)}, u32[]{:S(2)}, u32[]{:S(2)}) collective-permute-start(bf16[288,128]{1,0:T(8,128)(2,1)S(1)} %get-tuple-element.77), channel_id=1, source_target_pairs={{0,24},{4,28},{8,16},{12,20},{16,8},{20,12},{24,0},{28,4},{1,25},{... | collective-permute-start | bytes 221192 | tf_op jit(solution)/shard_map/ppermute | solution.py:28
  65.2 4.4 %collective-permute-start.23 = (bf16[288,128]{1,0:T(8,128)(2,1)S(1)}, bf16[288,128]{1,0:T(8,128)(2,1)S(1)}, u32[]{:S(2)}, u32[]{:S(2)}) collective-permute-start(bf16[288,128]{1,0:T(8,128)(2,1)S(1)} %get-tuple-element.82), channel_id=1, source_target_pairs={{0,8},{4,12},{8,0},{12,4},{16,24},{20,28},{24,16},{28,20},{1,9},{5... | collective-permute-start | bytes 221192 | tf_op jit(solution)/shard_map/ppermute | solution.py:28
  65.3 5.3 %collective-permute-start.24 = (bf16[288,128]{1,0:T(8,128)(2,1)S(1)}, bf16[288,128]{1,0:T(8,128)(2,1)S(1)}, u32[]{:S(2)}, u32[]{:S(2)}) collective-permute-start(bf16[288,128]{1,0:T(8,128)(2,1)S(1)} %get-tuple-element.81), channel_id=1, source_target_pairs={{0,16},{4,20},{8,24},{12,28},{16,0},{20,4},{24,8},{28,12},{1,17},{... | collective-permute-start | bytes 221192 | tf_op jit(solution)/shard_map/ppermute | solution.py:28

commit v2 on v1

--- a/solution.py
+++ b/solution.py
@@ -451,18 +451,18 @@
 
     strips = [hidden] + [over_z(hidden, k) for k in range(1, n_z)]
 
+    base = call(
+        strips_kernel, "strips", shape((n_z * cols // 2, LANES), half), [VMEM] * n_z, VMEM, [], 4,
+        tok * width, 0, *strips,
+    )
     turned_a, turned_b, hit_keep, hit_send, flat = call(
         functools.partial(turn_kernel, cols, n_z), "turn_weight",
         (shape((width // 2, vocab), half),) * 2
         + (shape((width, LANES), half), shape((width, LANES), half), shape((1, tokens), jnp.int32)),
         [VMEM, VMEM], (VMEM,) * 5, [pltpu.VMEM((vocab, tokens), half)],
-        8, 2 * tokens * vocab * width, 4 * vocab * width, targets, weight,
-    )
-
-    base = call(
-        strips_kernel, "strips", shape((n_z * cols // 2, LANES), half), [VMEM] * n_z, VMEM, [], 4,
-        tok * width, 0, *[hold(s, hit_send) for s in strips],
-    )
+        8, 2 * tokens * vocab * width, 4 * vocab * width, hold(targets, base), weight,
+    )
+
     one = to_one(base)
     two = to_two(base)
     table = call(
@@ -472,7 +472,7 @@
     half_rows = (shape((width // 2, LANES), half),) * 2
     hit_keep, hit_send = call(
         fold_core_kernel, "fold_rows", half_rows, [VMEM, VMEM], (VMEM, VMEM), [], 4,
-        0, 96 * width * LANES, hit_keep, over_core(hold(hit_send, base)),
+        0, 96 * width * LANES, hit_keep, over_core(hold(hit_send, one, two)),
     )
     three = to_two(one)
     stacks = [base, one, two, three]

time: 71.8 us -> 71.2 us (level)
  starting transfers between devices: 31 us -> 23.1 us
  waiting for transfers between devices: 19.5 us -> 25.9 us
  local copies, waits for them, and re-layouts: 4.4 us -> 5.29 us
    ppermute x18, waiting for transfers between devices: 8.11 us -> 19.6 us  [exchange(): return lax.ppermute(arr, axis, [(i, i ^ mask) for i in range(size)])]
    ppermute x4, waiting for transfers between devices: 5.75 us -> 0.01 us  [fast_path(): to_one = lambda a: lax.ppermute(a, both_axes, one_pairs)]
    ppermute x18, starting transfers between devices: 19.4 us -> 15.3 us  [exchange(): return lax.ppermute(arr, axis, [(i, i ^ mask) for i in range(size)])]
    ppermute x4, starting transfers between devices: 5.8 us -> 3.52 us  [fast_path(): to_one = lambda a: lax.ppermute(a, both_axes, one_pairs)]
    ppermute x4, starting transfers between devices: 5.79 us -> 4.31 us  [fast_path(): to_two = lambda a: lax.ppermute(a, both_axes, two_pairs)]
    unnamed x16 -> x18, local copies, waits for them, and re-layouts: 4.33 us -> 5.22 us
  transfers between devices with their start and end apart: 26 -> 26, of which waited for: 8 -> 14; matrix products, arithmetic and copies ran while one was open for 8% -> 8% of each run, Pallas kernels for 12% -> 12%
where the time goes in v2:
time: 71.2 us; the launch traced here: 71 us
  waiting for transfers between devices  25.9 us (36%)
  starting transfers between devices  23.1 us (32%)
  Pallas kernels  9.85 us (14%)
  matrix products  5.83 us (8%)
  local copies, waits for them, and re-layouts  5.29 us (7%)
  between operations  0.86 us (1%)
    ppermute x18, waiting for transfers between devices, exchange(): return lax.ppermute(arr, axis, [(i, i ^ mask) for i in range(size)])  19.6 us
    ppermute x18, starting transfers between devices, exchange(): return lax.ppermute(arr, axis, [(i, i ^ mask) for i in range(size)])  15.3 us
    pallas_call x16, Pallas kernels, call(): pl.pallas_call(kernel, out_shape=outs, in_specs=in_specs, out_specs=out_s...  9.85 us
    ppermute x4, waiting for transfers between devices, fast_path(): to_two = lambda a: lax.ppermute(a, both_axes, two_pairs)  6.31 us
    unnamed x18, local copies, waits for them, and re-layouts  5.22 us
    ppermute x4, starting transfers between devices, fast_path(): to_two = lambda a: lax.ppermute(a, both_axes, two_pairs)  4.31 us
    ppermute x4, starting transfers between devices, fast_path(): to_one = lambda a: lax.ppermute(a, both_axes, one_pairs)  3.52 us
    dot_general x2, matrix products, product(): lax.dot_general(turned, sloped, (((1,), (0,)), ((), ())), preferred_eleme...  2.92 us
  transfers between devices with their start and end apart: 26, of which 14 were waited for; matrix products, arithmetic and copies ran while one was open for 8% of the time, Pallas kernels for 12%

profile of v2, /device:TPU:0, one launch (start us, length us, event | category | flops | bytes accessed | tf_op | source)
XLA Modules:
  0.0 71.0 jit_solution(10707703800376911212)
XLA Ops:
  0.6 5.1 %collective-permute-start.2 = (bf16[64,576]{1,0:T(8,128)(2,1)}, bf16[64,576]{1,0:T(8,128)(2,1)S(1)}, u32[]{:S(2)}, u32[]{:S(2)}) collective-permute-start(bf16[64,576]{1,0:T(8,128)(2,1)} %hidden.1), channel_id=1, source_target_pairs={{0,24},{4,28},{8,16},{12,20},{16,8},{20,12},{24,0},{28,4},{1,25},{... | collective-permute-start | bytes 221192 | tf_op jit(solution)/shard_map/ppermute | solution.py:28
  5.7 0.6 collective-permute-start
  6.4 2.6 %collective-permute-done.2.refs_3_ = bf16[64,576]{1,0:T(8,128)(2,1)S(1)} collective-permute-done((bf16[64,576]{1,0:T(8,128)(2,1)}, bf16[64,576]{1,0:T(8,128)(2,1)S(1)}, u32[]{:S(2)}, u32[]{:S(2)}) %collective-permute-start.2) | collective-permute-done | bytes 73760 | tf_op jit(solution)/shard_map/ppermute | solution.py:28
  9.0 3.8 %collective-permute-done.1.refs_2_ = bf16[64,576]{1,0:T(8,128)(2,1)S(1)} collective-permute-done((bf16[64,576]{1,0:T(8,128)(2,1)}, bf16[64,576]{1,0:T(8,128)(2,1)S(1)}, u32[]{:S(2)}, u32[]{:S(2)}) %collective-permute-start.1) | collective-permute-done | bytes 73760 | tf_op jit(solution)/shard_map/ppermute | solution.py:28
  12.8 0.9 %copy-done.2 = bf16[64,576]{1,0:T(8,128)(2,1)S(1)} copy-done((bf16[64,576]{1,0:T(8,128)(2,1)S(1)}, bf16[64,576]{1,0:T(8,128)(2,1)}, u32[]{:S(2)}) %copy-start.2) | copy-done | bytes 73752
  13.7 0.3 strips.1.refs_0_
  14.0 1.6 %collective-permute-start.4 = (bf16[1152,128]{1,0:T(8,128)(2,1)S(1)}, bf16[1152,128]{1,0:T(8,128)(2,1)S(1)}, u32[]{:S(2)}, u32[]{:S(2)}) collective-permute-start(bf16[1152,128]{1,0:T(8,128)(2,1)S(1)} %strips.1.refs_0_), channel_id=1, source_target_pairs={{0,2},{1,5},{2,0},{3,7},{4,6},{5,1},{6,4},{7,3},{8,10},{9,13},{10,... | collective-permute-start | bytes 884744 | tf_op jit(solution)/shard_map/ppermute | solution.py:443
  15.6 1.5 %collective-permute-start.3 = (bf16[1152,128]{1,0:T(8,128)(2,1)S(1)}, bf16[1152,128]{1,0:T(8,128)(2,1)S(1)}, u32[]{:S(2)}, u32[]{:S(2)}) collective-permute-start(bf16[1152,128]{1,0:T(8,128)(2,1)S(1)} %strips.1.refs_0_), channel_id=1, source_target_pairs={{0,4},{1,3},{2,6},{3,1},{4,0},{5,7},{6,2},{7,5},{8,12},{9,11},{10,... | collective-permute-start | bytes 884744 | tf_op jit(solution)/shard_map/ppermute | solution.py:442
  17.1 3.6 %copy-done = bf16[1000,4608]{1,0:T(8,128)(2,1)S(1)} copy-done((bf16[1000,4608]{1,0:T(8,128)(2,1)S(1)}, bf16[1000,4608]{1,0:T(8,128)(2,1)}, u32[]{:S(2)}) %copy-start) | copy-done | bytes 9216024
  20.7 0.7 copy-done.5
  21.4 3.3 %turn_weight.1 = (bf16[2304,1000]{1,0:T(8,128)(2,1)S(1)}, bf16[2304,1000]{1,0:T(8,128)(2,1)S(1)}, bf16[4608,128]{1,0:T(8,128)(2,1)S(1)}, bf16[4608,128]{1,0:T(8,128)(2,1)S(1)}, s32[1,256]{1,0:T(1,128)S(1)}) custom-call(s32[4,64]{1,0:T(4,128)S(1)} %copy-done.5, bf16[1000,4608]{1,0:T(8,128)(2,1)S(1)} %copy-done), custom_call_target="tpu_custom_call" | custom-call | flops 2359296000 | bytes 18432000 | tf_op jit(solution)/shard_map/turn_weight/pallas_call | solution.py:411
  24.7 0.1 collective-permute-start.9
  24.8 0.6 collective-permute-start.5
  25.4 0.2 collective-permute-start.6
  25.6 0.7 gain_table.1.refs_8_
  26.2 0.4 collective-permute-start.8
  26.6 0.2 collective-permute-start.7
  26.8 0.8 %collective-permute-done.9.got = bf16[4608,128]{1,0:T(8,128)(2,1)S(1)} collective-permute-done((bf16[4608,128]{1,0:T(8,128)(2,1)S(1)}, bf16[4608,128]{1,0:T(8,128)(2,1)S(1)}, u32[]{:S(2)}, u32[]{:S(2)}) %collective-permute-start.9) | collective-permute-done | bytes 1179680 | tf_op jit(solution)/shard_map/ppermute | solution.py:28
  27.7 0.4 fold_rows.1
  28.1 3.5 %collective-permute-done.5.refs_3_ = bf16[1152,128]{1,0:T(8,128)(2,1)S(1)} collective-permute-done((bf16[1152,128]{1,0:T(8,128)(2,1)S(1)}, bf16[1152,128]{1,0:T(8,128)(2,1)S(1)}, u32[]{:S(2)}, u32[]{:S(2)}) %collective-permute-start.5) | collective-permute-done | bytes 294944 | tf_op jit(solution)/shard_map/ppermute | solution.py:443
  31.6 0.5 collective-permute-start.13
  32.2 1.0 %collective-permute-done.10.refs_7_ = bf16[1152,128]{1,0:T(8,128)(2,1)S(1)} collective-permute-done((bf16[1152,128]{1,0:T(8,128)(2,1)S(1)}, bf16[1152,128]{1,0:T(8,128)(2,1)S(1)}, u32[]{:S(2)}, u32[]{:S(2)}) %collective-permute-start.10) | collective-permute-done | bytes 294944 | tf_op jit(solution)/shard_map/ppermute | solution.py:28
  33.2 2.0 %norm.1 = (bf16[4608,256]{1,0:T(8,128)(2,1)S(1)}, f32[1,128]{1,0:T(1,128)S(1)}, f32[288,128]{1,0:T(8,128)S(1)}) custom-call(bf16[1152,128]{1,0:T(8,128)(2,1)S(1)} %strips.1.refs_0_, bf16[1152,128]{1,0:T(8,128)(2,1)S(1)} %collective-permute-done.3.refs_1_, bf16[1152,128]{1,0:T(8,128)(2,1)S(1)} %collective-permute-done.4.refs_2_, ...), custom_call_target="tpu_custom_call" | custom-call | flops 9437184 | tf_op jit(solution)/shard_map/norm/pallas_call | solution.py:411
  35.2 2.9 %fusion = (f32[256]{0:T(256)S(1)}, f32[256]{0:T(256)S(1)}, f32[256]{0:T(256)S(1)}, bf16[1000,256]{1,0:T(8,128)(2,1)S(1)}) fusion(s32[256]{0:T(256)S(1)} %bitcast.15, bf16[4608,256]{1,0:T(8,128)(2,1)S(1)} %get-tuple-element.52, bf16[1000,4608]{1,0:T(8,128)(2,1)S(1)} %copy-done.1), kind=kOutput, calls=%fused_computation.5 | convolution fusion | flops 2362623232 | bytes 12091392 | tf_op jit(solution)/shard_map/dot_general | solution.py:487
  38.1 0.2 collective-permute-start.11
  38.4 1.5 %fusion.3.grad.mine = f32[2304,256]{1,0:T(8,128)S(1)} fusion(bf16[2304,1000]{1,0:T(8,128)(2,1)S(1)} %get-tuple-element.54, bf16[1000,256]{1,0:T(8,128)(2,1)S(1)} %get-tuple-element.55), kind=kOutput, calls=%fused_computation.12 | convolution fusion | flops 1179648000 | bytes 7479296 | tf_op jit(solution)/shard_map/dot_general | solution.py:503
  39.8 0.1 post.2
  39.9 0.4 collective-permute-start.15
  40.4 0.6 collective-permute-start.12
  41.0 1.5 %fusion.4.grad.mine = f32[2304,256]{1,0:T(8,128)S(1)} fusion(bf16[2304,1000]{1,0:T(8,128)(2,1)S(1)} %get-tuple-element.44, bf16[1000,256]{1,0:T(8,128)(2,1)S(1)} %get-tuple-element.55), kind=kOutput, calls=%fused_computation.13 | convolution fusion | flops 1179648000 | bytes 7479296 | tf_op jit(solution)/shard_map/dot_general | solution.py:503
  42.4 1.6 %collective-permute-done.12 = f32[8,128]{1,0:T(8,128)S(1)} collective-permute-done((f32[8,128]{1,0:T(8,128)S(1)}, f32[8,128]{1,0:T(8,128)S(1)}, u32[]{:S(2)}, u32[]{:S(2)}) %collective-permute-start.12) | collective-permute-done | bytes 4128 | tf_op jit(solution)/shard_map/ppermute | solution.py:28
  44.0 0.1 post.3
  44.1 0.1 collective-permute-start.14
  44.2 0.6 collective-permute-start.18
  44.8 0.1 fold_core.2
  44.9 0.0 copy-start.6
  44.9 0.0 copy-start.7
  44.9 0.0 copy-start.3
  44.9 0.6 collective-permute-start.17
  45.5 0.7 collective-permute-done.14.got
  46.2 0.1 fold_core.3
  46.3 0.9 %collective-permute-start.16 = (bf16[1152,128]{1,0:T(8,128)(2,1)S(1)}, bf16[1152,128]{1,0:T(8,128)(2,1)S(1)}, u32[]{:S(2)}, u32[]{:S(2)}) collective-permute-start(bf16[1152,128]{1,0:T(8,128)(2,1)S(1)} %get-tuple-element.63), channel_id=1, source_target_pairs={{0,4},{1,3},{2,6},{3,1},{4,0},{5,7},{6,2},{7,5},{8,12},{9,11},{10,... | collective-permute-start | bytes 884744 | tf_op jit(solution)/shard_map/ppermute | solution.py:442
  47.2 0.6 collective-permute-done.18
  47.9 0.1 fusion.2
  48.0 0.1 maximum_add_fusion
  48.0 0.9 %collective-permute-start.19 = (f32[8,128]{1,0:T(8,128)S(1)}, f32[8,128]{1,0:T(8,128)S(1)}, u32[]{:S(2)}, u32[]{:S(2)}) collective-permute-start(f32[8,128]{1,0:T(8,128)S(1)} %maximum_add_fusion), channel_id=1, source_target_pairs={{0,8},{4,12},{8,0},{12,4},{16,24},{20,28},{24,16},{28,20},{1,9},{5... | collective-permute-start | bytes 12296 | tf_op jit(solution)/shard_map/ppermute | solution.py:28
  48.9 2.7 %collective-permute-done.19 = f32[8,128]{1,0:T(8,128)S(1)} collective-permute-done((f32[8,128]{1,0:T(8,128)S(1)}, f32[8,128]{1,0:T(8,128)S(1)}, u32[]{:S(2)}, u32[]{:S(2)}) %collective-permute-start.19) | collective-permute-done | bytes 4128 | tf_op jit(solution)/shard_map/ppermute | solution.py:28
  51.6 1.2 %collective-permute-start.20 = (f32[8,128]{1,0:T(8,128)S(1)}, f32[8,128]{1,0:T(8,128)S(1)}, u32[]{:S(2)}, u32[]{:S(2)}) collective-permute-start(f32[8,128]{1,0:T(8,128)S(1)} %add.11.sums), channel_id=1, source_target_pairs={{0,16},{4,20},{8,24},{12,28},{16,0},{20,4},{24,8},{28,12},{1,17},{... | collective-permute-start | bytes 12296 | tf_op jit(solution)/shard_map/ppermute | solution.py:28
  52.8 3.3 %collective-permute-done.20.heard = f32[8,128]{1,0:T(8,128)S(1)} collective-permute-done((f32[8,128]{1,0:T(8,128)S(1)}, f32[8,128]{1,0:T(8,128)S(1)}, u32[]{:S(2)}, u32[]{:S(2)}) %collective-permute-start.20) | collective-permute-done | bytes 4128 | tf_op jit(solution)/shard_map/ppermute | solution.py:28
  56.2 0.2 join_a.1
  56.4 0.9 %collective-permute-start.22 = (bf16[576,128]{1,0:T(8,128)(2,1)S(1)}, bf16[576,128]{1,0:T(8,128)(2,1)S(1)}, u32[]{:S(2)}, u32[]{:S(2)}) collective-permute-start(bf16[576,128]{1,0:T(8,128)(2,1)S(1)} %get-tuple-element.66), channel_id=1, source_target_pairs={{0,2},{1,5},{2,0},{3,7},{4,6},{5,1},{6,4},{7,3},{8,10},{9,13},{10,... | collective-permute-start | bytes 442376 | tf_op jit(solution)/shard_map/ppermute | solution.py:443
  57.3 0.2 join_b.1
  57.6 1.2 %collective-permute-start.21 = (bf16[576,128]{1,0:T(8,128)(2,1)S(1)}, bf16[576,128]{1,0:T(8,128)(2,1)S(1)}, u32[]{:S(2)}, u32[]{:S(2)}) collective-permute-start(bf16[576,128]{1,0:T(8,128)(2,1)S(1)} %get-tuple-element.69), channel_id=1, source_target_pairs={{0,2},{1,5},{2,0},{3,7},{4,6},{5,1},{6,4},{7,3},{8,10},{9,13},{10,... | collective-permute-start | bytes 442376 | tf_op jit(solution)/shard_map/ppermute | solution.py:443
  58.8 2.8 %collective-permute-done.22.got = bf16[576,128]{1,0:T(8,128)(2,1)S(1)} collective-permute-done((bf16[576,128]{1,0:T(8,128)(2,1)S(1)}, bf16[576,128]{1,0:T(8,128)(2,1)S(1)}, u32[]{:S(2)}, u32[]{:S(2)}) %collective-permute-start.22) | collective-permute-done | bytes 147488 | tf_op jit(solution)/shard_map/ppermute | solution.py:443
  61.6 0.1 fold_last_a.1
  61.7 2.7 %collective-permute-start.25 = (bf16[288,128]{1,0:T(8,128)(2,1)S(1)}, bf16[288,128]{1,0:T(8,128)(2,1)S(1)}, u32[]{:S(2)}, u32[]{:S(2)}) collective-permute-start(bf16[288,128]{1,0:T(8,128)(2,1)S(1)} %get-tuple-element.71), channel_id=1, source_target_pairs={{0,24},{4,28},{8,16},{12,20},{16,8},{20,12},{24,0},{28,4},{1,25},{... | collective-permute-start | bytes 221192 | tf_op jit(solution)/shard_map/ppermute | solution.py:28
  64.4 0.1 fold_last_b.1
  64.6 0.1 collective-permute-start.23
  64.6 1.9 %collective-permute-start.24 = (bf16[288,128]{1,0:T(8,128)(2,1)S(1)}, bf16[288,128]{1,0:T(8,128)(2,1)S(1)}, u32[]{:S(2)}, u32[]{:S(2)}) collective-permute-start(bf16[288,128]{1,0:T(8,128)(2,1)S(1)} %get-tuple-element.75), channel_id=1, source_target_pairs={{0,16},{4,20},{8,24},{12,28},{16,0},{20,4},{24,8},{28,12},{1,17},{... | collective-permute-start | bytes 221192 | tf_op jit(solution)/shard_map/ppermute | solution.py:28
  66.6 1.0 %tally.1 = (f32[8,128]{1,0:T(8,128)S(1)}, f32[1,4]{1,0:T(1,128)}, f32[1,1]{1,0:T(1,128)}) custom-call(f32[8,128]{1,0:T(8,128)S(1)} %add.11.sums, f32[8,128]{1,0:T(8,128)S(1)} %collective-permute-done.20.heard, s32[4,64]{1,0:T(4,128)S(1)} %copy-done.6, s32[4,8]{1,0:T(4,128)S(1)} %copy-done.7, f32[4,8]{1,0:T(4,128)S(1)} %copy-done.8), custom_call_target="tpu_custom_call" | custom-call | tf_op jit(solution)/shard_map/tally/pallas_call | solution.py:411
  67.6 0.3 collective-permute-done.25.three
  67.9 1.1 %collective-permute-done.23.one = bf16[288,128]{1,0:T(8,128)(2,1)S(1)} collective-permute-done((bf16[288,128]{1,0:T(8,128)(2,1)S(1)}, bf16[288,128]{1,0:T(8,128)(2,1)S(1)}, u32[]{:S(2)}, u32[]{:S(2)}) %collective-permute-start.23) | collective-permute-done | bytes 73760 | tf_op jit(solution)/shard_map/ppermute | solution.py:28
  69.0 1.0 %collective-permute-done.24.two = bf16[288,128]{1,0:T(8,128)(2,1)S(1)} collective-permute-done((bf16[288,128]{1,0:T(8,128)(2,1)S(1)}, bf16[288,128]{1,0:T(8,128)(2,1)S(1)}, u32[]{:S(2)}, u32[]{:S(2)}) %collective-permute-start.24) | collective-permute-done | bytes 73760 | tf_op jit(solution)/shard_map/ppermute | solution.py:28
  70.0 1.0 %finish.1 = f32[64,576]{1,0:T(8,128)} custom-call(f32[288,128]{1,0:T(8,128)S(1)} %get-tuple-element.73.mine, bf16[288,128]{1,0:T(8,128)(2,1)S(1)} %collective-permute-done.23.one, bf16[288,128]{1,0:T(8,128)(2,1)S(1)} %collective-permute-done.24.two, bf16[288,128]{1,0:T(8,128)(2,1)S(1)} %collective-permute-done.25.three, ...), custom_call_target="tpu_custom_call" | custom-call | tf_op jit(solution)/shard_map/finish/pallas_call | solution.py:411
  (30 shorter events, 0.1 us)
Async XLA Ops:
  0.6 8.4 %collective-permute-start.2 = (bf16[64,576]{1,0:T(8,128)(2,1)}, bf16[64,576]{1,0:T(8,128)(2,1)S(1)}, u32[]{:S(2)}, u32[]{:S(2)}) collective-permute-start(bf16[64,576]{1,0:T(8,128)(2,1)} %hidden.1), channel_id=1, source_target_pairs={{0,24},{4,28},{8,16},{12,20},{16,8},{20,12},{24,0},{28,4},{1,25},{... | collective-permute-start | bytes 221192 | tf_op jit(solution)/shard_map/ppermute | solution.py:28
  5.7 7.1 %collective-permute-start.1 = (bf16[64,576]{1,0:T(8,128)(2,1)}, bf16[64,576]{1,0:T(8,128)(2,1)S(1)}, u32[]{:S(2)}, u32[]{:S(2)}) collective-permute-start(bf16[64,576]{1,0:T(8,128)(2,1)} %hidden.1), channel_id=1, source_target_pairs={{0,16},{4,20},{8,24},{12,28},{16,0},{20,4},{24,8},{28,12},{1,17},{... | collective-permute-start | bytes 221192 | tf_op jit(solution)/shard_map/ppermute | solution.py:28
  5.7 7.1 %collective-permute-start = (bf16[64,576]{1,0:T(8,128)(2,1)}, bf16[64,576]{1,0:T(8,128)(2,1)S(1)}, u32[]{:S(2)}, u32[]{:S(2)}) collective-permute-start(bf16[64,576]{1,0:T(8,128)(2,1)} %hidden.1), channel_id=1, source_target_pairs={{0,8},{4,12},{8,0},{12,4},{16,24},{20,28},{24,16},{28,20},{1,9},{5... | collective-permute-start | bytes 221192 | tf_op jit(solution)/shard_map/ppermute | solution.py:28
  12.8 0.9 %copy-start.2 = (bf16[64,576]{1,0:T(8,128)(2,1)S(1)}, bf16[64,576]{1,0:T(8,128)(2,1)}, u32[]{:S(2)}) copy-start(bf16[64,576]{1,0:T(8,128)(2,1)} %hidden.1) | copy-start | bytes 221188
  13.7 11.9 %copy-start.4 = (f32[4608]{0:T(1024)S(1)}, f32[4608]{0:T(1024)}, u32[]{:S(2)}) copy-start(f32[4608]{0:T(1024)} %param.8) | copy-start | bytes 55300
  14.0 10.7 %collective-permute-start.4 = (bf16[1152,128]{1,0:T(8,128)(2,1)S(1)}, bf16[1152,128]{1,0:T(8,128)(2,1)S(1)}, u32[]{:S(2)}, u32[]{:S(2)}) collective-permute-start(bf16[1152,128]{1,0:T(8,128)(2,1)S(1)} %strips.1.refs_0_), channel_id=1, source_target_pairs={{0,2},{1,5},{2,0},{3,7},{4,6},{5,1},{6,4},{7,3},{8,10},{9,13},{10,... | collective-permute-start | bytes 884744 | tf_op jit(solution)/shard_map/ppermute | solution.py:443
  15.6 9.1 %collective-permute-start.3 = (bf16[1152,128]{1,0:T(8,128)(2,1)S(1)}, bf16[1152,128]{1,0:T(8,128)(2,1)S(1)}, u32[]{:S(2)}, u32[]{:S(2)}) collective-permute-start(bf16[1152,128]{1,0:T(8,128)(2,1)S(1)} %strips.1.refs_0_), channel_id=1, source_target_pairs={{0,4},{1,3},{2,6},{3,1},{4,0},{5,7},{6,2},{7,5},{8,12},{9,11},{10,... | collective-permute-start | bytes 884744 | tf_op jit(solution)/shard_map/ppermute | solution.py:442
  17.1 3.6 %copy-start = (bf16[1000,4608]{1,0:T(8,128)(2,1)S(1)}, bf16[1000,4608]{1,0:T(8,128)(2,1)}, u32[]{:S(2)}) copy-start(bf16[1000,4608]{1,0:T(8,128)(2,1)} %weight.1) | copy-start | bytes 27648004
  20.7 0.7 copy-start.5
  24.7 2.9 %collective-permute-start.9 = (bf16[4608,128]{1,0:T(8,128)(2,1)S(1)}, bf16[4608,128]{1,0:T(8,128)(2,1)S(1)}, u32[]{:S(2)}, u32[]{:S(2)}) collective-permute-start(bf16[4608,128]{1,0:T(8,128)(2,1)S(1)} %get-tuple-element.48), channel_id=1, source_target_pairs={{0,1},{1,0},{2,3},{3,2},{4,5},{5,4},{6,7},{7,6},{8,9},{9,8},{10,11... | collective-permute-start | bytes 3538952 | tf_op jit(solution)/shard_map/ppermute | solution.py:28
  24.8 6.8 %collective-permute-start.5 = (bf16[1152,128]{1,0:T(8,128)(2,1)S(1)}, bf16[1152,128]{1,0:T(8,128)(2,1)S(1)}, u32[]{:S(2)}, u32[]{:S(2)}) collective-permute-start(bf16[1152,128]{1,0:T(8,128)(2,1)S(1)} %collective-permute-done.3.refs_1_), channel_id=1, source_target_pairs={{0,2},{1,5},{2,0},{3,7},{4,6},{5,1},{6,4},{7,3},{8,10},{9,13},{10,... | collective-permute-start | bytes 884744 | tf_op jit(solution)/shard_map/ppermute | solution.py:443
  25.4 6.8 %collective-permute-start.6 = (bf16[1152,128]{1,0:T(8,128)(2,1)S(1)}, bf16[1152,128]{1,0:T(8,128)(2,1)S(1)}, u32[]{:S(2)}, u32[]{:S(2)}) collective-permute-start(bf16[1152,128]{1,0:T(8,128)(2,1)S(1)} %strips.1.refs_0_), channel_id=1, source_target_pairs={{0,1},{1,0},{2,3},{3,2},{4,5},{5,4},{6,7},{7,6},{8,9},{9,8},{10,11... | collective-permute-start | bytes 884744 | tf_op jit(solution)/shard_map/ppermute | solution.py:28
  25.6 9.6 %copy-start.1 = (bf16[1000,4608]{1,0:T(8,128)(2,1)S(1)}, bf16[1000,4608]{1,0:T(8,128)(2,1)}, u32[]{:S(2)}) copy-start(bf16[1000,4608]{1,0:T(8,128)(2,1)} %weight.1) | copy-start | bytes 27648004
  26.2 5.9 %collective-permute-start.8 = (bf16[1152,128]{1,0:T(8,128)(2,1)S(1)}, bf16[1152,128]{1,0:T(8,128)(2,1)S(1)}, u32[]{:S(2)}, u32[]{:S(2)}) collective-permute-start(bf16[1152,128]{1,0:T(8,128)(2,1)S(1)} %collective-permute-done.4.refs_2_), channel_id=1, source_target_pairs={{0,1},{1,0},{2,3},{3,2},{4,5},{5,4},{6,7},{7,6},{8,9},{9,8},{10,11... | collective-permute-start | bytes 884744 | tf_op jit(solution)/shard_map/ppermute | solution.py:28
  26.6 5.5 %collective-permute-start.7 = (bf16[1152,128]{1,0:T(8,128)(2,1)S(1)}, bf16[1152,128]{1,0:T(8,128)(2,1)S(1)}, u32[]{:S(2)}, u32[]{:S(2)}) collective-permute-start(bf16[1152,128]{1,0:T(8,128)(2,1)S(1)} %collective-permute-done.3.refs_1_), channel_id=1, source_target_pairs={{0,1},{1,0},{2,3},{3,2},{4,5},{5,4},{6,7},{7,6},{8,9},{9,8},{10,11... | collective-permute-start | bytes 884744 | tf_op jit(solution)/shard_map/ppermute | solution.py:28
  31.6 1.6 %collective-permute-start.10 = (bf16[1152,128]{1,0:T(8,128)(2,1)S(1)}, bf16[1152,128]{1,0:T(8,128)(2,1)S(1)}, u32[]{:S(2)}, u32[]{:S(2)}) collective-permute-start(bf16[1152,128]{1,0:T(8,128)(2,1)S(1)} %collective-permute-done.5.refs_3_), channel_id=1, source_target_pairs={{0,1},{1,0},{2,3},{3,2},{4,5},{5,4},{6,7},{7,6},{8,9},{9,8},{10,11... | collective-permute-start | bytes 884744 | tf_op jit(solution)/shard_map/ppermute | solution.py:28
  31.6 12.5 %collective-permute-start.13 = (bf16[2304,128]{1,0:T(8,128)(2,1)S(1)}, bf16[2304,128]{1,0:T(8,128)(2,1)S(1)}, u32[]{:S(2)}, u32[]{:S(2)}) collective-permute-start(bf16[2304,128]{1,0:T(8,128)(2,1)S(1)} %get-tuple-element.57), channel_id=1, source_target_pairs={{0,4},{1,3},{2,6},{3,1},{4,0},{5,7},{6,2},{7,5},{8,12},{9,11},{10,... | collective-permute-start | bytes 1769480 | tf_op jit(solution)/shard_map/ppermute | solution.py:442
  38.1 2.2 %collective-permute-start.11 = (f32[3,256]{1,0:T(4,128)S(1)}, f32[3,256]{1,0:T(4,128)S(1)}, u32[]{:S(2)}, u32[]{:S(2)}) collective-permute-start(f32[3,256]{1,0:T(4,128)S(1)} %pad_maximum_fusion.stats), channel_id=1, source_target_pairs={{0,1},{1,0},{2,3},{3,2},{4,5},{5,4},{6,7},{7,6},{8,9},{9,8},{10,11... | collective-permute-start | bytes 9224 | tf_op jit(solution)/shard_map/ppermute | solution.py:28
  39.9 4.9 %collective-permute-start.15 = (bf16[2304,128]{1,0:T(8,128)(2,1)S(1)}, bf16[2304,128]{1,0:T(8,128)(2,1)S(1)}, u32[]{:S(2)}, u32[]{:S(2)}) collective-permute-start(bf16[2304,128]{1,0:T(8,128)(2,1)S(1)} %post.2), channel_id=1, source_target_pairs={{0,1},{1,0},{2,3},{3,2},{4,5},{5,4},{6,7},{7,6},{8,9},{9,8},{10,11... | collective-permute-start | bytes 1769480 | tf_op jit(solution)/shard_map/ppermute | solution.py:28
  40.4 3.7 %collective-permute-start.12 = (f32[8,128]{1,0:T(8,128)S(1)}, f32[8,128]{1,0:T(8,128)S(1)}, u32[]{:S(2)}, u32[]{:S(2)}) collective-permute-start(f32[8,128]{1,0:T(8,128)S(1)} %count.1), channel_id=1, source_target_pairs={{0,4},{4,0},{8,12},{12,8},{16,20},{20,16},{24,28},{28,24},{1,5},{5... | collective-permute-start | bytes 12296 | tf_op jit(solution)/shard_map/ppermute | solution.py:28
  44.1 2.1 %collective-permute-start.14 = (bf16[2304,128]{1,0:T(8,128)(2,1)S(1)}, bf16[2304,128]{1,0:T(8,128)(2,1)S(1)}, u32[]{:S(2)}, u32[]{:S(2)}) collective-permute-start(bf16[2304,128]{1,0:T(8,128)(2,1)S(1)} %post.3), channel_id=1, source_target_pairs={{0,1},{1,0},{2,3},{3,2},{4,5},{5,4},{6,7},{7,6},{8,9},{9,8},{10,11... | collective-permute-start | bytes 1769480 | tf_op jit(solution)/shard_map/ppermute | solution.py:28
  44.2 3.7 %collective-permute-start.18 = (f32[8,128]{1,0:T(8,128)S(1)}, f32[8,128]{1,0:T(8,128)S(1)}, u32[]{:S(2)}, u32[]{:S(2)}) collective-permute-start(f32[8,128]{1,0:T(8,128)S(1)} %add.9), channel_id=1, source_target_pairs={{0,2},{1,3},{2,0},{3,1},{4,6},{5,7},{6,4},{7,5},{8,10},{9,11},{10,... | collective-permute-start | bytes 12296 | tf_op jit(solution)/shard_map/ppermute | solution.py:28
  44.9 21.7 %copy-start.6 = (s32[4,64]{1,0:T(4,128)S(1)}, s32[4,64]{1,0:T(4,128)}, u32[]{:S(2)}) copy-start(s32[4,64]{1,0:T(4,128)} %segments.1) | copy-start | bytes 3076
  44.9 21.7 %copy-start.7 = (s32[4,8]{1,0:T(4,128)S(1)}, s32[4,8]{1,0:T(4,128)}, u32[]{:S(2)}) copy-start(s32[4,8]{1,0:T(4,128)} %pairing.1) | copy-start | bytes 388
  44.9 21.7 %copy-start.8 = (f32[4,8]{1,0:T(4,128)S(1)}, f32[4,8]{1,0:T(4,128)}, u32[]{:S(2)}) copy-start(f32[4,8]{1,0:T(4,128)} %ref_logp.1) | copy-start | bytes 388
  44.9 25.0 %copy-start.3 = (bf16[64,576]{1,0:T(8,128)(2,1)S(1)}, bf16[64,576]{1,0:T(8,128)(2,1)}, u32[]{:S(2)}) copy-start(bf16[64,576]{1,0:T(8,128)(2,1)} %hidden.1) | copy-start | bytes 221188
  44.9 11.2 %collective-permute-start.17 = (bf16[1152,128]{1,0:T(8,128)(2,1)S(1)}, bf16[1152,128]{1,0:T(8,128)(2,1)S(1)}, u32[]{:S(2)}, u32[]{:S(2)}) collective-permute-start(bf16[1152,128]{1,0:T(8,128)(2,1)S(1)} %get-tuple-element.60), channel_id=1, source_target_pairs={{0,4},{1,3},{2,6},{3,1},{4,0},{5,7},{6,2},{7,5},{8,12},{9,11},{10,... | collective-permute-start | bytes 884744 | tf_op jit(solution)/shard_map/ppermute | solution.py:442
  46.3 11.0 %collective-permute-start.16 = (bf16[1152,128]{1,0:T(8,128)(2,1)S(1)}, bf16[1152,128]{1,0:T(8,128)(2,1)S(1)}, u32[]{:S(2)}, u32[]{:S(2)}) collective-permute-start(bf16[1152,128]{1,0:T(8,128)(2,1)S(1)} %get-tuple-element.63), channel_id=1, source_target_pairs={{0,4},{1,3},{2,6},{3,1},{4,0},{5,7},{6,2},{7,5},{8,12},{9,11},{10,... | collective-permute-start | bytes 884744 | tf_op jit(solution)/shard_map/ppermute | solution.py:442
  48.0 3.6 %collective-permute-start.19 = (f32[8,128]{1,0:T(8,128)S(1)}, f32[8,128]{1,0:T(8,128)S(1)}, u32[]{:S(2)}, u32[]{:S(2)}) collective-permute-start(f32[8,128]{1,0:T(8,128)S(1)} %maximum_add_fusion), channel_id=1, source_target_pairs={{0,8},{4,12},{8,0},{12,4},{16,24},{20,28},{24,16},{28,20},{1,9},{5... | collective-permute-start | bytes 12296 | tf_op jit(solution)/shard_map/ppermute | solution.py:28
  51.6 4.5 %collective-permute-start.20 = (f32[8,128]{1,0:T(8,128)S(1)}, f32[8,128]{1,0:T(8,128)S(1)}, u32[]{:S(2)}, u32[]{:S(2)}) collective-permute-start(f32[8,128]{1,0:T(8,128)S(1)} %add.11.sums), channel_id=1, source_target_pairs={{0,16},{4,20},{8,24},{12,28},{16,0},{20,4},{24,8},{28,12},{1,17},{... | collective-permute-start | bytes 12296 | tf_op jit(solution)/shard_map/ppermute | solution.py:28
  56.4 5.2 %collective-permute-start.22 = (bf16[576,128]{1,0:T(8,128)(2,1)S(1)}, bf16[576,128]{1,0:T(8,128)(2,1)S(1)}, u32[]{:S(2)}, u32[]{:S(2)}) collective-permute-start(bf16[576,128]{1,0:T(8,128)(2,1)S(1)} %get-tuple-element.66), channel_id=1, source_target_pairs={{0,2},{1,5},{2,0},{3,7},{4,6},{5,1},{6,4},{7,3},{8,10},{9,13},{10,... | collective-permute-start | bytes 442376 | tf_op jit(solution)/shard_map/ppermute | solution.py:443
  57.6 6.9 %collective-permute-start.21 = (bf16[576,128]{1,0:T(8,128)(2,1)S(1)}, bf16[576,128]{1,0:T(8,128)(2,1)S(1)}, u32[]{:S(2)}, u32[]{:S(2)}) collective-permute-start(bf16[576,128]{1,0:T(8,128)(2,1)S(1)} %get-tuple-element.69), channel_id=1, source_target_pairs={{0,2},{1,5},{2,0},{3,7},{4,6},{5,1},{6,4},{7,3},{8,10},{9,13},{10,... | collective-permute-start | bytes 442376 | tf_op jit(solution)/shard_map/ppermute | solution.py:443
  61.7 6.2 %collective-permute-start.25 = (bf16[288,128]{1,0:T(8,128)(2,1)S(1)}, bf16[288,128]{1,0:T(8,128)(2,1)S(1)}, u32[]{:S(2)}, u32[]{:S(2)}) collective-permute-start(bf16[288,128]{1,0:T(8,128)(2,1)S(1)} %get-tuple-element.71), channel_id=1, source_target_pairs={{0,24},{4,28},{8,16},{12,20},{16,8},{20,12},{24,0},{28,4},{1,25},{... | collective-permute-start | bytes 221192 | tf_op jit(solution)/shard_map/ppermute | solution.py:28
  64.6 4.4 %collective-permute-start.23 = (bf16[288,128]{1,0:T(8,128)(2,1)S(1)}, bf16[288,128]{1,0:T(8,128)(2,1)S(1)}, u32[]{:S(2)}, u32[]{:S(2)}) collective-permute-start(bf16[288,128]{1,0:T(8,128)(2,1)S(1)} %get-tuple-element.76), channel_id=1, source_target_pairs={{0,8},{4,12},{8,0},{12,4},{16,24},{20,28},{24,16},{28,20},{1,9},{5... | collective-permute-start | bytes 221192 | tf_op jit(solution)/shard_map/ppermute | solution.py:28
  64.6 5.3 %collective-permute-start.24 = (bf16[288,128]{1,0:T(8,128)(2,1)S(1)}, bf16[288,128]{1,0:T(8,128)(2,1)S(1)}, u32[]{:S(2)}, u32[]{:S(2)}) collective-permute-start(bf16[288,128]{1,0:T(8,128)(2,1)S(1)} %get-tuple-element.75), channel_id=1, source_target_pairs={{0,16},{4,20},{8,24},{12,28},{16,0},{20,4},{24,8},{28,12},{1,17},{... | collective-permute-start | bytes 221192 | tf_op jit(solution)/shard_map/ppermute | solution.py:28

commit v3 on v2

--- a/solution.py
+++ b/solution.py
@@ -193,11 +193,10 @@
     return [ids[pl.ds(dp ^ ((r & 1) * 2 + (r >> 1)), 1), :] for r in range(4)]
 
 
-def turn_kernel(cols, n_z, targets, weight, turned_a, turned_b, keep, send, flat, hot):
-    z, x, _, _, index = whereabouts()
+def turn_kernel(cols, n_z, flat, weight, turned_a, turned_b, keep, send, hot):
+    z, x, _, _, _ = whereabouts()
     vocab = weight.shape[0]
     block = 2 * cols
-    flat[...] = jnp.concatenate(relative_rows(targets), axis=1) - index * vocab
     row = lax.broadcasted_iota(jnp.int32, hot.shape, 0)
     hot[...] = jnp.where(row == flat[...], 1.0, 0.0).astype(jnp.bfloat16)
     for k in range(n_z):
@@ -217,13 +216,23 @@
             send[pl.ds(here, cols), :] = rows[:, LANES:]
 
 
-def strips_kernel(*refs):
+def flip(strip):
+    flipped = wide(strip).T
+    rows = flipped.shape[0] // 2
+    return jnp.concatenate([flipped[:rows], flipped[rows:]], axis=1).astype(jnp.bfloat16)
+
+
+def own_strip_kernel(vocab, strip, targets, out, flat):
+    out[...] = flip(strip[...])
+    flat[...] = jnp.concatenate(relative_rows(targets), axis=1) - whereabouts()[4] * vocab
+
+
+def strips_kernel(own, *refs):
     strips, out = refs[:-1], refs[-1]
-    rows = out.shape[0] // len(strips)
+    rows = own.shape[0]
+    out[:rows, :] = own[...]
     for k, strip in enumerate(strips):
-        flipped = wide(strip[...]).T
-        both = jnp.concatenate([flipped[:rows], flipped[rows:]], axis=1)
-        out[k * rows : (k + 1) * rows, :] = both.astype(out.dtype)
+        out[(k + 1) * rows : (k + 2) * rows, :] = flip(strip[...])
 
 
 def gain_kernel(gain, table):
@@ -451,16 +460,21 @@
 
     strips = [hidden] + [over_z(hidden, k) for k in range(1, n_z)]
 
+    strips[0], flat = call(
+        functools.partial(own_strip_kernel, vocab), "own_strip",
+        (shape((cols // 2, LANES), half), shape((1, tokens), jnp.int32)),
+        [VMEM, VMEM], (VMEM, VMEM), [], 4, 0, 16 * width * LANES, hidden, targets,
+    )
     base = call(
         strips_kernel, "strips", shape((n_z * cols // 2, LANES), half), [VMEM] * n_z, VMEM, [], 4,
         tok * width, 0, *strips,
     )
-    turned_a, turned_b, hit_keep, hit_send, flat = call(
+    turned_a, turned_b, hit_keep, hit_send = call(
         functools.partial(turn_kernel, cols, n_z), "turn_weight",
         (shape((width // 2, vocab), half),) * 2
-        + (shape((width, LANES), half), shape((width, LANES), half), shape((1, tokens), jnp.int32)),
-        [VMEM, VMEM], (VMEM,) * 5, [pltpu.VMEM((vocab, tokens), half)],
-        8, 2 * tokens * vocab * width, 4 * vocab * width, hold(targets, base), weight,
+        + (shape((width, LANES), half),) * 2,
+        [VMEM, VMEM], (VMEM,) * 4, [pltpu.VMEM((vocab, tokens), half)],
+        8, 2 * tokens * vocab * width, 4 * vocab * width, hold(flat, base), weight,
     )
 
     one = to_one(base)

time: 71.2 us -> 70.8 us (level)
  waiting for transfers between devices: 25.9 us -> 24.3 us
  starting transfers between devices: 23.1 us -> 24.3 us
    ppermute x18, waiting for transfers between devices: 19.6 us -> 17.9 us  [exchange(): return lax.ppermute(arr, axis, [(i, i ^ mask) for i in range(size)])]
    ppermute x18, starting transfers between devices: 15.3 us -> 16.4 us  [exchange(): return lax.ppermute(arr, axis, [(i, i ^ mask) for i in range(size)])]
    pallas_call x16 -> x17, Pallas kernels: 9.85 us -> 9.97 us  [call(): pl.pallas_call(kernel, out_shape=outs, in_specs=in_specs, out_specs=out_s...]
  transfers between devices with their start and end apart: 26 -> 26, of which waited for: 14 -> 15; matrix products, arithmetic and copies ran while one was open for 8% -> 8% of each run, Pallas kernels for 12% -> 12%
where the time goes in v3:
time: 70.8 us; the launch traced here: 70.5 us
  starting transfers between devices  24.3 us (34%)
  waiting for transfers between devices  24.3 us (34%)
  Pallas kernels  9.97 us (14%)
  matrix products  5.68 us (8%)
  local copies, waits for them, and re-layouts  5.35 us (8%)
  between operations  0.86 us (1%)
    ppermute x18, waiting for transfers between devices, exchange(): return lax.ppermute(arr, axis, [(i, i ^ mask) for i in range(size)])  17.9 us
    ppermute x18, starting transfers between devices, exchange(): return lax.ppermute(arr, axis, [(i, i ^ mask) for i in range(size)])  16.4 us
    pallas_call x17, Pallas kernels, call(): pl.pallas_call(kernel, out_shape=outs, in_specs=in_specs, out_specs=out_s...  9.97 us
    ppermute x4, waiting for transfers between devices, fast_path(): to_two = lambda a: lax.ppermute(a, both_axes, two_pairs)  6.31 us
    unnamed x18, local copies, waits for them, and re-layouts  5.28 us
    ppermute x4, starting transfers between devices, fast_path(): to_two = lambda a: lax.ppermute(a, both_axes, two_pairs)  4.4 us
    ppermute x4, starting transfers between devices, fast_path(): to_one = lambda a: lax.ppermute(a, both_axes, one_pairs)  3.48 us
    dot_general x1, matrix products, fast_path(): lax.dot_general(weight, normed, (((1,), (0,)), ((), ())), preferred_eleme...  2.9 us
  transfers between devices with their start and end apart: 26, of which 15 were waited for; matrix products, arithmetic and copies ran while one was open for 8% of the time, Pallas kernels for 12%

profile of v3, /device:TPU:0, one launch (start us, length us, event | category | flops | bytes accessed | tf_op | source)
XLA Modules:
  0.0 70.5 jit_solution(82246158061440773)
XLA Ops:
  0.6 4.1 %collective-permute-start.1 = (bf16[64,576]{1,0:T(8,128)(2,1)}, bf16[64,576]{1,0:T(8,128)(2,1)S(1)}, u32[]{:S(2)}, u32[]{:S(2)}) collective-permute-start(bf16[64,576]{1,0:T(8,128)(2,1)} %hidden.1), channel_id=1, source_target_pairs={{0,16},{4,20},{8,24},{12,28},{16,0},{20,4},{24,8},{28,12},{1,17},{... | collective-permute-start | bytes 221192 | tf_op jit(solution)/shard_map/ppermute | solution.py:28
  4.7 1.6 %collective-permute-start = (bf16[64,576]{1,0:T(8,128)(2,1)}, bf16[64,576]{1,0:T(8,128)(2,1)S(1)}, u32[]{:S(2)}, u32[]{:S(2)}) collective-permute-start(bf16[64,576]{1,0:T(8,128)(2,1)} %hidden.1), channel_id=1, source_target_pairs={{0,8},{4,12},{8,0},{12,4},{16,24},{20,28},{24,16},{28,20},{1,9},{5... | collective-permute-start | bytes 221192 | tf_op jit(solution)/shard_map/ppermute | solution.py:28
  6.3 1.0 %copy-done.2 = bf16[64,576]{1,0:T(8,128)(2,1)S(1)} copy-done((bf16[64,576]{1,0:T(8,128)(2,1)S(1)}, bf16[64,576]{1,0:T(8,128)(2,1)}, u32[]{:S(2)}) %copy-start.2) | copy-done | bytes 73752
  7.3 0.7 copy-done.8
  7.9 0.2 own_strip.1
  8.1 0.8 %collective-permute-done.1.refs_1_ = bf16[64,576]{1,0:T(8,128)(2,1)S(1)} collective-permute-done((bf16[64,576]{1,0:T(8,128)(2,1)}, bf16[64,576]{1,0:T(8,128)(2,1)S(1)}, u32[]{:S(2)}, u32[]{:S(2)}) %collective-permute-start.1) | collective-permute-done | bytes 73760 | tf_op jit(solution)/shard_map/ppermute | solution.py:28
  9.0 0.5 collective-permute-done.refs_0_
  9.5 3.3 %collective-permute-done.2.refs_2_ = bf16[64,576]{1,0:T(8,128)(2,1)S(1)} collective-permute-done((bf16[64,576]{1,0:T(8,128)(2,1)}, bf16[64,576]{1,0:T(8,128)(2,1)S(1)}, u32[]{:S(2)}, u32[]{:S(2)}) %collective-permute-start.2) | collective-permute-done | bytes 73760 | tf_op jit(solution)/shard_map/ppermute | solution.py:28
  12.8 0.3 strips.1.refs_0_
  13.0 1.7 %collective-permute-start.4 = (bf16[1152,128]{1,0:T(8,128)(2,1)S(1)}, bf16[1152,128]{1,0:T(8,128)(2,1)S(1)}, u32[]{:S(2)}, u32[]{:S(2)}) collective-permute-start(bf16[1152,128]{1,0:T(8,128)(2,1)S(1)} %strips.1.refs_0_), channel_id=1, source_target_pairs={{0,2},{1,5},{2,0},{3,7},{4,6},{5,1},{6,4},{7,3},{8,10},{9,13},{10,... | collective-permute-start | bytes 884744 | tf_op jit(solution)/shard_map/ppermute | solution.py:452
  14.7 1.5 %collective-permute-start.3 = (bf16[1152,128]{1,0:T(8,128)(2,1)S(1)}, bf16[1152,128]{1,0:T(8,128)(2,1)S(1)}, u32[]{:S(2)}, u32[]{:S(2)}) collective-permute-start(bf16[1152,128]{1,0:T(8,128)(2,1)S(1)} %strips.1.refs_0_), channel_id=1, source_target_pairs={{0,4},{1,3},{2,6},{3,1},{4,0},{5,7},{6,2},{7,5},{8,12},{9,11},{10,... | collective-permute-start | bytes 884744 | tf_op jit(solution)/shard_map/ppermute | solution.py:451
  16.2 3.6 %copy-done = bf16[1000,4608]{1,0:T(8,128)(2,1)S(1)} copy-done((bf16[1000,4608]{1,0:T(8,128)(2,1)S(1)}, bf16[1000,4608]{1,0:T(8,128)(2,1)}, u32[]{:S(2)}) %copy-start) | copy-done | bytes 9216024
  19.8 3.3 %turn_weight.1 = (bf16[2304,1000]{1,0:T(8,128)(2,1)S(1)}, bf16[2304,1000]{1,0:T(8,128)(2,1)S(1)}, bf16[4608,128]{1,0:T(8,128)(2,1)S(1)}, bf16[4608,128]{1,0:T(8,128)(2,1)S(1)}) custom-call(s32[1,256]{1,0:T(1,128)S(1)} %get-tuple-element.46.flat, bf16[1000,4608]{1,0:T(8,128)(2,1)S(1)} %copy-done), custom_call_target="tpu_custom_call" | custom-call | flops 2359296000 | bytes 18432000 | tf_op jit(solution)/shard_map/turn_weight/pallas_call | solution.py:420
  23.1 0.1 collective-permute-start.9
  23.2 0.6 collective-permute-start.5
  23.7 0.2 collective-permute-start.6
  23.9 0.7 gain_table.1.refs_8_
  24.6 0.4 collective-permute-start.8
  25.0 0.2 collective-permute-start.7
  25.2 0.8 %collective-permute-done.9.got = bf16[4608,128]{1,0:T(8,128)(2,1)S(1)} collective-permute-done((bf16[4608,128]{1,0:T(8,128)(2,1)S(1)}, bf16[4608,128]{1,0:T(8,128)(2,1)S(1)}, u32[]{:S(2)}, u32[]{:S(2)}) %collective-permute-start.9) | collective-permute-done | bytes 1179680 | tf_op jit(solution)/shard_map/ppermute | solution.py:28
  26.0 0.4 fold_rows.1
  26.5 3.5 %collective-permute-done.5.refs_3_ = bf16[1152,128]{1,0:T(8,128)(2,1)S(1)} collective-permute-done((bf16[1152,128]{1,0:T(8,128)(2,1)S(1)}, bf16[1152,128]{1,0:T(8,128)(2,1)S(1)}, u32[]{:S(2)}, u32[]{:S(2)}) %collective-permute-start.5) | collective-permute-done | bytes 294944 | tf_op jit(solution)/shard_map/ppermute | solution.py:452
  30.0 0.5 collective-permute-start.13
  30.5 1.0 %collective-permute-done.10.refs_7_ = bf16[1152,128]{1,0:T(8,128)(2,1)S(1)} collective-permute-done((bf16[1152,128]{1,0:T(8,128)(2,1)S(1)}, bf16[1152,128]{1,0:T(8,128)(2,1)S(1)}, u32[]{:S(2)}, u32[]{:S(2)}) %collective-permute-start.10) | collective-permute-done | bytes 294944 | tf_op jit(solution)/shard_map/ppermute | solution.py:28
  31.5 2.0 %norm.1 = (bf16[4608,256]{1,0:T(8,128)(2,1)S(1)}, f32[1,128]{1,0:T(1,128)S(1)}, f32[288,128]{1,0:T(8,128)S(1)}) custom-call(bf16[1152,128]{1,0:T(8,128)(2,1)S(1)} %strips.1.refs_0_, bf16[1152,128]{1,0:T(8,128)(2,1)S(1)} %collective-permute-done.3.refs_1_, bf16[1152,128]{1,0:T(8,128)(2,1)S(1)} %collective-permute-done.4.refs_2_, ...), custom_call_target="tpu_custom_call" | custom-call | flops 9437184 | tf_op jit(solution)/shard_map/norm/pallas_call | solution.py:420
  33.6 2.9 %fusion = (f32[256]{0:T(256)S(1)}, f32[256]{0:T(256)S(1)}, f32[256]{0:T(256)S(1)}, bf16[1000,256]{1,0:T(8,128)(2,1)S(1)}) fusion(s32[256]{0:T(256)S(1)} %bitcast.15, bf16[4608,256]{1,0:T(8,128)(2,1)S(1)} %get-tuple-element.54, bf16[1000,4608]{1,0:T(8,128)(2,1)S(1)} %copy-done.1), kind=kOutput, calls=%fused_computation.5 | convolution fusion | flops 2362623232 | bytes 12091392 | tf_op jit(solution)/shard_map/dot_general | solution.py:501
  36.5 0.2 collective-permute-start.11
  36.7 1.4 %fusion.3.grad.mine = f32[2304,256]{1,0:T(8,128)S(1)} fusion(bf16[2304,1000]{1,0:T(8,128)(2,1)S(1)} %get-tuple-element.56, bf16[1000,256]{1,0:T(8,128)(2,1)S(1)} %get-tuple-element.57), kind=kOutput, calls=%fused_computation.12 | convolution fusion | flops 1179648000 | bytes 7479296 | tf_op jit(solution)/shard_map/dot_general | solution.py:517
  38.1 0.1 post.2
  38.2 0.4 collective-permute-start.15
  38.7 0.6 collective-permute-start.12
  39.3 1.4 %fusion.4.grad.mine = f32[2304,256]{1,0:T(8,128)S(1)} fusion(bf16[2304,1000]{1,0:T(8,128)(2,1)S(1)} %get-tuple-element.47, bf16[1000,256]{1,0:T(8,128)(2,1)S(1)} %get-tuple-element.57), kind=kOutput, calls=%fused_computation.13 | convolution fusion | flops 1179648000 | bytes 7479296 | tf_op jit(solution)/shard_map/dot_general | solution.py:517
  40.7 1.7 %collective-permute-done.12 = f32[8,128]{1,0:T(8,128)S(1)} collective-permute-done((f32[8,128]{1,0:T(8,128)S(1)}, f32[8,128]{1,0:T(8,128)S(1)}, u32[]{:S(2)}, u32[]{:S(2)}) %collective-permute-start.12) | collective-permute-done | bytes 4128 | tf_op jit(solution)/shard_map/ppermute | solution.py:28
  42.3 0.1 post.3
  42.4 0.1 collective-permute-start.14
  42.5 0.6 collective-permute-start.18
  43.1 0.1 fold_core.2
  43.2 0.0 copy-start.7
  43.2 0.5 collective-permute-start.17
  43.8 0.7 %collective-permute-done.14.got = bf16[2304,128]{1,0:T(8,128)(2,1)S(1)} collective-permute-done((bf16[2304,128]{1,0:T(8,128)(2,1)S(1)}, bf16[2304,128]{1,0:T(8,128)(2,1)S(1)}, u32[]{:S(2)}, u32[]{:S(2)}) %collective-permute-start.14) | collective-permute-done | bytes 589856 | tf_op jit(solution)/shard_map/ppermute | solution.py:28
  44.5 0.1 fold_core.3
  44.6 0.9 %collective-permute-start.16 = (bf16[1152,128]{1,0:T(8,128)(2,1)S(1)}, bf16[1152,128]{1,0:T(8,128)(2,1)S(1)}, u32[]{:S(2)}, u32[]{:S(2)}) collective-permute-start(bf16[1152,128]{1,0:T(8,128)(2,1)S(1)} %get-tuple-element.65), channel_id=1, source_target_pairs={{0,4},{1,3},{2,6},{3,1},{4,0},{5,7},{6,2},{7,5},{8,12},{9,11},{10,... | collective-permute-start | bytes 884744 | tf_op jit(solution)/shard_map/ppermute | solution.py:451
  45.5 0.6 collective-permute-done.18
  46.2 0.1 fusion.2
  46.2 0.1 maximum_add_fusion
  46.3 0.9 %collective-permute-start.19 = (f32[8,128]{1,0:T(8,128)S(1)}, f32[8,128]{1,0:T(8,128)S(1)}, u32[]{:S(2)}, u32[]{:S(2)}) collective-permute-start(f32[8,128]{1,0:T(8,128)S(1)} %maximum_add_fusion), channel_id=1, source_target_pairs={{0,8},{4,12},{8,0},{12,4},{16,24},{20,28},{24,16},{28,20},{1,9},{5... | collective-permute-start | bytes 12296 | tf_op jit(solution)/shard_map/ppermute | solution.py:28
  47.2 2.8 %collective-permute-done.19 = f32[8,128]{1,0:T(8,128)S(1)} collective-permute-done((f32[8,128]{1,0:T(8,128)S(1)}, f32[8,128]{1,0:T(8,128)S(1)}, u32[]{:S(2)}, u32[]{:S(2)}) %collective-permute-start.19) | collective-permute-done | bytes 4128 | tf_op jit(solution)/shard_map/ppermute | solution.py:28
  49.9 2.7 %collective-permute-start.20 = (f32[8,128]{1,0:T(8,128)S(1)}, f32[8,128]{1,0:T(8,128)S(1)}, u32[]{:S(2)}, u32[]{:S(2)}) collective-permute-start(f32[8,128]{1,0:T(8,128)S(1)} %add.11.sums), channel_id=1, source_target_pairs={{0,16},{4,20},{8,24},{12,28},{16,0},{20,4},{24,8},{28,12},{1,17},{... | collective-permute-start | bytes 12296 | tf_op jit(solution)/shard_map/ppermute | solution.py:28
  52.6 1.8 %collective-permute-done.20.heard = f32[8,128]{1,0:T(8,128)S(1)} collective-permute-done((f32[8,128]{1,0:T(8,128)S(1)}, f32[8,128]{1,0:T(8,128)S(1)}, u32[]{:S(2)}, u32[]{:S(2)}) %collective-permute-start.20) | collective-permute-done | bytes 4128 | tf_op jit(solution)/shard_map/ppermute | solution.py:28
  54.4 0.2 join_a.1
  54.7 1.0 %collective-permute-start.22 = (bf16[576,128]{1,0:T(8,128)(2,1)S(1)}, bf16[576,128]{1,0:T(8,128)(2,1)S(1)}, u32[]{:S(2)}, u32[]{:S(2)}) collective-permute-start(bf16[576,128]{1,0:T(8,128)(2,1)S(1)} %get-tuple-element.68), channel_id=1, source_target_pairs={{0,2},{1,5},{2,0},{3,7},{4,6},{5,1},{6,4},{7,3},{8,10},{9,13},{10,... | collective-permute-start | bytes 442376 | tf_op jit(solution)/shard_map/ppermute | solution.py:452
  55.7 0.2 join_b.1
  55.9 1.2 %collective-permute-start.21 = (bf16[576,128]{1,0:T(8,128)(2,1)S(1)}, bf16[576,128]{1,0:T(8,128)(2,1)S(1)}, u32[]{:S(2)}, u32[]{:S(2)}) collective-permute-start(bf16[576,128]{1,0:T(8,128)(2,1)S(1)} %get-tuple-element.71), channel_id=1, source_target_pairs={{0,2},{1,5},{2,0},{3,7},{4,6},{5,1},{6,4},{7,3},{8,10},{9,13},{10,... | collective-permute-start | bytes 442376 | tf_op jit(solution)/shard_map/ppermute | solution.py:452
  57.1 2.8 %collective-permute-done.22.got = bf16[576,128]{1,0:T(8,128)(2,1)S(1)} collective-permute-done((bf16[576,128]{1,0:T(8,128)(2,1)S(1)}, bf16[576,128]{1,0:T(8,128)(2,1)S(1)}, u32[]{:S(2)}, u32[]{:S(2)}) %collective-permute-start.22) | collective-permute-done | bytes 147488 | tf_op jit(solution)/shard_map/ppermute | solution.py:452
  59.9 0.1 fold_last_a.1
  60.0 2.2 %collective-permute-start.25 = (bf16[288,128]{1,0:T(8,128)(2,1)S(1)}, bf16[288,128]{1,0:T(8,128)(2,1)S(1)}, u32[]{:S(2)}, u32[]{:S(2)}) collective-permute-start(bf16[288,128]{1,0:T(8,128)(2,1)S(1)} %get-tuple-element.73), channel_id=1, source_target_pairs={{0,24},{4,28},{8,16},{12,20},{16,8},{20,12},{24,0},{28,4},{1,25},{... | collective-permute-start | bytes 221192 | tf_op jit(solution)/shard_map/ppermute | solution.py:28
  62.2 0.1 fold_last_b.1
  62.3 1.2 %collective-permute-start.23 = (bf16[288,128]{1,0:T(8,128)(2,1)S(1)}, bf16[288,128]{1,0:T(8,128)(2,1)S(1)}, u32[]{:S(2)}, u32[]{:S(2)}) collective-permute-start(bf16[288,128]{1,0:T(8,128)(2,1)S(1)} %get-tuple-element.78), channel_id=1, source_target_pairs={{0,8},{4,12},{8,0},{12,4},{16,24},{20,28},{24,16},{28,20},{1,9},{5... | collective-permute-start | bytes 221192 | tf_op jit(solution)/shard_map/ppermute | solution.py:28
  63.5 1.2 %collective-permute-start.24 = (bf16[288,128]{1,0:T(8,128)(2,1)S(1)}, bf16[288,128]{1,0:T(8,128)(2,1)S(1)}, u32[]{:S(2)}, u32[]{:S(2)}) collective-permute-start(bf16[288,128]{1,0:T(8,128)(2,1)S(1)} %get-tuple-element.77), channel_id=1, source_target_pairs={{0,16},{4,20},{8,24},{12,28},{16,0},{20,4},{24,8},{28,12},{1,17},{... | collective-permute-start | bytes 221192 | tf_op jit(solution)/shard_map/ppermute | solution.py:28
  64.7 1.0 %tally.1 = (f32[8,128]{1,0:T(8,128)S(1)}, f32[1,4]{1,0:T(1,128)}, f32[1,1]{1,0:T(1,128)}) custom-call(f32[8,128]{1,0:T(8,128)S(1)} %add.11.sums, f32[8,128]{1,0:T(8,128)S(1)} %collective-permute-done.20.heard, s32[4,64]{1,0:T(4,128)S(1)} %copy-done.5, s32[4,8]{1,0:T(4,128)S(1)} %copy-done.6, f32[4,8]{1,0:T(4,128)S(1)} %copy-done.7), custom_call_target="tpu_custom_call" | custom-call | tf_op jit(solution)/shard_map/tally/pallas_call | solution.py:420
  65.7 0.6 collective-permute-done.25.three
  66.3 0.8 %collective-permute-done.23.one = bf16[288,128]{1,0:T(8,128)(2,1)S(1)} collective-permute-done((bf16[288,128]{1,0:T(8,128)(2,1)S(1)}, bf16[288,128]{1,0:T(8,128)(2,1)S(1)}, u32[]{:S(2)}, u32[]{:S(2)}) %collective-permute-start.23) | collective-permute-done | bytes 73760 | tf_op jit(solution)/shard_map/ppermute | solution.py:28
  67.1 2.5 %collective-permute-done.24.two = bf16[288,128]{1,0:T(8,128)(2,1)S(1)} collective-permute-done((bf16[288,128]{1,0:T(8,128)(2,1)S(1)}, bf16[288,128]{1,0:T(8,128)(2,1)S(1)}, u32[]{:S(2)}, u32[]{:S(2)}) %collective-permute-start.24) | collective-permute-done | bytes 73760 | tf_op jit(solution)/shard_map/ppermute | solution.py:28
  69.5 1.0 %finish.1 = f32[64,576]{1,0:T(8,128)} custom-call(f32[288,128]{1,0:T(8,128)S(1)} %get-tuple-element.75.mine, bf16[288,128]{1,0:T(8,128)(2,1)S(1)} %collective-permute-done.23.one, bf16[288,128]{1,0:T(8,128)(2,1)S(1)} %collective-permute-done.24.two, bf16[288,128]{1,0:T(8,128)(2,1)S(1)} %collective-permute-done.25.three, ...), custom_call_target="tpu_custom_call" | custom-call | tf_op jit(solution)/shard_map/finish/pallas_call | solution.py:420
  (31 shorter events, 0.1 us)
Async XLA Ops:
  0.6 8.3 %collective-permute-start.1 = (bf16[64,576]{1,0:T(8,128)(2,1)}, bf16[64,576]{1,0:T(8,128)(2,1)S(1)}, u32[]{:S(2)}, u32[]{:S(2)}) collective-permute-start(bf16[64,576]{1,0:T(8,128)(2,1)} %hidden.1), channel_id=1, source_target_pairs={{0,16},{4,20},{8,24},{12,28},{16,0},{20,4},{24,8},{28,12},{1,17},{... | collective-permute-start | bytes 221192 | tf_op jit(solution)/shard_map/ppermute | solution.py:28
  4.7 4.8 %collective-permute-start = (bf16[64,576]{1,0:T(8,128)(2,1)}, bf16[64,576]{1,0:T(8,128)(2,1)S(1)}, u32[]{:S(2)}, u32[]{:S(2)}) collective-permute-start(bf16[64,576]{1,0:T(8,128)(2,1)} %hidden.1), channel_id=1, source_target_pairs={{0,8},{4,12},{8,0},{12,4},{16,24},{20,28},{24,16},{28,20},{1,9},{5... | collective-permute-start | bytes 221192 | tf_op jit(solution)/shard_map/ppermute | solution.py:28
  6.3 6.4 %collective-permute-start.2 = (bf16[64,576]{1,0:T(8,128)(2,1)}, bf16[64,576]{1,0:T(8,128)(2,1)S(1)}, u32[]{:S(2)}, u32[]{:S(2)}) collective-permute-start(bf16[64,576]{1,0:T(8,128)(2,1)} %hidden.1), channel_id=1, source_target_pairs={{0,24},{4,28},{8,16},{12,20},{16,8},{20,12},{24,0},{28,4},{1,25},{... | collective-permute-start | bytes 221192 | tf_op jit(solution)/shard_map/ppermute | solution.py:28
  6.3 1.0 %copy-start.2 = (bf16[64,576]{1,0:T(8,128)(2,1)S(1)}, bf16[64,576]{1,0:T(8,128)(2,1)}, u32[]{:S(2)}) copy-start(bf16[64,576]{1,0:T(8,128)(2,1)} %hidden.1) | copy-start | bytes 221188
  7.3 0.7 copy-start.8
  12.8 11.2 %copy-start.4 = (f32[4608]{0:T(1024)S(1)}, f32[4608]{0:T(1024)}, u32[]{:S(2)}) copy-start(f32[4608]{0:T(1024)} %param.8) | copy-start | bytes 55300
  13.0 10.0 %collective-permute-start.4 = (bf16[1152,128]{1,0:T(8,128)(2,1)S(1)}, bf16[1152,128]{1,0:T(8,128)(2,1)S(1)}, u32[]{:S(2)}, u32[]{:S(2)}) collective-permute-start(bf16[1152,128]{1,0:T(8,128)(2,1)S(1)} %strips.1.refs_0_), channel_id=1, source_target_pairs={{0,2},{1,5},{2,0},{3,7},{4,6},{5,1},{6,4},{7,3},{8,10},{9,13},{10,... | collective-permute-start | bytes 884744 | tf_op jit(solution)/shard_map/ppermute | solution.py:452
  14.7 8.4 %collective-permute-start.3 = (bf16[1152,128]{1,0:T(8,128)(2,1)S(1)}, bf16[1152,128]{1,0:T(8,128)(2,1)S(1)}, u32[]{:S(2)}, u32[]{:S(2)}) collective-permute-start(bf16[1152,128]{1,0:T(8,128)(2,1)S(1)} %strips.1.refs_0_), channel_id=1, source_target_pairs={{0,4},{1,3},{2,6},{3,1},{4,0},{5,7},{6,2},{7,5},{8,12},{9,11},{10,... | collective-permute-start | bytes 884744 | tf_op jit(solution)/shard_map/ppermute | solution.py:451
  16.2 3.6 %copy-start = (bf16[1000,4608]{1,0:T(8,128)(2,1)S(1)}, bf16[1000,4608]{1,0:T(8,128)(2,1)}, u32[]{:S(2)}) copy-start(bf16[1000,4608]{1,0:T(8,128)(2,1)} %weight.1) | copy-start | bytes 27648004
  23.1 2.9 %collective-permute-start.9 = (bf16[4608,128]{1,0:T(8,128)(2,1)S(1)}, bf16[4608,128]{1,0:T(8,128)(2,1)S(1)}, u32[]{:S(2)}, u32[]{:S(2)}) collective-permute-start(bf16[4608,128]{1,0:T(8,128)(2,1)S(1)} %get-tuple-element.50), channel_id=1, source_target_pairs={{0,1},{1,0},{2,3},{3,2},{4,5},{5,4},{6,7},{7,6},{8,9},{9,8},{10,11... | collective-permute-start | bytes 3538952 | tf_op jit(solution)/shard_map/ppermute | solution.py:28
  23.2 6.8 %collective-permute-start.5 = (bf16[1152,128]{1,0:T(8,128)(2,1)S(1)}, bf16[1152,128]{1,0:T(8,128)(2,1)S(1)}, u32[]{:S(2)}, u32[]{:S(2)}) collective-permute-start(bf16[1152,128]{1,0:T(8,128)(2,1)S(1)} %collective-permute-done.3.refs_1_), channel_id=1, source_target_pairs={{0,2},{1,5},{2,0},{3,7},{4,6},{5,1},{6,4},{7,3},{8,10},{9,13},{10,... | collective-permute-start | bytes 884744 | tf_op jit(solution)/shard_map/ppermute | solution.py:452
  23.7 6.8 %collective-permute-start.6 = (bf16[1152,128]{1,0:T(8,128)(2,1)S(1)}, bf16[1152,128]{1,0:T(8,128)(2,1)S(1)}, u32[]{:S(2)}, u32[]{:S(2)}) collective-permute-start(bf16[1152,128]{1,0:T(8,128)(2,1)S(1)} %strips.1.refs_0_), channel_id=1, source_target_pairs={{0,1},{1,0},{2,3},{3,2},{4,5},{5,4},{6,7},{7,6},{8,9},{9,8},{10,11... | collective-permute-start | bytes 884744 | tf_op jit(solution)/shard_map/ppermute | solution.py:28
  23.9 9.7 %copy-start.1 = (bf16[1000,4608]{1,0:T(8,128)(2,1)S(1)}, bf16[1000,4608]{1,0:T(8,128)(2,1)}, u32[]{:S(2)}) copy-start(bf16[1000,4608]{1,0:T(8,128)(2,1)} %weight.1) | copy-start | bytes 27648004
  24.6 5.9 %collective-permute-start.8 = (bf16[1152,128]{1,0:T(8,128)(2,1)S(1)}, bf16[1152,128]{1,0:T(8,128)(2,1)S(1)}, u32[]{:S(2)}, u32[]{:S(2)}) collective-permute-start(bf16[1152,128]{1,0:T(8,128)(2,1)S(1)} %collective-permute-done.4.refs_2_), channel_id=1, source_target_pairs={{0,1},{1,0},{2,3},{3,2},{4,5},{5,4},{6,7},{7,6},{8,9},{9,8},{10,11... | collective-permute-start | bytes 884744 | tf_op jit(solution)/shard_map/ppermute | solution.py:28
  25.0 5.5 %collective-permute-start.7 = (bf16[1152,128]{1,0:T(8,128)(2,1)S(1)}, bf16[1152,128]{1,0:T(8,128)(2,1)S(1)}, u32[]{:S(2)}, u32[]{:S(2)}) collective-permute-start(bf16[1152,128]{1,0:T(8,128)(2,1)S(1)} %collective-permute-done.3.refs_1_), channel_id=1, source_target_pairs={{0,1},{1,0},{2,3},{3,2},{4,5},{5,4},{6,7},{7,6},{8,9},{9,8},{10,11... | collective-permute-start | bytes 884744 | tf_op jit(solution)/shard_map/ppermute | solution.py:28
  30.0 1.6 %collective-permute-start.10 = (bf16[1152,128]{1,0:T(8,128)(2,1)S(1)}, bf16[1152,128]{1,0:T(8,128)(2,1)S(1)}, u32[]{:S(2)}, u32[]{:S(2)}) collective-permute-start(bf16[1152,128]{1,0:T(8,128)(2,1)S(1)} %collective-permute-done.5.refs_3_), channel_id=1, source_target_pairs={{0,1},{1,0},{2,3},{3,2},{4,5},{5,4},{6,7},{7,6},{8,9},{9,8},{10,11... | collective-permute-start | bytes 884744 | tf_op jit(solution)/shard_map/ppermute | solution.py:28
  30.0 12.5 %collective-permute-start.13 = (bf16[2304,128]{1,0:T(8,128)(2,1)S(1)}, bf16[2304,128]{1,0:T(8,128)(2,1)S(1)}, u32[]{:S(2)}, u32[]{:S(2)}) collective-permute-start(bf16[2304,128]{1,0:T(8,128)(2,1)S(1)} %get-tuple-element.59), channel_id=1, source_target_pairs={{0,4},{1,3},{2,6},{3,1},{4,0},{5,7},{6,2},{7,5},{8,12},{9,11},{10,... | collective-permute-start | bytes 1769480 | tf_op jit(solution)/shard_map/ppermute | solution.py:451
  36.5 2.1 %collective-permute-start.11 = (f32[3,256]{1,0:T(4,128)S(1)}, f32[3,256]{1,0:T(4,128)S(1)}, u32[]{:S(2)}, u32[]{:S(2)}) collective-permute-start(f32[3,256]{1,0:T(4,128)S(1)} %pad_maximum_fusion.stats), channel_id=1, source_target_pairs={{0,1},{1,0},{2,3},{3,2},{4,5},{5,4},{6,7},{7,6},{8,9},{9,8},{10,11... | collective-permute-start | bytes 9224 | tf_op jit(solution)/shard_map/ppermute | solution.py:28
  38.2 4.9 %collective-permute-start.15 = (bf16[2304,128]{1,0:T(8,128)(2,1)S(1)}, bf16[2304,128]{1,0:T(8,128)(2,1)S(1)}, u32[]{:S(2)}, u32[]{:S(2)}) collective-permute-start(bf16[2304,128]{1,0:T(8,128)(2,1)S(1)} %post.2), channel_id=1, source_target_pairs={{0,1},{1,0},{2,3},{3,2},{4,5},{5,4},{6,7},{7,6},{8,9},{9,8},{10,11... | collective-permute-start | bytes 1769480 | tf_op jit(solution)/shard_map/ppermute | solution.py:28
  38.7 3.7 %collective-permute-start.12 = (f32[8,128]{1,0:T(8,128)S(1)}, f32[8,128]{1,0:T(8,128)S(1)}, u32[]{:S(2)}, u32[]{:S(2)}) collective-permute-start(f32[8,128]{1,0:T(8,128)S(1)} %count.1), channel_id=1, source_target_pairs={{0,4},{4,0},{8,12},{12,8},{16,20},{20,16},{24,28},{28,24},{1,5},{5... | collective-permute-start | bytes 12296 | tf_op jit(solution)/shard_map/ppermute | solution.py:28
  42.4 2.1 %collective-permute-start.14 = (bf16[2304,128]{1,0:T(8,128)(2,1)S(1)}, bf16[2304,128]{1,0:T(8,128)(2,1)S(1)}, u32[]{:S(2)}, u32[]{:S(2)}) collective-permute-start(bf16[2304,128]{1,0:T(8,128)(2,1)S(1)} %post.3), channel_id=1, source_target_pairs={{0,1},{1,0},{2,3},{3,2},{4,5},{5,4},{6,7},{7,6},{8,9},{9,8},{10,11... | collective-permute-start | bytes 1769480 | tf_op jit(solution)/shard_map/ppermute | solution.py:28
  42.5 3.7 %collective-permute-start.18 = (f32[8,128]{1,0:T(8,128)S(1)}, f32[8,128]{1,0:T(8,128)S(1)}, u32[]{:S(2)}, u32[]{:S(2)}) collective-permute-start(f32[8,128]{1,0:T(8,128)S(1)} %add.9), channel_id=1, source_target_pairs={{0,2},{1,3},{2,0},{3,1},{4,6},{5,7},{6,4},{7,5},{8,10},{9,11},{10,... | collective-permute-start | bytes 12296 | tf_op jit(solution)/shard_map/ppermute | solution.py:28
  43.2 21.5 %copy-start.5 = (s32[4,64]{1,0:T(4,128)S(1)}, s32[4,64]{1,0:T(4,128)}, u32[]{:S(2)}) copy-start(s32[4,64]{1,0:T(4,128)} %segments.1) | copy-start | bytes 3076
  43.2 21.5 %copy-start.6 = (s32[4,8]{1,0:T(4,128)S(1)}, s32[4,8]{1,0:T(4,128)}, u32[]{:S(2)}) copy-start(s32[4,8]{1,0:T(4,128)} %pairing.1) | copy-start | bytes 388
  43.2 21.4 %copy-start.7 = (f32[4,8]{1,0:T(4,128)S(1)}, f32[4,8]{1,0:T(4,128)}, u32[]{:S(2)}) copy-start(f32[4,8]{1,0:T(4,128)} %ref_logp.1) | copy-start | bytes 388
  43.2 26.3 %copy-start.3 = (bf16[64,576]{1,0:T(8,128)(2,1)S(1)}, bf16[64,576]{1,0:T(8,128)(2,1)}, u32[]{:S(2)}) copy-start(bf16[64,576]{1,0:T(8,128)(2,1)} %hidden.1) | copy-start | bytes 221188
  43.2 11.2 %collective-permute-start.17 = (bf16[1152,128]{1,0:T(8,128)(2,1)S(1)}, bf16[1152,128]{1,0:T(8,128)(2,1)S(1)}, u32[]{:S(2)}, u32[]{:S(2)}) collective-permute-start(bf16[1152,128]{1,0:T(8,128)(2,1)S(1)} %get-tuple-element.62), channel_id=1, source_target_pairs={{0,4},{1,3},{2,6},{3,1},{4,0},{5,7},{6,2},{7,5},{8,12},{9,11},{10,... | collective-permute-start | bytes 884744 | tf_op jit(solution)/shard_map/ppermute | solution.py:451
  44.6 11.0 %collective-permute-start.16 = (bf16[1152,128]{1,0:T(8,128)(2,1)S(1)}, bf16[1152,128]{1,0:T(8,128)(2,1)S(1)}, u32[]{:S(2)}, u32[]{:S(2)}) collective-permute-start(bf16[1152,128]{1,0:T(8,128)(2,1)S(1)} %get-tuple-element.65), channel_id=1, source_target_pairs={{0,4},{1,3},{2,6},{3,1},{4,0},{5,7},{6,2},{7,5},{8,12},{9,11},{10,... | collective-permute-start | bytes 884744 | tf_op jit(solution)/shard_map/ppermute | solution.py:451
  46.3 3.6 %collective-permute-start.19 = (f32[8,128]{1,0:T(8,128)S(1)}, f32[8,128]{1,0:T(8,128)S(1)}, u32[]{:S(2)}, u32[]{:S(2)}) collective-permute-start(f32[8,128]{1,0:T(8,128)S(1)} %maximum_add_fusion), channel_id=1, source_target_pairs={{0,8},{4,12},{8,0},{12,4},{16,24},{20,28},{24,16},{28,20},{1,9},{5... | collective-permute-start | bytes 12296 | tf_op jit(solution)/shard_map/ppermute | solution.py:28
  49.9 4.5 %collective-permute-start.20 = (f32[8,128]{1,0:T(8,128)S(1)}, f32[8,128]{1,0:T(8,128)S(1)}, u32[]{:S(2)}, u32[]{:S(2)}) collective-permute-start(f32[8,128]{1,0:T(8,128)S(1)} %add.11.sums), channel_id=1, source_target_pairs={{0,16},{4,20},{8,24},{12,28},{16,0},{20,4},{24,8},{28,12},{1,17},{... | collective-permute-start | bytes 12296 | tf_op jit(solution)/shard_map/ppermute | solution.py:28
  54.7 5.2 %collective-permute-start.22 = (bf16[576,128]{1,0:T(8,128)(2,1)S(1)}, bf16[576,128]{1,0:T(8,128)(2,1)S(1)}, u32[]{:S(2)}, u32[]{:S(2)}) collective-permute-start(bf16[576,128]{1,0:T(8,128)(2,1)S(1)} %get-tuple-element.68), channel_id=1, source_target_pairs={{0,2},{1,5},{2,0},{3,7},{4,6},{5,1},{6,4},{7,3},{8,10},{9,13},{10,... | collective-permute-start | bytes 442376 | tf_op jit(solution)/shard_map/ppermute | solution.py:452
  55.9 6.3 %collective-permute-start.21 = (bf16[576,128]{1,0:T(8,128)(2,1)S(1)}, bf16[576,128]{1,0:T(8,128)(2,1)S(1)}, u32[]{:S(2)}, u32[]{:S(2)}) collective-permute-start(bf16[576,128]{1,0:T(8,128)(2,1)S(1)} %get-tuple-element.71), channel_id=1, source_target_pairs={{0,2},{1,5},{2,0},{3,7},{4,6},{5,1},{6,4},{7,3},{8,10},{9,13},{10,... | collective-permute-start | bytes 442376 | tf_op jit(solution)/shard_map/ppermute | solution.py:452
  60.0 6.3 %collective-permute-start.25 = (bf16[288,128]{1,0:T(8,128)(2,1)S(1)}, bf16[288,128]{1,0:T(8,128)(2,1)S(1)}, u32[]{:S(2)}, u32[]{:S(2)}) collective-permute-start(bf16[288,128]{1,0:T(8,128)(2,1)S(1)} %get-tuple-element.73), channel_id=1, source_target_pairs={{0,24},{4,28},{8,16},{12,20},{16,8},{20,12},{24,0},{28,4},{1,25},{... | collective-permute-start | bytes 221192 | tf_op jit(solution)/shard_map/ppermute | solution.py:28
  62.3 4.8 %collective-permute-start.23 = (bf16[288,128]{1,0:T(8,128)(2,1)S(1)}, bf16[288,128]{1,0:T(8,128)(2,1)S(1)}, u32[]{:S(2)}, u32[]{:S(2)}) collective-permute-start(bf16[288,128]{1,0:T(8,128)(2,1)S(1)} %get-tuple-element.78), channel_id=1, source_target_pairs={{0,8},{4,12},{8,0},{12,4},{16,24},{20,28},{24,16},{28,20},{1,9},{5... | collective-permute-start | bytes 221192 | tf_op jit(solution)/shard_map/ppermute | solution.py:28
  63.5 6.0 %collective-permute-start.24 = (bf16[288,128]{1,0:T(8,128)(2,1)S(1)}, bf16[288,128]{1,0:T(8,128)(2,1)S(1)}, u32[]{:S(2)}, u32[]{:S(2)}) collective-permute-start(bf16[288,128]{1,0:T(8,128)(2,1)S(1)} %get-tuple-element.77), channel_id=1, source_target_pairs={{0,16},{4,20},{8,24},{12,28},{16,0},{20,4},{24,8},{28,12},{1,17},{... | collective-permute-start | bytes 221192 | tf_op jit(solution)/shard_map/ppermute | solution.py:28

commit v4 on v3

--- a/solution.py
+++ b/solution.py
@@ -557,9 +557,9 @@
     keep_b, send_b = join("join_b", rows, keep_b, hold(got_b, send_a))
     got_b = to_two(send_b)
     send_1, send_3 = fold(fold_half_kernel, "fold_last_a", keep_a, got_a, half)
-    got_3 = over_z(send_3, 3)
+    got_3, got_1 = over_z(send_3, 3), over_z(send_1, 1)
     keep, send_2 = fold(fold_half_kernel, "fold_last_b", keep_b, hold(got_b, send_3))
-    got_2, got_1 = over_z(send_2, 2), over_z(hold(send_1, send_2), 1)
+    got_2 = over_z(send_2, 2)
     scales, margins, dpo_loss = call(
         tally_kernel, "tally",
         (shape((8, LANES), full), shape((1, ref_logp.shape[1] // 2), full), shape((1, 1), full)),

time: 70.8 us -> 70.9 us (level)
  transfers between devices with their start and end apart: 26 -> 26, of which waited for: 15 -> 14; matrix products, arithmetic and copies ran while one was open for 8% -> 8% of each run, Pallas kernels for 12% -> 12%
where the time goes in v4:
time: 70.9 us; the launch traced here: 70.6 us
  waiting for transfers between devices  24.6 us (35%)
  starting transfers between devices  24.1 us (34%)
  Pallas kernels  9.97 us (14%)
  matrix products  5.68 us (8%)
  local copies, waits for them, and re-layouts  5.35 us (8%)
  between operations  0.88 us (1%)
    ppermute x18, waiting for transfers between devices, exchange(): return lax.ppermute(arr, axis, [(i, i ^ mask) for i in range(size)])  18.3 us
    ppermute x18, starting transfers between devices, exchange(): return lax.ppermute(arr, axis, [(i, i ^ mask) for i in range(size)])  16.2 us
    pallas_call x17, Pallas kernels, call(): pl.pallas_call(kernel, out_shape=outs, in_specs=in_specs, out_specs=out_s...  9.97 us
    ppermute x4, waiting for transfers between devices, fast_path(): to_two = lambda a: lax.ppermute(a, both_axes, two_pairs)  6.31 us
    unnamed x18, local copies, waits for them, and re-layouts  5.28 us
    ppermute x4, starting transfers between devices, fast_path(): to_two = lambda a: lax.ppermute(a, both_axes, two_pairs)  4.4 us
    ppermute x4, starting transfers between devices, fast_path(): to_one = lambda a: lax.ppermute(a, both_axes, one_pairs)  3.48 us
    dot_general x1, matrix products, fast_path(): lax.dot_general(weight, normed, (((1,), (0,)), ((), ())), preferred_eleme...  2.9 us
  transfers between devices with their start and end apart: 26, of which 14 were waited for; matrix products, arithmetic and copies ran while one was open for 8% of the time, Pallas kernels for 12%

profile of v4, /device:TPU:0, one launch (start us, length us, event | category | flops | bytes accessed | tf_op | source)
XLA Modules:
  0.0 70.6 jit_solution(690437958489065944)
XLA Ops:
  0.6 4.1 %collective-permute-start.1 = (bf16[64,576]{1,0:T(8,128)(2,1)}, bf16[64,576]{1,0:T(8,128)(2,1)S(1)}, u32[]{:S(2)}, u32[]{:S(2)}) collective-permute-start(bf16[64,576]{1,0:T(8,128)(2,1)} %hidden.1), channel_id=1, source_target_pairs={{0,16},{4,20},{8,24},{12,28},{16,0},{20,4},{24,8},{28,12},{1,17},{... | collective-permute-start | bytes 221192 | tf_op jit(solution)/shard_map/ppermute | solution.py:28
  4.7 1.6 %collective-permute-start = (bf16[64,576]{1,0:T(8,128)(2,1)}, bf16[64,576]{1,0:T(8,128)(2,1)S(1)}, u32[]{:S(2)}, u32[]{:S(2)}) collective-permute-start(bf16[64,576]{1,0:T(8,128)(2,1)} %hidden.1), channel_id=1, source_target_pairs={{0,8},{4,12},{8,0},{12,4},{16,24},{20,28},{24,16},{28,20},{1,9},{5... | collective-permute-start | bytes 221192 | tf_op jit(solution)/shard_map/ppermute | solution.py:28
  6.3 1.0 %copy-done.2 = bf16[64,576]{1,0:T(8,128)(2,1)S(1)} copy-done((bf16[64,576]{1,0:T(8,128)(2,1)S(1)}, bf16[64,576]{1,0:T(8,128)(2,1)}, u32[]{:S(2)}) %copy-start.2) | copy-done | bytes 73752
  7.3 0.7 copy-done.8
  7.9 0.2 own_strip.1
  8.1 0.8 %collective-permute-done.1.refs_1_ = bf16[64,576]{1,0:T(8,128)(2,1)S(1)} collective-permute-done((bf16[64,576]{1,0:T(8,128)(2,1)}, bf16[64,576]{1,0:T(8,128)(2,1)S(1)}, u32[]{:S(2)}, u32[]{:S(2)}) %collective-permute-start.1) | collective-permute-done | bytes 73760 | tf_op jit(solution)/shard_map/ppermute | solution.py:28
  9.0 0.5 collective-permute-done.refs_0_
  9.5 3.3 %collective-permute-done.2.refs_2_ = bf16[64,576]{1,0:T(8,128)(2,1)S(1)} collective-permute-done((bf16[64,576]{1,0:T(8,128)(2,1)}, bf16[64,576]{1,0:T(8,128)(2,1)S(1)}, u32[]{:S(2)}, u32[]{:S(2)}) %collective-permute-start.2) | collective-permute-done | bytes 73760 | tf_op jit(solution)/shard_map/ppermute | solution.py:28
  12.8 0.3 strips.1.refs_0_
  13.0 1.7 %collective-permute-start.4 = (bf16[1152,128]{1,0:T(8,128)(2,1)S(1)}, bf16[1152,128]{1,0:T(8,128)(2,1)S(1)}, u32[]{:S(2)}, u32[]{:S(2)}) collective-permute-start(bf16[1152,128]{1,0:T(8,128)(2,1)S(1)} %strips.1.refs_0_), channel_id=1, source_target_pairs={{0,2},{1,5},{2,0},{3,7},{4,6},{5,1},{6,4},{7,3},{8,10},{9,13},{10,... | collective-permute-start | bytes 884744 | tf_op jit(solution)/shard_map/ppermute | solution.py:452
  14.7 1.5 %collective-permute-start.3 = (bf16[1152,128]{1,0:T(8,128)(2,1)S(1)}, bf16[1152,128]{1,0:T(8,128)(2,1)S(1)}, u32[]{:S(2)}, u32[]{:S(2)}) collective-permute-start(bf16[1152,128]{1,0:T(8,128)(2,1)S(1)} %strips.1.refs_0_), channel_id=1, source_target_pairs={{0,4},{1,3},{2,6},{3,1},{4,0},{5,7},{6,2},{7,5},{8,12},{9,11},{10,... | collective-permute-start | bytes 884744 | tf_op jit(solution)/shard_map/ppermute | solution.py:451
  16.2 3.6 %copy-done = bf16[1000,4608]{1,0:T(8,128)(2,1)S(1)} copy-done((bf16[1000,4608]{1,0:T(8,128)(2,1)S(1)}, bf16[1000,4608]{1,0:T(8,128)(2,1)}, u32[]{:S(2)}) %copy-start) | copy-done | bytes 9216024
  19.8 3.3 %turn_weight.1 = (bf16[2304,1000]{1,0:T(8,128)(2,1)S(1)}, bf16[2304,1000]{1,0:T(8,128)(2,1)S(1)}, bf16[4608,128]{1,0:T(8,128)(2,1)S(1)}, bf16[4608,128]{1,0:T(8,128)(2,1)S(1)}) custom-call(s32[1,256]{1,0:T(1,128)S(1)} %get-tuple-element.45.flat, bf16[1000,4608]{1,0:T(8,128)(2,1)S(1)} %copy-done), custom_call_target="tpu_custom_call" | custom-call | flops 2359296000 | bytes 18432000 | tf_op jit(solution)/shard_map/turn_weight/pallas_call | solution.py:420
  23.1 0.1 collective-permute-start.9
  23.2 0.6 collective-permute-start.5
  23.7 0.2 collective-permute-start.6
  23.9 0.7 gain_table.1.refs_8_
  24.6 0.4 collective-permute-start.8
  25.0 0.2 collective-permute-start.7
  25.2 0.8 %collective-permute-done.9.got = bf16[4608,128]{1,0:T(8,128)(2,1)S(1)} collective-permute-done((bf16[4608,128]{1,0:T(8,128)(2,1)S(1)}, bf16[4608,128]{1,0:T(8,128)(2,1)S(1)}, u32[]{:S(2)}, u32[]{:S(2)}) %collective-permute-start.9) | collective-permute-done | bytes 1179680 | tf_op jit(solution)/shard_map/ppermute | solution.py:28
  26.0 0.4 fold_rows.1
  26.5 3.5 %collective-permute-done.5.refs_3_ = bf16[1152,128]{1,0:T(8,128)(2,1)S(1)} collective-permute-done((bf16[1152,128]{1,0:T(8,128)(2,1)S(1)}, bf16[1152,128]{1,0:T(8,128)(2,1)S(1)}, u32[]{:S(2)}, u32[]{:S(2)}) %collective-permute-start.5) | collective-permute-done | bytes 294944 | tf_op jit(solution)/shard_map/ppermute | solution.py:452
  30.0 0.5 collective-permute-start.13
  30.5 1.0 %collective-permute-done.10.refs_7_ = bf16[1152,128]{1,0:T(8,128)(2,1)S(1)} collective-permute-done((bf16[1152,128]{1,0:T(8,128)(2,1)S(1)}, bf16[1152,128]{1,0:T(8,128)(2,1)S(1)}, u32[]{:S(2)}, u32[]{:S(2)}) %collective-permute-start.10) | collective-permute-done | bytes 294944 | tf_op jit(solution)/shard_map/ppermute | solution.py:28
  31.5 2.0 %norm.1 = (bf16[4608,256]{1,0:T(8,128)(2,1)S(1)}, f32[1,128]{1,0:T(1,128)S(1)}, f32[288,128]{1,0:T(8,128)S(1)}) custom-call(bf16[1152,128]{1,0:T(8,128)(2,1)S(1)} %strips.1.refs_0_, bf16[1152,128]{1,0:T(8,128)(2,1)S(1)} %collective-permute-done.3.refs_1_, bf16[1152,128]{1,0:T(8,128)(2,1)S(1)} %collective-permute-done.4.refs_2_, ...), custom_call_target="tpu_custom_call" | custom-call | flops 9437184 | tf_op jit(solution)/shard_map/norm/pallas_call | solution.py:420
  33.6 2.9 %fusion = (f32[256]{0:T(256)S(1)}, f32[256]{0:T(256)S(1)}, f32[256]{0:T(256)S(1)}, bf16[1000,256]{1,0:T(8,128)(2,1)S(1)}) fusion(s32[256]{0:T(256)S(1)} %bitcast.15, bf16[4608,256]{1,0:T(8,128)(2,1)S(1)} %get-tuple-element.53, bf16[1000,4608]{1,0:T(8,128)(2,1)S(1)} %copy-done.1), kind=kOutput, calls=%fused_computation.5 | convolution fusion | flops 2362623232 | bytes 12091392 | tf_op jit(solution)/shard_map/dot_general | solution.py:501
  36.5 0.2 collective-permute-start.11
  36.7 1.4 %fusion.3.grad.mine = f32[2304,256]{1,0:T(8,128)S(1)} fusion(bf16[2304,1000]{1,0:T(8,128)(2,1)S(1)} %get-tuple-element.55, bf16[1000,256]{1,0:T(8,128)(2,1)S(1)} %get-tuple-element.56), kind=kOutput, calls=%fused_computation.12 | convolution fusion | flops 1179648000 | bytes 7479296 | tf_op jit(solution)/shard_map/dot_general | solution.py:517
  38.1 0.1 post.2
  38.2 0.4 collective-permute-start.15
  38.7 0.6 collective-permute-start.12
  39.3 1.4 %fusion.4.grad.mine = f32[2304,256]{1,0:T(8,128)S(1)} fusion(bf16[2304,1000]{1,0:T(8,128)(2,1)S(1)} %get-tuple-element.46, bf16[1000,256]{1,0:T(8,128)(2,1)S(1)} %get-tuple-element.56), kind=kOutput, calls=%fused_computation.13 | convolution fusion | flops 1179648000 | bytes 7479296 | tf_op jit(solution)/shard_map/dot_general | solution.py:517
  40.7 1.7 %collective-permute-done.12 = f32[8,128]{1,0:T(8,128)S(1)} collective-permute-done((f32[8,128]{1,0:T(8,128)S(1)}, f32[8,128]{1,0:T(8,128)S(1)}, u32[]{:S(2)}, u32[]{:S(2)}) %collective-permute-start.12) | collective-permute-done | bytes 4128 | tf_op jit(solution)/shard_map/ppermute | solution.py:28
  42.3 0.1 post.3
  42.4 0.1 collective-permute-start.14
  42.5 0.6 collective-permute-start.18
  43.1 0.1 fold_core.2
  43.2 0.0 copy-start.7
  43.2 0.0 copy-start.3
  43.2 0.5 collective-permute-start.17
  43.8 0.7 %collective-permute-done.14.got = bf16[2304,128]{1,0:T(8,128)(2,1)S(1)} collective-permute-done((bf16[2304,128]{1,0:T(8,128)(2,1)S(1)}, bf16[2304,128]{1,0:T(8,128)(2,1)S(1)}, u32[]{:S(2)}, u32[]{:S(2)}) %collective-permute-start.14) | collective-permute-done | bytes 589856 | tf_op jit(solution)/shard_map/ppermute | solution.py:28
  44.5 0.1 fold_core.3
  44.6 0.9 %collective-permute-start.16 = (bf16[1152,128]{1,0:T(8,128)(2,1)S(1)}, bf16[1152,128]{1,0:T(8,128)(2,1)S(1)}, u32[]{:S(2)}, u32[]{:S(2)}) collective-permute-start(bf16[1152,128]{1,0:T(8,128)(2,1)S(1)} %get-tuple-element.64), channel_id=1, source_target_pairs={{0,4},{1,3},{2,6},{3,1},{4,0},{5,7},{6,2},{7,5},{8,12},{9,11},{10,... | collective-permute-start | bytes 884744 | tf_op jit(solution)/shard_map/ppermute | solution.py:451
  45.5 0.6 collective-permute-done.18
  46.2 0.1 fusion.2
  46.2 0.1 maximum_add_fusion
  46.3 0.9 %collective-permute-start.19 = (f32[8,128]{1,0:T(8,128)S(1)}, f32[8,128]{1,0:T(8,128)S(1)}, u32[]{:S(2)}, u32[]{:S(2)}) collective-permute-start(f32[8,128]{1,0:T(8,128)S(1)} %maximum_add_fusion), channel_id=1, source_target_pairs={{0,8},{4,12},{8,0},{12,4},{16,24},{20,28},{24,16},{28,20},{1,9},{5... | collective-permute-start | bytes 12296 | tf_op jit(solution)/shard_map/ppermute | solution.py:28
  47.2 2.8 %collective-permute-done.19 = f32[8,128]{1,0:T(8,128)S(1)} collective-permute-done((f32[8,128]{1,0:T(8,128)S(1)}, f32[8,128]{1,0:T(8,128)S(1)}, u32[]{:S(2)}, u32[]{:S(2)}) %collective-permute-start.19) | collective-permute-done | bytes 4128 | tf_op jit(solution)/shard_map/ppermute | solution.py:28
  49.9 2.7 %collective-permute-start.20 = (f32[8,128]{1,0:T(8,128)S(1)}, f32[8,128]{1,0:T(8,128)S(1)}, u32[]{:S(2)}, u32[]{:S(2)}) collective-permute-start(f32[8,128]{1,0:T(8,128)S(1)} %add.11.sums), channel_id=1, source_target_pairs={{0,16},{4,20},{8,24},{12,28},{16,0},{20,4},{24,8},{28,12},{1,17},{... | collective-permute-start | bytes 12296 | tf_op jit(solution)/shard_map/ppermute | solution.py:28
  52.6 1.8 %collective-permute-done.20.heard = f32[8,128]{1,0:T(8,128)S(1)} collective-permute-done((f32[8,128]{1,0:T(8,128)S(1)}, f32[8,128]{1,0:T(8,128)S(1)}, u32[]{:S(2)}, u32[]{:S(2)}) %collective-permute-start.20) | collective-permute-done | bytes 4128 | tf_op jit(solution)/shard_map/ppermute | solution.py:28
  54.4 0.2 join_a.1
  54.7 1.0 %collective-permute-start.22 = (bf16[576,128]{1,0:T(8,128)(2,1)S(1)}, bf16[576,128]{1,0:T(8,128)(2,1)S(1)}, u32[]{:S(2)}, u32[]{:S(2)}) collective-permute-start(bf16[576,128]{1,0:T(8,128)(2,1)S(1)} %get-tuple-element.67), channel_id=1, source_target_pairs={{0,2},{1,5},{2,0},{3,7},{4,6},{5,1},{6,4},{7,3},{8,10},{9,13},{10,... | collective-permute-start | bytes 442376 | tf_op jit(solution)/shard_map/ppermute | solution.py:452
  55.7 0.2 join_b.1
  55.9 1.2 %collective-permute-start.21 = (bf16[576,128]{1,0:T(8,128)(2,1)S(1)}, bf16[576,128]{1,0:T(8,128)(2,1)S(1)}, u32[]{:S(2)}, u32[]{:S(2)}) collective-permute-start(bf16[576,128]{1,0:T(8,128)(2,1)S(1)} %get-tuple-element.70), channel_id=1, source_target_pairs={{0,2},{1,5},{2,0},{3,7},{4,6},{5,1},{6,4},{7,3},{8,10},{9,13},{10,... | collective-permute-start | bytes 442376 | tf_op jit(solution)/shard_map/ppermute | solution.py:452
  57.1 2.8 %collective-permute-done.22.got = bf16[576,128]{1,0:T(8,128)(2,1)S(1)} collective-permute-done((bf16[576,128]{1,0:T(8,128)(2,1)S(1)}, bf16[576,128]{1,0:T(8,128)(2,1)S(1)}, u32[]{:S(2)}, u32[]{:S(2)}) %collective-permute-start.22) | collective-permute-done | bytes 147488 | tf_op jit(solution)/shard_map/ppermute | solution.py:452
  59.9 0.1 fold_last_a.1
  60.0 0.9 %collective-permute-start.23 = (bf16[288,128]{1,0:T(8,128)(2,1)S(1)}, bf16[288,128]{1,0:T(8,128)(2,1)S(1)}, u32[]{:S(2)}, u32[]{:S(2)}) collective-permute-start(bf16[288,128]{1,0:T(8,128)(2,1)S(1)} %get-tuple-element.75), channel_id=1, source_target_pairs={{0,8},{4,12},{8,0},{12,4},{16,24},{20,28},{24,16},{28,20},{1,9},{5... | collective-permute-start | bytes 221192 | tf_op jit(solution)/shard_map/ppermute | solution.py:28
  60.9 3.3 %collective-permute-start.25 = (bf16[288,128]{1,0:T(8,128)(2,1)S(1)}, bf16[288,128]{1,0:T(8,128)(2,1)S(1)}, u32[]{:S(2)}, u32[]{:S(2)}) collective-permute-start(bf16[288,128]{1,0:T(8,128)(2,1)S(1)} %get-tuple-element.72), channel_id=1, source_target_pairs={{0,24},{4,28},{8,16},{12,20},{16,8},{20,12},{24,0},{28,4},{1,25},{... | collective-permute-start | bytes 221192 | tf_op jit(solution)/shard_map/ppermute | solution.py:28
  64.2 0.1 fold_last_b.1
  64.3 0.1 collective-permute-start.24
  64.4 1.0 %tally.1 = (f32[8,128]{1,0:T(8,128)S(1)}, f32[1,4]{1,0:T(1,128)}, f32[1,1]{1,0:T(1,128)}) custom-call(f32[8,128]{1,0:T(8,128)S(1)} %add.11.sums, f32[8,128]{1,0:T(8,128)S(1)} %collective-permute-done.20.heard, s32[4,64]{1,0:T(4,128)S(1)} %copy-done.5, s32[4,8]{1,0:T(4,128)S(1)} %copy-done.6, f32[4,8]{1,0:T(4,128)S(1)} %copy-done.7), custom_call_target="tpu_custom_call" | custom-call | tf_op jit(solution)/shard_map/tally/pallas_call | solution.py:420
  65.5 1.9 %collective-permute-done.25.three = bf16[288,128]{1,0:T(8,128)(2,1)S(1)} collective-permute-done((bf16[288,128]{1,0:T(8,128)(2,1)S(1)}, bf16[288,128]{1,0:T(8,128)(2,1)S(1)}, u32[]{:S(2)}, u32[]{:S(2)}) %collective-permute-start.25) | collective-permute-done | bytes 73760 | tf_op jit(solution)/shard_map/ppermute | solution.py:28
  67.3 2.3 %collective-permute-done.24.two = bf16[288,128]{1,0:T(8,128)(2,1)S(1)} collective-permute-done((bf16[288,128]{1,0:T(8,128)(2,1)S(1)}, bf16[288,128]{1,0:T(8,128)(2,1)S(1)}, u32[]{:S(2)}, u32[]{:S(2)}) %collective-permute-start.24) | collective-permute-done | bytes 73760 | tf_op jit(solution)/shard_map/ppermute | solution.py:28
  69.6 1.0 %finish.1 = f32[64,576]{1,0:T(8,128)} custom-call(f32[288,128]{1,0:T(8,128)S(1)} %get-tuple-element.74.mine, bf16[288,128]{1,0:T(8,128)(2,1)S(1)} %collective-permute-done.23.one, bf16[288,128]{1,0:T(8,128)(2,1)S(1)} %collective-permute-done.24.two, bf16[288,128]{1,0:T(8,128)(2,1)S(1)} %collective-permute-done.25.three, ...), custom_call_target="tpu_custom_call" | custom-call | tf_op jit(solution)/shard_map/finish/pallas_call | solution.py:420
  (31 shorter events, 0.1 us)
Async XLA Ops:
  0.6 8.3 %collective-permute-start.1 = (bf16[64,576]{1,0:T(8,128)(2,1)}, bf16[64,576]{1,0:T(8,128)(2,1)S(1)}, u32[]{:S(2)}, u32[]{:S(2)}) collective-permute-start(bf16[64,576]{1,0:T(8,128)(2,1)} %hidden.1), channel_id=1, source_target_pairs={{0,16},{4,20},{8,24},{12,28},{16,0},{20,4},{24,8},{28,12},{1,17},{... | collective-permute-start | bytes 221192 | tf_op jit(solution)/shard_map/ppermute | solution.py:28
  4.7 4.8 %collective-permute-start = (bf16[64,576]{1,0:T(8,128)(2,1)}, bf16[64,576]{1,0:T(8,128)(2,1)S(1)}, u32[]{:S(2)}, u32[]{:S(2)}) collective-permute-start(bf16[64,576]{1,0:T(8,128)(2,1)} %hidden.1), channel_id=1, source_target_pairs={{0,8},{4,12},{8,0},{12,4},{16,24},{20,28},{24,16},{28,20},{1,9},{5... | collective-permute-start | bytes 221192 | tf_op jit(solution)/shard_map/ppermute | solution.py:28
  6.3 6.4 %collective-permute-start.2 = (bf16[64,576]{1,0:T(8,128)(2,1)}, bf16[64,576]{1,0:T(8,128)(2,1)S(1)}, u32[]{:S(2)}, u32[]{:S(2)}) collective-permute-start(bf16[64,576]{1,0:T(8,128)(2,1)} %hidden.1), channel_id=1, source_target_pairs={{0,24},{4,28},{8,16},{12,20},{16,8},{20,12},{24,0},{28,4},{1,25},{... | collective-permute-start | bytes 221192 | tf_op jit(solution)/shard_map/ppermute | solution.py:28
  6.3 1.0 %copy-start.2 = (bf16[64,576]{1,0:T(8,128)(2,1)S(1)}, bf16[64,576]{1,0:T(8,128)(2,1)}, u32[]{:S(2)}) copy-start(bf16[64,576]{1,0:T(8,128)(2,1)} %hidden.1) | copy-start | bytes 221188
  7.3 0.7 copy-start.8
  12.8 11.2 %copy-start.4 = (f32[4608]{0:T(1024)S(1)}, f32[4608]{0:T(1024)}, u32[]{:S(2)}) copy-start(f32[4608]{0:T(1024)} %param.8) | copy-start | bytes 55300
  13.0 10.0 %collective-permute-start.4 = (bf16[1152,128]{1,0:T(8,128)(2,1)S(1)}, bf16[1152,128]{1,0:T(8,128)(2,1)S(1)}, u32[]{:S(2)}, u32[]{:S(2)}) collective-permute-start(bf16[1152,128]{1,0:T(8,128)(2,1)S(1)} %strips.1.refs_0_), channel_id=1, source_target_pairs={{0,2},{1,5},{2,0},{3,7},{4,6},{5,1},{6,4},{7,3},{8,10},{9,13},{10,... | collective-permute-start | bytes 884744 | tf_op jit(solution)/shard_map/ppermute | solution.py:452
  14.7 8.4 %collective-permute-start.3 = (bf16[1152,128]{1,0:T(8,128)(2,1)S(1)}, bf16[1152,128]{1,0:T(8,128)(2,1)S(1)}, u32[]{:S(2)}, u32[]{:S(2)}) collective-permute-start(bf16[1152,128]{1,0:T(8,128)(2,1)S(1)} %strips.1.refs_0_), channel_id=1, source_target_pairs={{0,4},{1,3},{2,6},{3,1},{4,0},{5,7},{6,2},{7,5},{8,12},{9,11},{10,... | collective-permute-start | bytes 884744 | tf_op jit(solution)/shard_map/ppermute | solution.py:451
  16.2 3.6 %copy-start = (bf16[1000,4608]{1,0:T(8,128)(2,1)S(1)}, bf16[1000,4608]{1,0:T(8,128)(2,1)}, u32[]{:S(2)}) copy-start(bf16[1000,4608]{1,0:T(8,128)(2,1)} %weight.1) | copy-start | bytes 27648004
  23.1 2.9 %collective-permute-start.9 = (bf16[4608,128]{1,0:T(8,128)(2,1)S(1)}, bf16[4608,128]{1,0:T(8,128)(2,1)S(1)}, u32[]{:S(2)}, u32[]{:S(2)}) collective-permute-start(bf16[4608,128]{1,0:T(8,128)(2,1)S(1)} %get-tuple-element.49), channel_id=1, source_target_pairs={{0,1},{1,0},{2,3},{3,2},{4,5},{5,4},{6,7},{7,6},{8,9},{9,8},{10,11... | collective-permute-start | bytes 3538952 | tf_op jit(solution)/shard_map/ppermute | solution.py:28
  23.2 6.8 %collective-permute-start.5 = (bf16[1152,128]{1,0:T(8,128)(2,1)S(1)}, bf16[1152,128]{1,0:T(8,128)(2,1)S(1)}, u32[]{:S(2)}, u32[]{:S(2)}) collective-permute-start(bf16[1152,128]{1,0:T(8,128)(2,1)S(1)} %collective-permute-done.3.refs_1_), channel_id=1, source_target_pairs={{0,2},{1,5},{2,0},{3,7},{4,6},{5,1},{6,4},{7,3},{8,10},{9,13},{10,... | collective-permute-start | bytes 884744 | tf_op jit(solution)/shard_map/ppermute | solution.py:452
  23.7 6.8 %collective-permute-start.6 = (bf16[1152,128]{1,0:T(8,128)(2,1)S(1)}, bf16[1152,128]{1,0:T(8,128)(2,1)S(1)}, u32[]{:S(2)}, u32[]{:S(2)}) collective-permute-start(bf16[1152,128]{1,0:T(8,128)(2,1)S(1)} %strips.1.refs_0_), channel_id=1, source_target_pairs={{0,1},{1,0},{2,3},{3,2},{4,5},{5,4},{6,7},{7,6},{8,9},{9,8},{10,11... | collective-permute-start | bytes 884744 | tf_op jit(solution)/shard_map/ppermute | solution.py:28
  23.9 9.7 %copy-start.1 = (bf16[1000,4608]{1,0:T(8,128)(2,1)S(1)}, bf16[1000,4608]{1,0:T(8,128)(2,1)}, u32[]{:S(2)}) copy-start(bf16[1000,4608]{1,0:T(8,128)(2,1)} %weight.1) | copy-start | bytes 27648004
  24.6 5.9 %collective-permute-start.8 = (bf16[1152,128]{1,0:T(8,128)(2,1)S(1)}, bf16[1152,128]{1,0:T(8,128)(2,1)S(1)}, u32[]{:S(2)}, u32[]{:S(2)}) collective-permute-start(bf16[1152,128]{1,0:T(8,128)(2,1)S(1)} %collective-permute-done.4.refs_2_), channel_id=1, source_target_pairs={{0,1},{1,0},{2,3},{3,2},{4,5},{5,4},{6,7},{7,6},{8,9},{9,8},{10,11... | collective-permute-start | bytes 884744 | tf_op jit(solution)/shard_map/ppermute | solution.py:28
  25.0 5.5 %collective-permute-start.7 = (bf16[1152,128]{1,0:T(8,128)(2,1)S(1)}, bf16[1152,128]{1,0:T(8,128)(2,1)S(1)}, u32[]{:S(2)}, u32[]{:S(2)}) collective-permute-start(bf16[1152,128]{1,0:T(8,128)(2,1)S(1)} %collective-permute-done.3.refs_1_), channel_id=1, source_target_pairs={{0,1},{1,0},{2,3},{3,2},{4,5},{5,4},{6,7},{7,6},{8,9},{9,8},{10,11... | collective-permute-start | bytes 884744 | tf_op jit(solution)/shard_map/ppermute | solution.py:28
  30.0 1.6 %collective-permute-start.10 = (bf16[1152,128]{1,0:T(8,128)(2,1)S(1)}, bf16[1152,128]{1,0:T(8,128)(2,1)S(1)}, u32[]{:S(2)}, u32[]{:S(2)}) collective-permute-start(bf16[1152,128]{1,0:T(8,128)(2,1)S(1)} %collective-permute-done.5.refs_3_), channel_id=1, source_target_pairs={{0,1},{1,0},{2,3},{3,2},{4,5},{5,4},{6,7},{7,6},{8,9},{9,8},{10,11... | collective-permute-start | bytes 884744 | tf_op jit(solution)/shard_map/ppermute | solution.py:28
  30.0 12.5 %collective-permute-start.13 = (bf16[2304,128]{1,0:T(8,128)(2,1)S(1)}, bf16[2304,128]{1,0:T(8,128)(2,1)S(1)}, u32[]{:S(2)}, u32[]{:S(2)}) collective-permute-start(bf16[2304,128]{1,0:T(8,128)(2,1)S(1)} %get-tuple-element.58), channel_id=1, source_target_pairs={{0,4},{1,3},{2,6},{3,1},{4,0},{5,7},{6,2},{7,5},{8,12},{9,11},{10,... | collective-permute-start | bytes 1769480 | tf_op jit(solution)/shard_map/ppermute | solution.py:451
  36.5 2.1 %collective-permute-start.11 = (f32[3,256]{1,0:T(4,128)S(1)}, f32[3,256]{1,0:T(4,128)S(1)}, u32[]{:S(2)}, u32[]{:S(2)}) collective-permute-start(f32[3,256]{1,0:T(4,128)S(1)} %pad_maximum_fusion.stats), channel_id=1, source_target_pairs={{0,1},{1,0},{2,3},{3,2},{4,5},{5,4},{6,7},{7,6},{8,9},{9,8},{10,11... | collective-permute-start | bytes 9224 | tf_op jit(solution)/shard_map/ppermute | solution.py:28
  38.2 4.9 %collective-permute-start.15 = (bf16[2304,128]{1,0:T(8,128)(2,1)S(1)}, bf16[2304,128]{1,0:T(8,128)(2,1)S(1)}, u32[]{:S(2)}, u32[]{:S(2)}) collective-permute-start(bf16[2304,128]{1,0:T(8,128)(2,1)S(1)} %post.2), channel_id=1, source_target_pairs={{0,1},{1,0},{2,3},{3,2},{4,5},{5,4},{6,7},{7,6},{8,9},{9,8},{10,11... | collective-permute-start | bytes 1769480 | tf_op jit(solution)/shard_map/ppermute | solution.py:28
  38.7 3.7 %collective-permute-start.12 = (f32[8,128]{1,0:T(8,128)S(1)}, f32[8,128]{1,0:T(8,128)S(1)}, u32[]{:S(2)}, u32[]{:S(2)}) collective-permute-start(f32[8,128]{1,0:T(8,128)S(1)} %count.1), channel_id=1, source_target_pairs={{0,4},{4,0},{8,12},{12,8},{16,20},{20,16},{24,28},{28,24},{1,5},{5... | collective-permute-start | bytes 12296 | tf_op jit(solution)/shard_map/ppermute | solution.py:28
  42.4 2.1 %collective-permute-start.14 = (bf16[2304,128]{1,0:T(8,128)(2,1)S(1)}, bf16[2304,128]{1,0:T(8,128)(2,1)S(1)}, u32[]{:S(2)}, u32[]{:S(2)}) collective-permute-start(bf16[2304,128]{1,0:T(8,128)(2,1)S(1)} %post.3), channel_id=1, source_target_pairs={{0,1},{1,0},{2,3},{3,2},{4,5},{5,4},{6,7},{7,6},{8,9},{9,8},{10,11... | collective-permute-start | bytes 1769480 | tf_op jit(solution)/shard_map/ppermute | solution.py:28
  42.5 3.7 %collective-permute-start.18 = (f32[8,128]{1,0:T(8,128)S(1)}, f32[8,128]{1,0:T(8,128)S(1)}, u32[]{:S(2)}, u32[]{:S(2)}) collective-permute-start(f32[8,128]{1,0:T(8,128)S(1)} %add.9), channel_id=1, source_target_pairs={{0,2},{1,3},{2,0},{3,1},{4,6},{5,7},{6,4},{7,5},{8,10},{9,11},{10,... | collective-permute-start | bytes 12296 | tf_op jit(solution)/shard_map/ppermute | solution.py:28
  43.2 21.2 %copy-start.5 = (s32[4,64]{1,0:T(4,128)S(1)}, s32[4,64]{1,0:T(4,128)}, u32[]{:S(2)}) copy-start(s32[4,64]{1,0:T(4,128)} %segments.1) | copy-start | bytes 3076
  43.2 21.2 %copy-start.6 = (s32[4,8]{1,0:T(4,128)S(1)}, s32[4,8]{1,0:T(4,128)}, u32[]{:S(2)}) copy-start(s32[4,8]{1,0:T(4,128)} %pairing.1) | copy-start | bytes 388
  43.2 21.2 %copy-start.7 = (f32[4,8]{1,0:T(4,128)S(1)}, f32[4,8]{1,0:T(4,128)}, u32[]{:S(2)}) copy-start(f32[4,8]{1,0:T(4,128)} %ref_logp.1) | copy-start | bytes 388
  43.2 26.4 %copy-start.3 = (bf16[64,576]{1,0:T(8,128)(2,1)S(1)}, bf16[64,576]{1,0:T(8,128)(2,1)}, u32[]{:S(2)}) copy-start(bf16[64,576]{1,0:T(8,128)(2,1)} %hidden.1) | copy-start | bytes 221188
  43.2 11.2 %collective-permute-start.17 = (bf16[1152,128]{1,0:T(8,128)(2,1)S(1)}, bf16[1152,128]{1,0:T(8,128)(2,1)S(1)}, u32[]{:S(2)}, u32[]{:S(2)}) collective-permute-start(bf16[1152,128]{1,0:T(8,128)(2,1)S(1)} %get-tuple-element.61), channel_id=1, source_target_pairs={{0,4},{1,3},{2,6},{3,1},{4,0},{5,7},{6,2},{7,5},{8,12},{9,11},{10,... | collective-permute-start | bytes 884744 | tf_op jit(solution)/shard_map/ppermute | solution.py:451
  44.6 11.0 %collective-permute-start.16 = (bf16[1152,128]{1,0:T(8,128)(2,1)S(1)}, bf16[1152,128]{1,0:T(8,128)(2,1)S(1)}, u32[]{:S(2)}, u32[]{:S(2)}) collective-permute-start(bf16[1152,128]{1,0:T(8,128)(2,1)S(1)} %get-tuple-element.64), channel_id=1, source_target_pairs={{0,4},{1,3},{2,6},{3,1},{4,0},{5,7},{6,2},{7,5},{8,12},{9,11},{10,... | collective-permute-start | bytes 884744 | tf_op jit(solution)/shard_map/ppermute | solution.py:451
  46.3 3.6 %collective-permute-start.19 = (f32[8,128]{1,0:T(8,128)S(1)}, f32[8,128]{1,0:T(8,128)S(1)}, u32[]{:S(2)}, u32[]{:S(2)}) collective-permute-start(f32[8,128]{1,0:T(8,128)S(1)} %maximum_add_fusion), channel_id=1, source_target_pairs={{0,8},{4,12},{8,0},{12,4},{16,24},{20,28},{24,16},{28,20},{1,9},{5... | collective-permute-start | bytes 12296 | tf_op jit(solution)/shard_map/ppermute | solution.py:28
  49.9 4.5 %collective-permute-start.20 = (f32[8,128]{1,0:T(8,128)S(1)}, f32[8,128]{1,0:T(8,128)S(1)}, u32[]{:S(2)}, u32[]{:S(2)}) collective-permute-start(f32[8,128]{1,0:T(8,128)S(1)} %add.11.sums), channel_id=1, source_target_pairs={{0,16},{4,20},{8,24},{12,28},{16,0},{20,4},{24,8},{28,12},{1,17},{... | collective-permute-start | bytes 12296 | tf_op jit(solution)/shard_map/ppermute | solution.py:28
  54.7 5.2 %collective-permute-start.22 = (bf16[576,128]{1,0:T(8,128)(2,1)S(1)}, bf16[576,128]{1,0:T(8,128)(2,1)S(1)}, u32[]{:S(2)}, u32[]{:S(2)}) collective-permute-start(bf16[576,128]{1,0:T(8,128)(2,1)S(1)} %get-tuple-element.67), channel_id=1, source_target_pairs={{0,2},{1,5},{2,0},{3,7},{4,6},{5,1},{6,4},{7,3},{8,10},{9,13},{10,... | collective-permute-start | bytes 442376 | tf_op jit(solution)/shard_map/ppermute | solution.py:452
  55.9 8.3 %collective-permute-start.21 = (bf16[576,128]{1,0:T(8,128)(2,1)S(1)}, bf16[576,128]{1,0:T(8,128)(2,1)S(1)}, u32[]{:S(2)}, u32[]{:S(2)}) collective-permute-start(bf16[576,128]{1,0:T(8,128)(2,1)S(1)} %get-tuple-element.70), channel_id=1, source_target_pairs={{0,2},{1,5},{2,0},{3,7},{4,6},{5,1},{6,4},{7,3},{8,10},{9,13},{10,... | collective-permute-start | bytes 442376 | tf_op jit(solution)/shard_map/ppermute | solution.py:452
  60.0 5.4 %collective-permute-start.23 = (bf16[288,128]{1,0:T(8,128)(2,1)S(1)}, bf16[288,128]{1,0:T(8,128)(2,1)S(1)}, u32[]{:S(2)}, u32[]{:S(2)}) collective-permute-start(bf16[288,128]{1,0:T(8,128)(2,1)S(1)} %get-tuple-element.75), channel_id=1, source_target_pairs={{0,8},{4,12},{8,0},{12,4},{16,24},{20,28},{24,16},{28,20},{1,9},{5... | collective-permute-start | bytes 221192 | tf_op jit(solution)/shard_map/ppermute | solution.py:28
  60.9 6.4 %collective-permute-start.25 = (bf16[288,128]{1,0:T(8,128)(2,1)S(1)}, bf16[288,128]{1,0:T(8,128)(2,1)S(1)}, u32[]{:S(2)}, u32[]{:S(2)}) collective-permute-start(bf16[288,128]{1,0:T(8,128)(2,1)S(1)} %get-tuple-element.72), channel_id=1, source_target_pairs={{0,24},{4,28},{8,16},{12,20},{16,8},{20,12},{24,0},{28,4},{1,25},{... | collective-permute-start | bytes 221192 | tf_op jit(solution)/shard_map/ppermute | solution.py:28
  64.3 5.3 %collective-permute-start.24 = (bf16[288,128]{1,0:T(8,128)(2,1)S(1)}, bf16[288,128]{1,0:T(8,128)(2,1)S(1)}, u32[]{:S(2)}, u32[]{:S(2)}) collective-permute-start(bf16[288,128]{1,0:T(8,128)(2,1)S(1)} %get-tuple-element.76), channel_id=1, source_target_pairs={{0,16},{4,20},{8,24},{12,28},{16,0},{20,4},{24,8},{28,12},{1,17},{... | collective-permute-start | bytes 221192 | tf_op jit(solution)/shard_map/ppermute | solution.py:28
